TPU v7x, 32 devices: a whole 2x2x4 slice. The times are simulated.
32 devices in a mesh: group: 2 (over y), ctx: 4 (over z), req: 4 (over x, core).
Axes of the slice: x: 2, y: 2, z: 4, core: 2. Of those that a mesh axis runs over, the one named last changes fastest.
Arguments:
- hidden_states: bfloat16 [8, 512, 3584], P(('group', 'req'), 'ctx'), parts along dimension 0, may hold values from -6 to 6
- queries_base: bfloat16 [8, 512, 2688], P(('group', 'req'), 'ctx'), parts along dimension 0, may hold values from -6 to 6
- kv_base: bfloat16 [8, 512, 768], P(('group', 'req'), 'ctx'), parts along dimension 0, may hold values from -6 to 6
- adapter_down: bfloat16 [128, 3584, 128], P(('group', 'req'), 'ctx'), parts along dimension 0, may hold values from -0.09375 to 0.09375
- adapter_up: bfloat16 [128, 128, 2688], P(('group', 'req'), 'ctx'), parts along dimension 0, may hold values from -0.75 to 0.75
- adapter_ids: int32 [8], P('group'), parts along dimension 0, may hold values from 0 to 63
- adapter_slots: int32 [128], P('group'), parts along dimension 0, may hold values from 0 to 63, each once
- rank_buckets: int32 [128], P('group'), parts along dimension 0, may hold values from 16 to 128, as said below
- lengths: int32 [8], P(('group', 'req')), parts along dimension 0, may hold values from 128 to 512, as said below
Outputs:
- attended: bfloat16 [8, 512, 2688], P(('group', 'req'), 'ctx'), parts along dimension 0
There are 2 independent parts, one for each index of `group`. A program takes and returns all parts, laid end to end along the dimension named above; each array names one. Nothing has to cross between parts.
Inputs may be any that keep to these rules, and one draw needn't show every extreme that they name: `adapter_slots`: each slot once; slot k lies on store shard k // 16. `rank_buckets`: each is 16, 64 or 128. `lengths`: multiples of 128.
All inputs are finite; a program needn't handle non-finite values.
Results may differ from a plain program's by a relative error of at most 0.0076.
Values may be sent and summed in bfloat16 or wider, within the bound.
No kernel may reach another device: no remote copies, remote signals or barrier semaphores. Data moves between devices by JAX's collectives and lax.ppermute only.
A program may use at most 128 MiB of HBM per device.

v0:
```python
import functools
import math

import jax
import jax.numpy as jnp
from jax import lax
from jax.experimental import pallas as pl
from jax.experimental.pallas import tpu as pltpu
from jax.sharding import PartitionSpec as P

HD = 128
KVH = 3
GROUP = 7
HEADS = KVH * GROUP
SMEM = pltpu.SMEM
VMEM = pltpu.VMEM
HBM = pltpu.HBM
LOG2E = 1.0 / math.log(2.0)
PARAMS = pltpu.CompilerParams(vmem_limit_bytes=48 * 1024 * 1024)
WHOLE = pltpu.CompilerParams(vmem_limit_bytes=52 * 1024 * 1024)


def spec(space):
    return pl.BlockSpec(memory_space=space)


def select_kernel(table, *rest, requests):
    stores, outs, sems = rest[:2], rest[2:6], rest[6]
    per_shard = stores[0].shape[0]
    me = lax.axis_index("req")
    first = me * per_shard
    copies = []
    for i, flip in enumerate((0, 2, 1, 3)):
        local = table[requests + table[me ^ flip]] - first
        held = (local >= 0) & (local < per_shard)
        for f, store in enumerate(stores):
            out = outs[2 * f + i // 2]
            copies.append((held, local, store, out, i % 2, sems.at[4 * f + i]))
    for held, local, store, out, k, sem in copies:

        @pl.when(held)
        def _():
            pltpu.make_async_copy(store.at[local], out.at[k], sem).start()

    for held, local, store, out, k, sem in copies:

        @pl.when(jnp.logical_not(held))
        def _():
            out[k] = jnp.zeros(out.shape[1:], out.dtype)

    for held, local, store, out, k, sem in copies:

        @pl.when(held)
        def _():
            pltpu.make_async_copy(store.at[local], out.at[k], sem).wait()


def select(ids, slots, down, up):
    shapes = [jax.ShapeDtypeStruct((2, *x.shape[1:]), x.dtype) for x in (down, down, up, up)]
    return pl.pallas_call(
        functools.partial(select_kernel, requests=ids.shape[0]),
        out_shape=shapes,
        in_specs=[spec(SMEM), spec(HBM), spec(HBM)],
        out_specs=[spec(VMEM)] * 4,
        scratch_shapes=[pltpu.SemaphoreType.DMA((8,))],
        compiler_params=WHOLE,
    )(jnp.concatenate([ids, slots]), down, up)


SIBLING = [(0, 1), (1, 0), (2, 3), (3, 2)]
ACROSS = [(0, 2), (1, 3), (2, 0), (3, 1)]
ONE = [(i, i ^ 1) for i in range(4)]
TWO = [(i, i ^ 2) for i in range(4)]
LAST = [(0, 0), (1, 1), (2, 3), (3, 2)]


def spread(shard):
    return lax.ppermute(shard, "ctx", ONE), lax.ppermute(shard, "ctx", TWO)


def low_rank_kernel(ids, ranks, hidden, *rest):
    pieces, out, accum = rest[:-2], rest[-2], rest[-1]
    rows = pieces[0].shape[0]
    rank = ranks[ids[lax.axis_index("req")]]
    accum[...] = jnp.zeros_like(accum)
    for flip, piece in enumerate(pieces):
        place = lax.axis_index("ctx") ^ flip
        columns = pl.ds(pl.multiple_of(place * rows, HD), rows)
        accum[...] += jnp.dot(hidden[:, columns], piece[...], preferred_element_type=jnp.float32)

    column = lax.broadcasted_iota(jnp.int32, accum.shape, 1)
    out[...] = jnp.where(column < rank, accum[...], 0.0).astype(jnp.bfloat16)


def low_rank(ids, ranks, hidden, pieces):
    shape = (hidden.shape[0], pieces[0].shape[1])
    return pl.pallas_call(
        low_rank_kernel,
        out_shape=jax.ShapeDtypeStruct(shape, jnp.bfloat16),
        in_specs=[spec(SMEM)] * 2 + [spec(VMEM)] * (1 + len(pieces)),
        out_specs=spec(VMEM),
        scratch_shapes=[VMEM(shape, jnp.float32)],
        compiler_params=PARAMS,
        cost_estimate=pl.CostEstimate(flops=1 << 27, bytes_accessed=1 << 22, transcendentals=0),
    )(ids, ranks, hidden, *pieces)


FACTOR = LOG2E / math.sqrt(HD)


def head_columns(kvs, h):
    keys = [kv[:, h * HD : (h + 1) * HD] for kv in kvs]
    values = [kv[:, (KVH + h) * HD : (KVH + h + 1) * HD] for kv in kvs]
    return jnp.concatenate(keys, axis=0), jnp.concatenate(values, axis=0)


def dot_keys(queries, keys):
    return lax.dot_general(
        queries, keys, (((1,), (1,)), ((), ())), preferred_element_type=jnp.float32
    )


def out_copies(result, out, sems):
    width = GROUP * HD
    return [
        pltpu.make_async_copy(result.at[h], out.at[:, pl.ds(h * width, width)], sems.at[h])
        for h in range(KVH)
    ]


def attend_kernel(lengths, base, low, *rest):
    kvs, ups = rest[:3], rest[3:7]
    out, queries, sums, highs, counts, upper, result, sems = rest[7:]
    tokens = base.shape[0]
    rows = ups[0].shape[0]
    z = lax.axis_index("ctx")
    live = z * tokens < lengths[0]
    block = GROUP * tokens
    copies = out_copies(result, out, sems)

    @pl.when(jnp.logical_not(live))
    def _():
        result[...] = jnp.zeros_like(result)
        for copy in copies:
            copy.start()

    @pl.when(live)
    def _():
        for flip, piece in enumerate(ups):
            upper[pl.ds(pl.multiple_of((z ^ flip) * rows, rows), rows), :] = piece[...]
        for j in range(HEADS):
            columns = slice(j * HD, (j + 1) * HD)
            delta = jnp.dot(low[...], upper[:, columns], preferred_element_type=jnp.float32)
            queries[j * tokens : (j + 1) * tokens, :] = (
                base[:, columns].astype(jnp.float32) + delta
            ).astype(jnp.bfloat16)

    query_pos = lax.broadcasted_iota(jnp.int32, (tokens, tokens), 0)
    key_pos = lax.broadcasted_iota(jnp.int32, (tokens, tokens), 1)
    causal = key_pos <= query_pos
    for mine, needed in enumerate(((0,), (0, 1), (0, 2), (0, 1, 2))):

        @pl.when(live & (z == mine))
        def _():
            for h in range(KVH):
                keys, values = head_columns([kvs[i] for i in needed], h)
                scores = dot_keys(queries[h * block : (h + 1) * block, :], keys)
                weights, tops, totals = [], [], []
                for g in range(GROUP):
                    score = scores[g * tokens : (g + 1) * tokens, :]
                    own = jnp.where(causal, score[:, :tokens], -1e30)
                    if mine:
                        own = jnp.concatenate([own, score[:, tokens:]], axis=1)
                    tops.append(jnp.max(own, axis=1, keepdims=True))
                    weight = jnp.exp2((own - tops[g]) * FACTOR)
                    totals.append(jnp.sum(weight, axis=1, keepdims=True))
                    weights.append(weight.astype(jnp.bfloat16))
                product = jnp.dot(
                    jnp.concatenate(weights, axis=0), values, preferred_element_type=jnp.float32
                )
                if mine < 2:
                    for g in range(GROUP):
                        result[h, :, g * HD : (g + 1) * HD] = (
                            product[g * tokens : (g + 1) * tokens, :] / totals[g]
                        ).astype(jnp.bfloat16)
                    copies[h].start()
                else:
                    sums[h * block : (h + 1) * block, :] = product
                    for g in range(GROUP):
                        at = slice(h * block + g * tokens, h * block + (g + 1) * tokens)
                        highs[at, :] = jnp.broadcast_to(tops[g], (tokens, HD))
                        counts[at, :] = jnp.broadcast_to(totals[g], (tokens, HD))

    @pl.when(jnp.logical_not(live) | (z < 2))
    def _():
        for copy in copies:
            copy.wait()


def attend(lengths, base, low, kvs, ups):
    tokens, width = base.shape
    rows = HEADS * tokens
    shapes = [
        jax.ShapeDtypeStruct(base.shape, jnp.bfloat16),
        jax.ShapeDtypeStruct((rows, HD), jnp.bfloat16),
    ] + [jax.ShapeDtypeStruct((rows, HD), jnp.float32)] * 3
    return pl.pallas_call(
        attend_kernel,
        out_shape=shapes,
        in_specs=[spec(SMEM)] + [spec(VMEM)] * (2 + len(kvs) + len(ups)),
        out_specs=[spec(HBM)] + [spec(VMEM)] * 4,
        scratch_shapes=[
            VMEM((low.shape[1], width), jnp.bfloat16),
            VMEM((KVH, tokens, GROUP * HD), jnp.bfloat16),
            pltpu.SemaphoreType.DMA((KVH,)),
        ],
        compiler_params=PARAMS,
        cost_estimate=pl.CostEstimate(
            flops=1 << 30, bytes_accessed=1 << 22, transcendentals=1 << 21
        ),
    )(lengths, base, low, *kvs, *ups)


def finish_kernel(lengths, so_far, queries, sums, highs, counts, kv, out, result, sems):
    del so_far
    tokens = result.shape[1]
    z = lax.axis_index("ctx")
    block = GROUP * tokens
    copies = out_copies(result, out, sems)

    @pl.when((z * tokens < lengths[0]) & (z >= 2))
    def _():
        for h in range(KVH):
            keys, values = head_columns([kv], h)
            scores = dot_keys(queries[h * block : (h + 1) * block, :], keys)
            weights, factors, totals = [], [], []
            for g in range(GROUP):
                at = slice(h * block + g * tokens, h * block + (g + 1) * tokens)
                score = scores[g * tokens : (g + 1) * tokens, :]
                newest = jnp.maximum(highs[at, :], jnp.max(score, axis=1, keepdims=True))
                weight = jnp.exp2((score - newest) * FACTOR)
                factors.append(jnp.exp2((highs[at, :] - newest) * FACTOR))
                added = jnp.sum(weight, axis=1, keepdims=True)
                totals.append(counts[at, :] * factors[g] + added)
                weights.append(weight.astype(jnp.bfloat16))
            product = jnp.dot(
                jnp.concatenate(weights, axis=0), values, preferred_element_type=jnp.float32
            )
            for g in range(GROUP):
                at = slice(h * block + g * tokens, h * block + (g + 1) * tokens)
                whole = sums[at, :] * factors[g] + product[g * tokens : (g + 1) * tokens, :]
                result[h, :, g * HD : (g + 1) * HD] = (whole / totals[g]).astype(jnp.bfloat16)
            copies[h].start()
        for copy in copies:
            copy.wait()


def finish(lengths, so_far, queries, sums, highs, counts, kv):
    tokens = so_far.shape[0]
    return pl.pallas_call(
        finish_kernel,
        out_shape=jax.ShapeDtypeStruct(so_far.shape, so_far.dtype),
        in_specs=[spec(SMEM), spec(HBM)] + [spec(VMEM)] * 5,
        out_specs=spec(HBM),
        input_output_aliases={1: 0},
        scratch_shapes=[
            VMEM((KVH, tokens, GROUP * HD), jnp.bfloat16),
            pltpu.SemaphoreType.DMA((KVH,)),
        ],
        compiler_params=PARAMS,
        cost_estimate=pl.CostEstimate(
            flops=1 << 28, bytes_accessed=1 << 21, transcendentals=1 << 19
        ),
    )(lengths, so_far, queries, sums, highs, counts, kv)


def body(
    hidden_states,
    queries_base,
    kv_base,
    adapter_down,
    adapter_up,
    adapter_ids,
    adapter_slots,
    rank_buckets,
    lengths,
):
    keep_down, give_down, keep_up, give_up = select(
        adapter_ids, adapter_slots, adapter_down, adapter_up
    )
    kv = kv_base[0]
    kv_one, kv_two = spread(kv)
    near_down = lax.ppermute(give_down, "req", SIBLING)
    near_up = lax.ppermute(give_up, "req", SIBLING)
    far_down = lax.ppermute(keep_down[1] + near_down[1], "req", ACROSS)
    far_up = lax.ppermute(keep_up[1] + near_up[1], "req", ACROSS)
    down = keep_down[0] + near_down[0] + far_down
    down, kv_one = lax.optimization_barrier((down, kv_one))
    down_one, down_two = spread(down)
    up = keep_up[0] + near_up[0] + far_up
    up_one, up_two = spread(up)
    down_two = lax.optimization_barrier((down_two, down_one, kv_two))[0]
    down_three = lax.ppermute(down_two, "ctx", ONE)
    up_two = lax.optimization_barrier((up_two, up_one))[0]
    up_three = lax.ppermute(up_two, "ctx", ONE)
    kv_last = lax.optimization_barrier((kv_two, up_two))[0]
    kv_three = lax.ppermute(kv_last, "ctx", LAST)
    downs = [down, down_one, down_two, down_three]
    ups = [up, up_one, up_two, up_three]
    low = low_rank(adapter_ids, rank_buckets, hidden_states[0], downs)
    parts = attend(lengths, queries_base[0], low, [kv, kv_one, kv_two], ups)
    return finish(lengths, *parts, kv_three)[None]


def plain_body(
    hidden_states,
    queries_base,
    kv_base,
    adapter_down,
    adapter_up,
    adapter_ids,
    adapter_slots,
    rank_buckets,
    lengths,
):
    req_index = lax.axis_index("req")
    ctx_index = lax.axis_index("ctx")
    per_shard = adapter_down.shape[0]
    requests = adapter_ids.shape[0]
    store = adapter_slots.shape[0]
    rank_width = adapter_down.shape[2]
    tokens = hidden_states.shape[1]
    query_width = queries_base.shape[2]
    store_range = jnp.arange(store, dtype=jnp.int32)
    chosen = adapter_ids[:, None] == store_range[None, :]
    slot_of = jnp.sum(jnp.where(chosen, adapter_slots[None, :], 0), axis=1)
    rank_of = jnp.sum(jnp.where(chosen, rank_buckets[None, :], 0), axis=1)
    mine = jnp.arange(requests, dtype=jnp.int32) == req_index
    my_slot = jnp.sum(jnp.where(mine, slot_of, 0))
    my_rank = jnp.sum(jnp.where(mine, rank_of, 0))
    held = (
        slot_of[:, None] == req_index * per_shard + jnp.arange(per_shard, dtype=jnp.int32)[None, :]
    )
    select = held.astype(jnp.bfloat16)
    send_down = jnp.einsum(
        "qa,ard->qrd", select, adapter_down, preferred_element_type=jnp.float32
    ).astype(jnp.bfloat16)
    send_up = jnp.einsum(
        "qa,ard->qrd", select, adapter_up, preferred_element_type=jnp.float32
    ).astype(jnp.bfloat16)
    got_down, got_up = (
        lax.all_to_all(send_down, "req", split_axis=0, concat_axis=0, tiled=True),
        lax.all_to_all(send_up, "req", split_axis=0, concat_axis=0, tiled=True),
    )
    owner = my_slot // per_shard
    down_mine = lax.dynamic_index_in_dim(got_down, owner, 0, keepdims=False)
    up_mine = lax.dynamic_index_in_dim(got_up, owner, 0, keepdims=False)
    features = hidden_states[0]
    columns = features
    low_rank = jnp.dot(
        columns,
        lax.all_gather(down_mine, "ctx", axis=0, tiled=True),
        preferred_element_type=jnp.float32,
    )
    low_rank = jnp.where(
        jnp.arange(rank_width, dtype=jnp.int32)[None, :] < my_rank, low_rank, 0.0
    ).astype(jnp.bfloat16)
    columns = low_rank
    delta = jnp.dot(
        columns,
        lax.all_gather(up_mine, "ctx", axis=0, tiled=True),
        preferred_element_type=jnp.float32,
    )
    queries = (
        (queries_base[0].astype(jnp.float32) + delta)
        .astype(jnp.bfloat16)
        .reshape(tokens, KVH, GROUP, HD)
    )
    length = lengths[0]
    first_query = ctx_index * tokens
    query_pos = first_query + jnp.arange(tokens, dtype=jnp.int32)
    last_needed = jnp.minimum(first_query + tokens - 1, length - 1)
    scale = 1.0 / math.sqrt(HD)
    key_width = KVH * HD
    initial = (
        jnp.full((KVH, GROUP, tokens), -1e30, jnp.float32),
        jnp.zeros((KVH, GROUP, tokens), jnp.float32),
        jnp.zeros((KVH, GROUP, tokens, HD), jnp.float32),
    )
    piece = lax.all_gather(kv_base[0], "ctx", axis=0, tiled=True)
    count = piece.shape[0]
    width = math.gcd(count, 512)

    def key_block(index, state):
        largest, total, accum = state
        offset = index * width
        rows = lax.dynamic_slice_in_dim(piece, offset, width, 0)
        keys = rows[:, :key_width].reshape(width, KVH, HD)
        values = rows[:, key_width:].reshape(width, KVH, HD)
        key_pos = offset + jnp.arange(width, dtype=jnp.int32)
        score = (
            jnp.einsum("tkgd,skd->kgts", queries, keys, preferred_element_type=jnp.float32) * scale
        )
        allowed = (key_pos[None, :] <= query_pos[:, None]) & (key_pos[None, :] < length)
        masked = jnp.where(allowed, score, -1e30)
        newest = jnp.maximum(largest, jnp.max(masked, axis=-1))
        weight = jnp.where(allowed, jnp.exp(score - newest[..., None]), 0.0)
        factor = jnp.exp(largest - newest)
        total = total * factor + jnp.sum(weight, axis=-1)
        product = jnp.einsum(
            "kgts,skd->kgtd",
            weight.astype(jnp.bfloat16),
            values,
            preferred_element_type=jnp.float32,
        )
        accum = accum * factor[..., None] + product
        return (newest, total, accum)

    def compute(state):
        return lax.fori_loop(0, count // width, key_block, state)

    needed = (jnp.int32(0) <= last_needed) & (first_query < length)
    largest, total, accum = lax.cond(needed, compute, lambda state: state, initial)
    safe_total = jnp.where(total > 0.0, total, 1.0)
    output = accum / safe_total[..., None]
    output = jnp.transpose(output, (2, 0, 1, 3)).reshape(tokens, query_width)
    output = jnp.where(query_pos[:, None] < length, output, 0.0).astype(jnp.bfloat16)
    return output[None]


def solution(mesh):
    paired = mesh.shape["ctx"] == 4 and mesh.shape["req"] == 4
    return jax.shard_map(
        body if paired else plain_body,
        mesh=mesh,
        in_specs=(
            P(("group", "req"), "ctx", None),
            P(("group", "req"), "ctx", None),
            P(("group", "req"), "ctx", None),
            P(("group", "req"), "ctx", None),
            P(("group", "req"), "ctx", None),
            P("group"),
            P("group"),
            P("group"),
            P(("group", "req")),
        ),
        out_specs=P(("group", "req"), "ctx", None),
        check_vma=False,
    )
```

profile of v0, /device:TPU:18, one launch (start us, length us, event | category | flops | bytes accessed | tf_op | source)
XLA Modules:
  0.0 48.5 jit_solution(15521334967163861942)
XLA Ops:
  0.0 0.7 %pad_add_fusion.table = s32[68]{0:T(128)S(1)} fusion(s32[64]{0:T(128)} %param.15, s32[4]{0:T(128)} %ids.1), kind=kLoop, calls=%fused_computation.10 | loop fusion | flops 68 | bytes 544 | tf_op jit(solution)/shard_map/concatenate | solution.py:67
  0.7 0.0 copy-start.5
  0.7 1.9 %shard_map.91 = (bf16[2,896,128]{2,1,0:T(8,128)(2,1)S(1)}, bf16[2,896,128]{2,1,0:T(8,128)(2,1)S(1)}, bf16[2,32,2688]{2,1,0:T(8,128)(2,1)S(1)}, bf16[2,32,2688]{2,1,0:T(8,128)(2,1)S(1)}) custom-call(s32[68]{0:T(128)S(1)} %pad_add_fusion.table, bf16[16,896,128]{2,1,0:T(8,128)(2,1)} %rest_0_.1, bf16[16,32,2688]{2,1,0:T(8,128)(2,1)} %rest_1_.1), custom_call_target="tpu_custom_call" | custom-call | tf_op jit(solution)/shard_map/pallas_call | solution.py:60
  2.6 0.1 collective-permute-start
  2.7 0.5 %collective-permute-start.7 = (bf16[2,32,2688]{2,1,0:T(8,128)(2,1)S(1)}, bf16[2,32,2688]{2,1,0:T(8,128)(2,1)S(1)}, u32[]{:S(2)}, u32[]{:S(2)}) collective-permute-start(bf16[2,32,2688]{2,1,0:T(8,128)(2,1)S(1)} %get-tuple-element.25), channel_id=1, source_target_pairs={{0,1},{1,0},{2,3},{3,2},{4,5},{5,4},{6,7},{7,6},{8,9},{9,8},{10,11... | collective-permute-start | bytes 1032200 | tf_op jit(solution)/shard_map/ppermute | solution.py:294
  3.2 0.0 copy-done.5
  3.2 1.6 %collective-permute-start.2 = (bf16[128,768]{1,0:T(8,128)(2,1)S(1)}, bf16[128,768]{1,0:T(8,128)(2,1)S(1)}, u32[]{:S(2)}, u32[]{:S(2)}) collective-permute-start(bf16[128,768]{1,0:T(8,128)(2,1)S(1)} %bitcast.18), channel_id=1, source_target_pairs={{0,4},{4,0},{8,12},{12,8},{1,5},{5,1},{9,13},{13,9},{2,6},{6,2},{1... | collective-permute-start | bytes 589832 | tf_op jit(solution)/shard_map/ppermute | solution.py:78
  4.8 0.3 collective-permute-start.5
  5.1 0.0 collective-permute-done
  5.1 0.0 copy-start.1
  5.1 0.0 copy-start.2
  5.1 0.0 copy-start.3
  5.2 0.6 %collective-permute-start.1 = (bf16[896,128]{1,0:T(8,128)(2,1)S(1)}, bf16[896,128]{1,0:T(8,128)(2,1)S(1)}, u32[]{:S(2)}, u32[]{:S(2)}) collective-permute-start(bf16[896,128]{1,0:T(8,128)(2,1)S(1)} %fusion), channel_id=1, source_target_pairs={{0,2},{1,3},{2,0},{3,1},{4,6},{5,7},{6,4},{7,5},{8,10},{9,11},{10,... | collective-permute-start | bytes 688136 | tf_op jit(solution)/shard_map/ppermute | solution.py:295
  5.8 0.0 collective-permute-done.7
  5.8 1.6 %collective-permute-start.8 = (bf16[32,2688]{1,0:T(8,128)(2,1)S(1)}, bf16[32,2688]{1,0:T(8,128)(2,1)S(1)}, u32[]{:S(2)}, u32[]{:S(2)}) collective-permute-start(bf16[32,2688]{1,0:T(8,128)(2,1)S(1)} %fusion.3), channel_id=1, source_target_pairs={{0,2},{1,3},{2,0},{3,1},{4,6},{5,7},{6,4},{7,5},{8,10},{9,11},{10,... | collective-permute-start | bytes 516104 | tf_op jit(solution)/shard_map/ppermute | solution.py:296
  7.3 6.4 %collective-permute-done.1 = bf16[896,128]{1,0:T(8,128)(2,1)S(1)} collective-permute-done((bf16[896,128]{1,0:T(8,128)(2,1)S(1)}, bf16[896,128]{1,0:T(8,128)(2,1)S(1)}, u32[]{:S(2)}, u32[]{:S(2)}) %collective-permute-start.1) | collective-permute-done | bytes 229408 | tf_op jit(solution)/shard_map/ppermute | solution.py:295
  13.8 0.0 copy-start.4
  13.8 0.0 collective-permute-done.2.rest_1_
  13.8 0.9 %collective-permute-start.3 = (bf16[896,128]{1,0:T(8,128)(2,1)S(1)}, bf16[896,128]{1,0:T(8,128)(2,1)S(1)}, u32[]{:S(2)}, u32[]{:S(2)}) collective-permute-start(bf16[896,128]{1,0:T(8,128)(2,1)S(1)} %fusion.2.rest_0_), channel_id=1, source_target_pairs={{0,4},{4,0},{8,12},{12,8},{1,5},{5,1},{9,13},{13,9},{2,6},{6,2},{1... | collective-permute-start | bytes 688136 | tf_op jit(solution)/shard_map/ppermute | solution.py:78
  14.8 2.2 %collective-permute-start.4 = (bf16[896,128]{1,0:T(8,128)(2,1)S(1)}, bf16[896,128]{1,0:T(8,128)(2,1)S(1)}, u32[]{:S(2)}, u32[]{:S(2)}) collective-permute-start(bf16[896,128]{1,0:T(8,128)(2,1)S(1)} %fusion.2.rest_0_), channel_id=1, source_target_pairs={{0,8},{4,12},{8,0},{12,4},{1,9},{5,13},{9,1},{13,5},{2,10},{6,14},... | collective-permute-start | bytes 688136 | tf_op jit(solution)/shard_map/ppermute | solution.py:78
  16.9 0.0 collective-permute-done.8
  17.0 1.6 %collective-permute-start.9 = (bf16[32,2688]{1,0:T(8,128)(2,1)S(1)}, bf16[32,2688]{1,0:T(8,128)(2,1)S(1)}, u32[]{:S(2)}, u32[]{:S(2)}) collective-permute-start(bf16[32,2688]{1,0:T(8,128)(2,1)S(1)} %fusion.5.rest_3_), channel_id=1, source_target_pairs={{0,4},{4,0},{8,12},{12,8},{1,5},{5,1},{9,13},{13,9},{2,6},{6,2},{1... | collective-permute-start | bytes 516104 | tf_op jit(solution)/shard_map/ppermute | solution.py:78
  18.6 0.5 collective-permute-start.10
  19.1 0.0 collective-permute-done.5.rest_2_
  19.1 6.4 %collective-permute-done.3.rest_1_ = bf16[896,128]{1,0:T(8,128)(2,1)S(1)} collective-permute-done((bf16[896,128]{1,0:T(8,128)(2,1)S(1)}, bf16[896,128]{1,0:T(8,128)(2,1)S(1)}, u32[]{:S(2)}, u32[]{:S(2)}) %collective-permute-start.3) | collective-permute-done | bytes 229408 | tf_op jit(solution)/shard_map/ppermute | solution.py:78
  25.5 2.9 %collective-permute-done.4.rest_2_ = bf16[896,128]{1,0:T(8,128)(2,1)S(1)} collective-permute-done((bf16[896,128]{1,0:T(8,128)(2,1)S(1)}, bf16[896,128]{1,0:T(8,128)(2,1)S(1)}, u32[]{:S(2)}, u32[]{:S(2)}) %collective-permute-start.4) | collective-permute-done | bytes 229408 | tf_op jit(solution)/shard_map/ppermute | solution.py:78
  28.4 2.3 %collective-permute-start.6 = (bf16[896,128]{1,0:T(8,128)(2,1)S(1)}, bf16[896,128]{1,0:T(8,128)(2,1)S(1)}, u32[]{:S(2)}, u32[]{:S(2)}) collective-permute-start(bf16[896,128]{1,0:T(8,128)(2,1)S(1)} %collective-permute-done.4.rest_2_), channel_id=1, source_target_pairs={{0,4},{4,0},{8,12},{12,8},{1,5},{5,1},{9,13},{13,9},{2,6},{6,2},{1... | collective-permute-start | bytes 688136 | tf_op jit(solution)/shard_map/ppermute | solution.py:303
  30.7 1.5 %collective-permute-done.9.rest_4_ = bf16[32,2688]{1,0:T(8,128)(2,1)S(1)} collective-permute-done((bf16[32,2688]{1,0:T(8,128)(2,1)S(1)}, bf16[32,2688]{1,0:T(8,128)(2,1)S(1)}, u32[]{:S(2)}, u32[]{:S(2)}) %collective-permute-start.9) | collective-permute-done | bytes 172064 | tf_op jit(solution)/shard_map/ppermute | solution.py:78
  32.2 3.6 %collective-permute-done.10.rest_5_ = bf16[32,2688]{1,0:T(8,128)(2,1)S(1)} collective-permute-done((bf16[32,2688]{1,0:T(8,128)(2,1)S(1)}, bf16[32,2688]{1,0:T(8,128)(2,1)S(1)}, u32[]{:S(2)}, u32[]{:S(2)}) %collective-permute-start.10) | collective-permute-done | bytes 172064 | tf_op jit(solution)/shard_map/ppermute | solution.py:78
  35.8 0.0 collective-permute-start.11
  35.8 3.9 %collective-permute-start.12 = (bf16[128,768]{1,0:T(8,128)(2,1)S(1)}, bf16[128,768]{1,0:T(8,128)(2,1)S(1)}, u32[]{:S(2)}, u32[]{:S(2)}) collective-permute-start(bf16[128,768]{1,0:T(8,128)(2,1)S(1)} %collective-permute-done.5.rest_2_), channel_id=1, source_target_pairs={{0,0},{4,4},{8,12},{12,8},{1,1},{5,5},{9,13},{13,9},{2,2},{6,6},{1... | collective-permute-start | bytes 589832 | tf_op jit(solution)/shard_map/ppermute | solution.py:307
  40.3 0.0 collective-permute-done.6.rest_3_
  40.4 0.0 copy-done.1
  40.4 0.0 copy-done.2
  40.4 0.0 copy-done.3
  40.4 0.9 %shard_map.92.low = bf16[128,128]{1,0:T(8,128)(2,1)S(1)} custom-call(s32[4]{0:T(128)S(1)} %copy-done.2, s32[64]{0:T(128)S(1)} %copy-done.3, bf16[128,3584]{1,0:T(8,128)(2,1)S(1)} %bitcast.16, bf16[896,128]{1,0:T(8,128)(2,1)S(1)} %fusion.2.rest_0_, bf16[896,128]{1,0:T(8,128)(2,1)S(1)} %collective-permute-done.3.rest_1_, ...), custom_call_target="tpu_custom_call" | custom-call | flops 134217728 | bytes 4194304 | tf_op jit(solution)/shard_map/pallas_call | solution.py:97
  41.3 1.3 %collective-permute-done.11.rest_6_ = bf16[32,2688]{1,0:T(8,128)(2,1)S(1)} collective-permute-done((bf16[32,2688]{1,0:T(8,128)(2,1)S(1)}, bf16[32,2688]{1,0:T(8,128)(2,1)S(1)}, u32[]{:S(2)}, u32[]{:S(2)}) %collective-permute-start.11) | collective-permute-done | bytes 172064 | tf_op jit(solution)/shard_map/ppermute | solution.py:305
  42.7 0.0 copy-done.4
  42.7 2.6 %shard_map.93 = (bf16[128,2688]{1,0:T(8,128)(2,1)}, bf16[2688,128]{1,0:T(8,128)(2,1)S(1)}, f32[2688,128]{1,0:T(8,128)S(1)}, f32[2688,128]{1,0:T(8,128)S(1)}, f32[2688,128]{1,0:T(8,128)}) custom-call(s32[1]{0:T(128)S(6)} %copy.12.lengths, bf16[128,2688]{1,0:T(8,128)(2,1)S(1)} %bitcast.17, bf16[128,128]{1,0:T(8,128)(2,1)S(1)} %shard_map.92.low, ...), custom_call_target="tpu_custom_call" | custom-call | flops 1073741824 | bytes 4194304 | tf_op jit(solution)/shard_map/pallas_call | solution.py:207
  45.3 0.0 collective-permute-done.12.kv
  45.3 0.0 copy-start
  45.3 1.3 %copy-done = f32[2688,128]{1,0:T(8,128)S(1)} copy-done((f32[2688,128]{1,0:T(8,128)S(1)}, f32[2688,128]{1,0:T(8,128)}, u32[]{:S(2)}) %copy-start) | copy-done | bytes 1376280
  46.6 1.8 %shard_map.94 = bf16[128,2688]{1,0:T(8,128)(2,1)} custom-call(s32[1]{0:T(128)S(6)} %copy.12.lengths, bf16[128,2688]{1,0:T(8,128)(2,1)} %get-tuple-element.27.so_far, bf16[2688,128]{1,0:T(8,128)(2,1)S(1)} %get-tuple-element.28.queries, f32[2688,128]{1,0:T(8,128)S(1)} %get-tuple-element.29.sums, ...), custom_call_target="tpu_custom_call", output_to_operand_aliasing={{}: (1, {})} | custom-call | flops 268435456 | bytes 2097152 | tf_op jit(solution)/shard_map/pallas_call | solution.py:260
  (4 shorter events, 0.1 us)
Async XLA Ops:
  0.7 2.4 %copy-start.5 = (bf16[1,128,768]{2,1,0:T(8,128)(2,1)S(1)}, bf16[1,128,768]{2,1,0:T(8,128)(2,1)}, u32[]{:S(2)}) copy-start(bf16[1,128,768]{2,1,0:T(8,128)(2,1)} %param.11) | copy-start | bytes 589828
  2.6 2.5 %collective-permute-start = (bf16[2,896,128]{2,1,0:T(8,128)(2,1)S(1)}, bf16[2,896,128]{2,1,0:T(8,128)(2,1)S(1)}, u32[]{:S(2)}, u32[]{:S(2)}) collective-permute-start(bf16[2,896,128]{2,1,0:T(8,128)(2,1)S(1)} %get-tuple-element.20), channel_id=1, source_target_pairs={{0,1},{1,0},{2,3},{3,2},{4,5},{5,4},{6,7},{7,6},{8,9},{9,8},{10,11... | collective-permute-start | bytes 1376264 | tf_op jit(solution)/shard_map/ppermute | solution.py:293
  2.7 3.1 %collective-permute-start.7 = (bf16[2,32,2688]{2,1,0:T(8,128)(2,1)S(1)}, bf16[2,32,2688]{2,1,0:T(8,128)(2,1)S(1)}, u32[]{:S(2)}, u32[]{:S(2)}) collective-permute-start(bf16[2,32,2688]{2,1,0:T(8,128)(2,1)S(1)} %get-tuple-element.25), channel_id=1, source_target_pairs={{0,1},{1,0},{2,3},{3,2},{4,5},{5,4},{6,7},{7,6},{8,9},{9,8},{10,11... | collective-permute-start | bytes 1032200 | tf_op jit(solution)/shard_map/ppermute | solution.py:294
  3.2 10.6 %collective-permute-start.2 = (bf16[128,768]{1,0:T(8,128)(2,1)S(1)}, bf16[128,768]{1,0:T(8,128)(2,1)S(1)}, u32[]{:S(2)}, u32[]{:S(2)}) collective-permute-start(bf16[128,768]{1,0:T(8,128)(2,1)S(1)} %bitcast.18), channel_id=1, source_target_pairs={{0,4},{4,0},{8,12},{12,8},{1,5},{5,1},{9,13},{13,9},{2,6},{6,2},{1... | collective-permute-start | bytes 589832 | tf_op jit(solution)/shard_map/ppermute | solution.py:78
  4.8 14.3 %collective-permute-start.5 = (bf16[128,768]{1,0:T(8,128)(2,1)S(1)}, bf16[128,768]{1,0:T(8,128)(2,1)S(1)}, u32[]{:S(2)}, u32[]{:S(2)}) collective-permute-start(bf16[128,768]{1,0:T(8,128)(2,1)S(1)} %bitcast.19), channel_id=1, source_target_pairs={{0,8},{4,12},{8,0},{12,4},{1,9},{5,13},{9,1},{13,5},{2,10},{6,14},... | collective-permute-start | bytes 589832 | tf_op jit(solution)/shard_map/ppermute | solution.py:78
  5.1 35.3 %copy-start.1 = (bf16[1,128,3584]{2,1,0:T(8,128)(2,1)S(1)}, bf16[1,128,3584]{2,1,0:T(8,128)(2,1)}, u32[]{:S(2)}) copy-start(bf16[1,128,3584]{2,1,0:T(8,128)(2,1)} %param.9) | copy-start | bytes 2752516
  5.1 35.3 %copy-start.2 = (s32[4]{0:T(128)S(1)}, s32[4]{0:T(128)}, u32[]{:S(2)}) copy-start(s32[4]{0:T(128)} %ids.1) | copy-start | bytes 52
  5.1 35.3 %copy-start.3 = (s32[64]{0:T(128)S(1)}, s32[64]{0:T(128)}, u32[]{:S(2)}) copy-start(s32[64]{0:T(128)} %ranks.1) | copy-start | bytes 772
  5.2 8.6 %collective-permute-start.1 = (bf16[896,128]{1,0:T(8,128)(2,1)S(1)}, bf16[896,128]{1,0:T(8,128)(2,1)S(1)}, u32[]{:S(2)}, u32[]{:S(2)}) collective-permute-start(bf16[896,128]{1,0:T(8,128)(2,1)S(1)} %fusion), channel_id=1, source_target_pairs={{0,2},{1,3},{2,0},{3,1},{4,6},{5,7},{6,4},{7,5},{8,10},{9,11},{10,... | collective-permute-start | bytes 688136 | tf_op jit(solution)/shard_map/ppermute | solution.py:295
  5.8 11.1 %collective-permute-start.8 = (bf16[32,2688]{1,0:T(8,128)(2,1)S(1)}, bf16[32,2688]{1,0:T(8,128)(2,1)S(1)}, u32[]{:S(2)}, u32[]{:S(2)}) collective-permute-start(bf16[32,2688]{1,0:T(8,128)(2,1)S(1)} %fusion.3), channel_id=1, source_target_pairs={{0,2},{1,3},{2,0},{3,1},{4,6},{5,7},{6,4},{7,5},{8,10},{9,11},{10,... | collective-permute-start | bytes 516104 | tf_op jit(solution)/shard_map/ppermute | solution.py:296
  13.8 28.9 %copy-start.4 = (bf16[1,128,2688]{2,1,0:T(8,128)(2,1)S(1)}, bf16[1,128,2688]{2,1,0:T(8,128)(2,1)}, u32[]{:S(2)}) copy-start(bf16[1,128,2688]{2,1,0:T(8,128)(2,1)} %param.10) | copy-start | bytes 2064388
  13.8 11.7 %collective-permute-start.3 = (bf16[896,128]{1,0:T(8,128)(2,1)S(1)}, bf16[896,128]{1,0:T(8,128)(2,1)S(1)}, u32[]{:S(2)}, u32[]{:S(2)}) collective-permute-start(bf16[896,128]{1,0:T(8,128)(2,1)S(1)} %fusion.2.rest_0_), channel_id=1, source_target_pairs={{0,4},{4,0},{8,12},{12,8},{1,5},{5,1},{9,13},{13,9},{2,6},{6,2},{1... | collective-permute-start | bytes 688136 | tf_op jit(solution)/shard_map/ppermute | solution.py:78
  14.8 13.6 %collective-permute-start.4 = (bf16[896,128]{1,0:T(8,128)(2,1)S(1)}, bf16[896,128]{1,0:T(8,128)(2,1)S(1)}, u32[]{:S(2)}, u32[]{:S(2)}) collective-permute-start(bf16[896,128]{1,0:T(8,128)(2,1)S(1)} %fusion.2.rest_0_), channel_id=1, source_target_pairs={{0,8},{4,12},{8,0},{12,4},{1,9},{5,13},{9,1},{13,5},{2,10},{6,14},... | collective-permute-start | bytes 688136 | tf_op jit(solution)/shard_map/ppermute | solution.py:78
  17.0 15.2 %collective-permute-start.9 = (bf16[32,2688]{1,0:T(8,128)(2,1)S(1)}, bf16[32,2688]{1,0:T(8,128)(2,1)S(1)}, u32[]{:S(2)}, u32[]{:S(2)}) collective-permute-start(bf16[32,2688]{1,0:T(8,128)(2,1)S(1)} %fusion.5.rest_3_), channel_id=1, source_target_pairs={{0,4},{4,0},{8,12},{12,8},{1,5},{5,1},{9,13},{13,9},{2,6},{6,2},{1... | collective-permute-start | bytes 516104 | tf_op jit(solution)/shard_map/ppermute | solution.py:78
  18.6 17.2 %collective-permute-start.10 = (bf16[32,2688]{1,0:T(8,128)(2,1)S(1)}, bf16[32,2688]{1,0:T(8,128)(2,1)S(1)}, u32[]{:S(2)}, u32[]{:S(2)}) collective-permute-start(bf16[32,2688]{1,0:T(8,128)(2,1)S(1)} %fusion.5.rest_3_), channel_id=1, source_target_pairs={{0,8},{4,12},{8,0},{12,4},{1,9},{5,13},{9,1},{13,5},{2,10},{6,14},... | collective-permute-start | bytes 516104 | tf_op jit(solution)/shard_map/ppermute | solution.py:78
  28.4 12.0 %collective-permute-start.6 = (bf16[896,128]{1,0:T(8,128)(2,1)S(1)}, bf16[896,128]{1,0:T(8,128)(2,1)S(1)}, u32[]{:S(2)}, u32[]{:S(2)}) collective-permute-start(bf16[896,128]{1,0:T(8,128)(2,1)S(1)} %collective-permute-done.4.rest_2_), channel_id=1, source_target_pairs={{0,4},{4,0},{8,12},{12,8},{1,5},{5,1},{9,13},{13,9},{2,6},{6,2},{1... | collective-permute-start | bytes 688136 | tf_op jit(solution)/shard_map/ppermute | solution.py:303
  35.8 6.9 %collective-permute-start.11 = (bf16[32,2688]{1,0:T(8,128)(2,1)S(1)}, bf16[32,2688]{1,0:T(8,128)(2,1)S(1)}, u32[]{:S(2)}, u32[]{:S(2)}) collective-permute-start(bf16[32,2688]{1,0:T(8,128)(2,1)S(1)} %collective-permute-done.10.rest_5_), channel_id=1, source_target_pairs={{0,4},{4,0},{8,12},{12,8},{1,5},{5,1},{9,13},{13,9},{2,6},{6,2},{1... | collective-permute-start | bytes 516104 | tf_op jit(solution)/shard_map/ppermute | solution.py:305
  35.8 9.5 %collective-permute-start.12 = (bf16[128,768]{1,0:T(8,128)(2,1)S(1)}, bf16[128,768]{1,0:T(8,128)(2,1)S(1)}, u32[]{:S(2)}, u32[]{:S(2)}) collective-permute-start(bf16[128,768]{1,0:T(8,128)(2,1)S(1)} %collective-permute-done.5.rest_2_), channel_id=1, source_target_pairs={{0,0},{4,4},{8,12},{12,8},{1,1},{5,5},{9,13},{13,9},{2,2},{6,6},{1... | collective-permute-start | bytes 589832 | tf_op jit(solution)/shard_map/ppermute | solution.py:307
  45.3 1.3 %copy-start = (f32[2688,128]{1,0:T(8,128)S(1)}, f32[2688,128]{1,0:T(8,128)}, u32[]{:S(2)}) copy-start(f32[2688,128]{1,0:T(8,128)} %get-tuple-element.31.counts) | copy-start | bytes 4128772
where the time goes:
time: 48.8 us; the launch traced here: 48.5 us
  waiting for transfers between devices  22.2 us (45%)
  starting transfers between devices  16 us (33%)
  Pallas kernels  7.24 us (15%)
  local copies, waits for them, and re-layouts  1.35 us (3%)
  other arithmetic  0.89 us (2%)
  between operations  0.78 us (2%)
    ppermute x6, waiting for transfers between devices, spread(): return (lax.ppermute(shard, 'ctx', ONE), lax.ppermute(shard, 'ctx', TWO))  14.4 us
    ppermute x6, starting transfers between devices, spread(): return (lax.ppermute(shard, 'ctx', ONE), lax.ppermute(shard, 'ctx', TWO))  7.12 us
    ppermute x1, waiting for transfers between devices, body(): far_down = lax.ppermute(keep_down[1] + near_down[1], 'req', ACROSS)  6.41 us
    ppermute x1, starting transfers between devices, body(): kv_three = lax.ppermute(kv_last, 'ctx', LAST)  3.92 us
    pallas_call x1, Pallas kernels, attend(): pl.pallas_call(attend_kernel, out_shape=shapes, in_specs=[spec(SMEM)] + [...  2.61 us
    ppermute x1, starting transfers between devices, body(): down_three = lax.ppermute(down_two, 'ctx', ONE)  2.26 us
    pallas_call x1, Pallas kernels, select(): pl.pallas_call(functools.partial(select_kernel, requests=ids.shape[0]), o...  1.86 us
    pallas_call x1, Pallas kernels, finish(): pl.pallas_call(finish_kernel, out_shape=jax.ShapeDtypeStruct(so_far.shape...  1.83 us
  transfers between devices with their start and end apart: 13, of which 6 were waited for; matrix products, arithmetic and copies ran while one was open for 0% of the time, Pallas kernels for 7%

commit v1 on v0

--- a/solution.py
+++ b/solution.py
@@ -16,7 +16,7 @@
 VMEM = pltpu.VMEM
 HBM = pltpu.HBM
 LOG2E = 1.0 / math.log(2.0)
-PARAMS = pltpu.CompilerParams(vmem_limit_bytes=48 * 1024 * 1024)
+PARAMS = pltpu.CompilerParams(vmem_limit_bytes=32 * 1024 * 1024)
 WHOLE = pltpu.CompilerParams(vmem_limit_bytes=52 * 1024 * 1024)
 
 

time: 48.8 us -> 47.3 us (0.969)
  Pallas kernels: 7.24 us -> 5.11 us
  starting transfers between devices: 16 us -> 17.7 us
  local copies, waits for them, and re-layouts: 1.35 us -> 0.02 us
    ppermute x6, waiting for transfers between devices: 14.4 us -> 12.8 us  [spread(): return (lax.ppermute(shard, 'ctx', ONE), lax.ppermute(shard, 'ctx', TWO))]
    unnamed x12 -> x10, local copies, waits for them, and re-layouts: 1.35 us -> 0.02 us
    pallas_call x1, Pallas kernels: 2.61 us -> 1.53 us  [attend(): pl.pallas_call(attend_kernel, out_shape=shapes, in_specs=[spec(SMEM)] + [...]
    pallas_call x1, Pallas kernels: 1.86 us -> 0.81 us  [select(): pl.pallas_call(functools.partial(select_kernel, requests=ids.shape[0]), o...]
    ppermute x1, starting transfers between devices: 2.26 us -> 3.27 us  [body(): down_three = lax.ppermute(down_two, 'ctx', ONE)]
    ppermute x1, waiting for transfers between devices: 1.34 us -> 2.2 us  [body(): up_three = lax.ppermute(up_two, 'ctx', ONE)]
    ppermute x1, starting transfers between devices: 1.55 us -> 0.77 us  [body(): far_up = lax.ppermute(keep_up[1] + near_up[1], 'req', ACROSS)]
    ppermute x1, starting transfers between devices: 0.61 us -> 1.39 us  [body(): far_down = lax.ppermute(keep_down[1] + near_down[1], 'req', ACROSS)]
  transfers between devices with their start and end apart: 13 -> 13, of which waited for: 6 -> 7; matrix products, arithmetic and copies ran while one was open for 0% -> 0% of each run, Pallas kernels for 7% -> 5%
where the time goes in v1:
time: 47.3 us; the launch traced here: 46.6 us
  waiting for transfers between devices  22.1 us (47%)
  starting transfers between devices  17.7 us (37%)
  Pallas kernels  5.11 us (11%)
  other arithmetic  0.89 us (2%)
  between operations  0.76 us (2%)
    ppermute x6, waiting for transfers between devices, spread(): return (lax.ppermute(shard, 'ctx', ONE), lax.ppermute(shard, 'ctx', TWO))  12.8 us
    ppermute x6, starting transfers between devices, spread(): return (lax.ppermute(shard, 'ctx', ONE), lax.ppermute(shard, 'ctx', TWO))  7.54 us
    ppermute x1, waiting for transfers between devices, body(): far_down = lax.ppermute(keep_down[1] + near_down[1], 'req', ACROSS)  6.36 us
    ppermute x1, starting transfers between devices, body(): kv_three = lax.ppermute(kv_last, 'ctx', LAST)  3.92 us
    ppermute x1, starting transfers between devices, body(): down_three = lax.ppermute(down_two, 'ctx', ONE)  3.27 us
    ppermute x1, waiting for transfers between devices, body(): up_three = lax.ppermute(up_two, 'ctx', ONE)  2.2 us
    pallas_call x1, Pallas kernels, finish(): pl.pallas_call(finish_kernel, out_shape=jax.ShapeDtypeStruct(so_far.shape...  1.83 us
    pallas_call x1, Pallas kernels, attend(): pl.pallas_call(attend_kernel, out_shape=shapes, in_specs=[spec(SMEM)] + [...  1.53 us
  transfers between devices with their start and end apart: 13, of which 7 were waited for; matrix products, arithmetic and copies ran while one was open for 0% of the time, Pallas kernels for 5%

profile of v1, /device:TPU:18, one launch (start us, length us, event | category | flops | bytes accessed | tf_op | source)
XLA Modules:
  0.0 46.6 jit_solution(10174400770954678636)
XLA Ops:
  0.0 0.7 %pad_add_fusion.table = s32[68]{0:T(128)S(1)} fusion(s32[64]{0:T(128)} %param.15, s32[4]{0:T(128)} %ids.1), kind=kLoop, calls=%fused_computation.10 | loop fusion | flops 68 | bytes 544 | tf_op jit(solution)/shard_map/concatenate | solution.py:67
  0.7 0.0 copy-start.4
  0.7 0.8 %shard_map.91 = (bf16[2,896,128]{2,1,0:T(8,128)(2,1)S(1)}, bf16[2,896,128]{2,1,0:T(8,128)(2,1)S(1)}, bf16[2,32,2688]{2,1,0:T(8,128)(2,1)S(1)}, bf16[2,32,2688]{2,1,0:T(8,128)(2,1)S(1)}) custom-call(s32[68]{0:T(128)S(1)} %pad_add_fusion.table, bf16[16,896,128]{2,1,0:T(8,128)(2,1)} %rest_0_.1, bf16[16,32,2688]{2,1,0:T(8,128)(2,1)} %rest_1_.1), custom_call_target="tpu_custom_call" | custom-call | tf_op jit(solution)/shard_map/pallas_call | solution.py:60
  1.6 0.8 %collective-permute-start = (bf16[2,896,128]{2,1,0:T(8,128)(2,1)S(1)}, bf16[2,896,128]{2,1,0:T(8,128)(2,1)S(1)}, u32[]{:S(2)}, u32[]{:S(2)}) collective-permute-start(bf16[2,896,128]{2,1,0:T(8,128)(2,1)S(1)} %get-tuple-element.20), channel_id=1, source_target_pairs={{0,1},{1,0},{2,3},{3,2},{4,5},{5,4},{6,7},{7,6},{8,9},{9,8},{10,11... | collective-permute-start | bytes 1376264 | tf_op jit(solution)/shard_map/ppermute | solution.py:293
  2.3 0.1 collective-permute-start.7
  2.4 0.0 copy-done.4
  2.4 1.6 %collective-permute-start.2 = (bf16[128,768]{1,0:T(8,128)(2,1)S(1)}, bf16[128,768]{1,0:T(8,128)(2,1)S(1)}, u32[]{:S(2)}, u32[]{:S(2)}) collective-permute-start(bf16[128,768]{1,0:T(8,128)(2,1)S(1)} %bitcast.18), channel_id=1, source_target_pairs={{0,4},{4,0},{8,12},{12,8},{1,5},{5,1},{9,13},{13,9},{2,6},{6,2},{1... | collective-permute-start | bytes 589832 | tf_op jit(solution)/shard_map/ppermute | solution.py:78
  4.0 0.3 collective-permute-start.5
  4.3 0.0 collective-permute-done
  4.3 0.0 copy-start
  4.3 0.0 copy-start.1
  4.3 0.0 copy-start.2
  4.4 1.4 %collective-permute-start.1 = (bf16[896,128]{1,0:T(8,128)(2,1)S(1)}, bf16[896,128]{1,0:T(8,128)(2,1)S(1)}, u32[]{:S(2)}, u32[]{:S(2)}) collective-permute-start(bf16[896,128]{1,0:T(8,128)(2,1)S(1)} %fusion), channel_id=1, source_target_pairs={{0,2},{1,3},{2,0},{3,1},{4,6},{5,7},{6,4},{7,5},{8,10},{9,11},{10,... | collective-permute-start | bytes 688136 | tf_op jit(solution)/shard_map/ppermute | solution.py:295
  5.8 0.0 collective-permute-done.7
  5.8 0.8 %collective-permute-start.8 = (bf16[32,2688]{1,0:T(8,128)(2,1)S(1)}, bf16[32,2688]{1,0:T(8,128)(2,1)S(1)}, u32[]{:S(2)}, u32[]{:S(2)}) collective-permute-start(bf16[32,2688]{1,0:T(8,128)(2,1)S(1)} %fusion.3), channel_id=1, source_target_pairs={{0,2},{1,3},{2,0},{3,1},{4,6},{5,7},{6,4},{7,5},{8,10},{9,11},{10,... | collective-permute-start | bytes 516104 | tf_op jit(solution)/shard_map/ppermute | solution.py:296
  6.6 6.4 %collective-permute-done.1 = bf16[896,128]{1,0:T(8,128)(2,1)S(1)} collective-permute-done((bf16[896,128]{1,0:T(8,128)(2,1)S(1)}, bf16[896,128]{1,0:T(8,128)(2,1)S(1)}, u32[]{:S(2)}, u32[]{:S(2)}) %collective-permute-start.1) | collective-permute-done | bytes 229408 | tf_op jit(solution)/shard_map/ppermute | solution.py:295
  13.0 0.0 copy-start.3
  13.0 0.0 collective-permute-done.2.rest_1_
  13.0 1.2 %collective-permute-start.3 = (bf16[896,128]{1,0:T(8,128)(2,1)S(1)}, bf16[896,128]{1,0:T(8,128)(2,1)S(1)}, u32[]{:S(2)}, u32[]{:S(2)}) collective-permute-start(bf16[896,128]{1,0:T(8,128)(2,1)S(1)} %fusion.2.rest_0_), channel_id=1, source_target_pairs={{0,4},{4,0},{8,12},{12,8},{1,5},{5,1},{9,13},{13,9},{2,6},{6,2},{1... | collective-permute-start | bytes 688136 | tf_op jit(solution)/shard_map/ppermute | solution.py:78
  14.2 1.9 %collective-permute-start.4 = (bf16[896,128]{1,0:T(8,128)(2,1)S(1)}, bf16[896,128]{1,0:T(8,128)(2,1)S(1)}, u32[]{:S(2)}, u32[]{:S(2)}) collective-permute-start(bf16[896,128]{1,0:T(8,128)(2,1)S(1)} %fusion.2.rest_0_), channel_id=1, source_target_pairs={{0,8},{4,12},{8,0},{12,4},{1,9},{5,13},{9,1},{13,5},{2,10},{6,14},... | collective-permute-start | bytes 688136 | tf_op jit(solution)/shard_map/ppermute | solution.py:78
  16.1 0.0 collective-permute-done.8
  16.1 1.6 %collective-permute-start.9 = (bf16[32,2688]{1,0:T(8,128)(2,1)S(1)}, bf16[32,2688]{1,0:T(8,128)(2,1)S(1)}, u32[]{:S(2)}, u32[]{:S(2)}) collective-permute-start(bf16[32,2688]{1,0:T(8,128)(2,1)S(1)} %fusion.5.rest_3_), channel_id=1, source_target_pairs={{0,4},{4,0},{8,12},{12,8},{1,5},{5,1},{9,13},{13,9},{2,6},{6,2},{1... | collective-permute-start | bytes 516104 | tf_op jit(solution)/shard_map/ppermute | solution.py:78
  17.8 0.9 %collective-permute-start.10 = (bf16[32,2688]{1,0:T(8,128)(2,1)S(1)}, bf16[32,2688]{1,0:T(8,128)(2,1)S(1)}, u32[]{:S(2)}, u32[]{:S(2)}) collective-permute-start(bf16[32,2688]{1,0:T(8,128)(2,1)S(1)} %fusion.5.rest_3_), channel_id=1, source_target_pairs={{0,8},{4,12},{8,0},{12,4},{1,9},{5,13},{9,1},{13,5},{2,10},{6,14},... | collective-permute-start | bytes 516104 | tf_op jit(solution)/shard_map/ppermute | solution.py:78
  18.7 0.0 collective-permute-done.5.rest_2_
  18.7 6.7 %collective-permute-done.3.rest_1_ = bf16[896,128]{1,0:T(8,128)(2,1)S(1)} collective-permute-done((bf16[896,128]{1,0:T(8,128)(2,1)S(1)}, bf16[896,128]{1,0:T(8,128)(2,1)S(1)}, u32[]{:S(2)}, u32[]{:S(2)}) %collective-permute-start.3) | collective-permute-done | bytes 229408 | tf_op jit(solution)/shard_map/ppermute | solution.py:78
  25.3 2.1 %collective-permute-done.4.rest_2_ = bf16[896,128]{1,0:T(8,128)(2,1)S(1)} collective-permute-done((bf16[896,128]{1,0:T(8,128)(2,1)S(1)}, bf16[896,128]{1,0:T(8,128)(2,1)S(1)}, u32[]{:S(2)}, u32[]{:S(2)}) %collective-permute-start.4) | collective-permute-done | bytes 229408 | tf_op jit(solution)/shard_map/ppermute | solution.py:78
  27.4 3.3 %collective-permute-start.6 = (bf16[896,128]{1,0:T(8,128)(2,1)S(1)}, bf16[896,128]{1,0:T(8,128)(2,1)S(1)}, u32[]{:S(2)}, u32[]{:S(2)}) collective-permute-start(bf16[896,128]{1,0:T(8,128)(2,1)S(1)} %collective-permute-done.4.rest_2_), channel_id=1, source_target_pairs={{0,4},{4,0},{8,12},{12,8},{1,5},{5,1},{9,13},{13,9},{2,6},{6,2},{1... | collective-permute-start | bytes 688136 | tf_op jit(solution)/shard_map/ppermute | solution.py:303
  30.7 1.6 %collective-permute-done.9.rest_4_ = bf16[32,2688]{1,0:T(8,128)(2,1)S(1)} collective-permute-done((bf16[32,2688]{1,0:T(8,128)(2,1)S(1)}, bf16[32,2688]{1,0:T(8,128)(2,1)S(1)}, u32[]{:S(2)}, u32[]{:S(2)}) %collective-permute-start.9) | collective-permute-done | bytes 172064 | tf_op jit(solution)/shard_map/ppermute | solution.py:78
  32.2 2.5 %collective-permute-done.10.rest_5_ = bf16[32,2688]{1,0:T(8,128)(2,1)S(1)} collective-permute-done((bf16[32,2688]{1,0:T(8,128)(2,1)S(1)}, bf16[32,2688]{1,0:T(8,128)(2,1)S(1)}, u32[]{:S(2)}, u32[]{:S(2)}) %collective-permute-start.10) | collective-permute-done | bytes 172064 | tf_op jit(solution)/shard_map/ppermute | solution.py:78
  34.8 0.0 collective-permute-start.11
  34.8 3.9 %collective-permute-start.12 = (bf16[128,768]{1,0:T(8,128)(2,1)S(1)}, bf16[128,768]{1,0:T(8,128)(2,1)S(1)}, u32[]{:S(2)}, u32[]{:S(2)}) collective-permute-start(bf16[128,768]{1,0:T(8,128)(2,1)S(1)} %collective-permute-done.5.rest_2_), channel_id=1, source_target_pairs={{0,0},{4,4},{8,12},{12,8},{1,1},{5,5},{9,13},{13,9},{2,2},{6,6},{1... | collective-permute-start | bytes 589832 | tf_op jit(solution)/shard_map/ppermute | solution.py:307
  39.3 0.0 collective-permute-done.6.rest_3_
  39.4 0.0 copy-done
  39.4 0.0 copy-done.1
  39.4 0.0 copy-done.2
  39.4 0.9 %shard_map.92.low = bf16[128,128]{1,0:T(8,128)(2,1)S(1)} custom-call(s32[4]{0:T(128)S(1)} %copy-done.1, s32[64]{0:T(128)S(1)} %copy-done.2, bf16[128,3584]{1,0:T(8,128)(2,1)S(1)} %bitcast.16, bf16[896,128]{1,0:T(8,128)(2,1)S(1)} %fusion.2.rest_0_, bf16[896,128]{1,0:T(8,128)(2,1)S(1)} %collective-permute-done.3.rest_1_, ...), custom_call_target="tpu_custom_call" | custom-call | flops 134217728 | bytes 4194304 | tf_op jit(solution)/shard_map/pallas_call | solution.py:97
  40.3 2.2 %collective-permute-done.11.rest_6_ = bf16[32,2688]{1,0:T(8,128)(2,1)S(1)} collective-permute-done((bf16[32,2688]{1,0:T(8,128)(2,1)S(1)}, bf16[32,2688]{1,0:T(8,128)(2,1)S(1)}, u32[]{:S(2)}, u32[]{:S(2)}) %collective-permute-start.11) | collective-permute-done | bytes 172064 | tf_op jit(solution)/shard_map/ppermute | solution.py:305
  42.5 0.0 copy-done.3
  42.5 1.5 %shard_map.93 = (bf16[128,2688]{1,0:T(8,128)(2,1)}, bf16[2688,128]{1,0:T(8,128)(2,1)S(1)}, f32[2688,128]{1,0:T(8,128)S(1)}, f32[2688,128]{1,0:T(8,128)S(1)}, f32[2688,128]{1,0:T(8,128)S(1)}) custom-call(s32[1]{0:T(128)S(6)} %copy.12.lengths, bf16[128,2688]{1,0:T(8,128)(2,1)S(1)} %bitcast.17, bf16[128,128]{1,0:T(8,128)(2,1)S(1)} %shard_map.92.low, ...), custom_call_target="tpu_custom_call" | custom-call | flops 1073741824 | bytes 4194304 | tf_op jit(solution)/shard_map/pallas_call | solution.py:207
  44.1 0.7 %collective-permute-done.12.kv = bf16[128,768]{1,0:T(8,128)(2,1)S(1)} collective-permute-done((bf16[128,768]{1,0:T(8,128)(2,1)S(1)}, bf16[128,768]{1,0:T(8,128)(2,1)S(1)}, u32[]{:S(2)}, u32[]{:S(2)}) %collective-permute-start.12) | collective-permute-done | bytes 196640 | tf_op jit(solution)/shard_map/ppermute | solution.py:307
  44.8 1.8 %shard_map.94 = bf16[128,2688]{1,0:T(8,128)(2,1)} custom-call(s32[1]{0:T(128)S(6)} %copy.12.lengths, bf16[128,2688]{1,0:T(8,128)(2,1)} %get-tuple-element.27.so_far, bf16[2688,128]{1,0:T(8,128)(2,1)S(1)} %get-tuple-element.28.queries, f32[2688,128]{1,0:T(8,128)S(1)} %get-tuple-element.29.sums, ...), custom_call_target="tpu_custom_call", output_to_operand_aliasing={{}: (1, {})} | custom-call | flops 268435456 | bytes 2097152 | tf_op jit(solution)/shard_map/pallas_call | solution.py:260
  (4 shorter events, 0.1 us)
Async XLA Ops:
  0.7 1.7 %copy-start.4 = (bf16[1,128,768]{2,1,0:T(8,128)(2,1)S(1)}, bf16[1,128,768]{2,1,0:T(8,128)(2,1)}, u32[]{:S(2)}) copy-start(bf16[1,128,768]{2,1,0:T(8,128)(2,1)} %param.11) | copy-start | bytes 589828
  1.6 2.8 %collective-permute-start = (bf16[2,896,128]{2,1,0:T(8,128)(2,1)S(1)}, bf16[2,896,128]{2,1,0:T(8,128)(2,1)S(1)}, u32[]{:S(2)}, u32[]{:S(2)}) collective-permute-start(bf16[2,896,128]{2,1,0:T(8,128)(2,1)S(1)} %get-tuple-element.20), channel_id=1, source_target_pairs={{0,1},{1,0},{2,3},{3,2},{4,5},{5,4},{6,7},{7,6},{8,9},{9,8},{10,11... | collective-permute-start | bytes 1376264 | tf_op jit(solution)/shard_map/ppermute | solution.py:293
  2.3 3.4 %collective-permute-start.7 = (bf16[2,32,2688]{2,1,0:T(8,128)(2,1)S(1)}, bf16[2,32,2688]{2,1,0:T(8,128)(2,1)S(1)}, u32[]{:S(2)}, u32[]{:S(2)}) collective-permute-start(bf16[2,32,2688]{2,1,0:T(8,128)(2,1)S(1)} %get-tuple-element.25), channel_id=1, source_target_pairs={{0,1},{1,0},{2,3},{3,2},{4,5},{5,4},{6,7},{7,6},{8,9},{9,8},{10,11... | collective-permute-start | bytes 1032200 | tf_op jit(solution)/shard_map/ppermute | solution.py:294
  2.4 10.6 %collective-permute-start.2 = (bf16[128,768]{1,0:T(8,128)(2,1)S(1)}, bf16[128,768]{1,0:T(8,128)(2,1)S(1)}, u32[]{:S(2)}, u32[]{:S(2)}) collective-permute-start(bf16[128,768]{1,0:T(8,128)(2,1)S(1)} %bitcast.18), channel_id=1, source_target_pairs={{0,4},{4,0},{8,12},{12,8},{1,5},{5,1},{9,13},{13,9},{2,6},{6,2},{1... | collective-permute-start | bytes 589832 | tf_op jit(solution)/shard_map/ppermute | solution.py:78
  4.0 14.7 %collective-permute-start.5 = (bf16[128,768]{1,0:T(8,128)(2,1)S(1)}, bf16[128,768]{1,0:T(8,128)(2,1)S(1)}, u32[]{:S(2)}, u32[]{:S(2)}) collective-permute-start(bf16[128,768]{1,0:T(8,128)(2,1)S(1)} %bitcast.19), channel_id=1, source_target_pairs={{0,8},{4,12},{8,0},{12,4},{1,9},{5,13},{9,1},{13,5},{2,10},{6,14},... | collective-permute-start | bytes 589832 | tf_op jit(solution)/shard_map/ppermute | solution.py:78
  4.3 35.0 %copy-start = (bf16[1,128,3584]{2,1,0:T(8,128)(2,1)S(1)}, bf16[1,128,3584]{2,1,0:T(8,128)(2,1)}, u32[]{:S(2)}) copy-start(bf16[1,128,3584]{2,1,0:T(8,128)(2,1)} %param.9) | copy-start | bytes 2752516
  4.3 35.0 %copy-start.1 = (s32[4]{0:T(128)S(1)}, s32[4]{0:T(128)}, u32[]{:S(2)}) copy-start(s32[4]{0:T(128)} %ids.1) | copy-start | bytes 52
  4.3 35.1 %copy-start.2 = (s32[64]{0:T(128)S(1)}, s32[64]{0:T(128)}, u32[]{:S(2)}) copy-start(s32[64]{0:T(128)} %ranks.1) | copy-start | bytes 772
  4.4 8.6 %collective-permute-start.1 = (bf16[896,128]{1,0:T(8,128)(2,1)S(1)}, bf16[896,128]{1,0:T(8,128)(2,1)S(1)}, u32[]{:S(2)}, u32[]{:S(2)}) collective-permute-start(bf16[896,128]{1,0:T(8,128)(2,1)S(1)} %fusion), channel_id=1, source_target_pairs={{0,2},{1,3},{2,0},{3,1},{4,6},{5,7},{6,4},{7,5},{8,10},{9,11},{10,... | collective-permute-start | bytes 688136 | tf_op jit(solution)/shard_map/ppermute | solution.py:295
  5.8 10.3 %collective-permute-start.8 = (bf16[32,2688]{1,0:T(8,128)(2,1)S(1)}, bf16[32,2688]{1,0:T(8,128)(2,1)S(1)}, u32[]{:S(2)}, u32[]{:S(2)}) collective-permute-start(bf16[32,2688]{1,0:T(8,128)(2,1)S(1)} %fusion.3), channel_id=1, source_target_pairs={{0,2},{1,3},{2,0},{3,1},{4,6},{5,7},{6,4},{7,5},{8,10},{9,11},{10,... | collective-permute-start | bytes 516104 | tf_op jit(solution)/shard_map/ppermute | solution.py:296
  13.0 29.6 %copy-start.3 = (bf16[1,128,2688]{2,1,0:T(8,128)(2,1)S(1)}, bf16[1,128,2688]{2,1,0:T(8,128)(2,1)}, u32[]{:S(2)}) copy-start(bf16[1,128,2688]{2,1,0:T(8,128)(2,1)} %param.10) | copy-start | bytes 2064388
  13.0 12.4 %collective-permute-start.3 = (bf16[896,128]{1,0:T(8,128)(2,1)S(1)}, bf16[896,128]{1,0:T(8,128)(2,1)S(1)}, u32[]{:S(2)}, u32[]{:S(2)}) collective-permute-start(bf16[896,128]{1,0:T(8,128)(2,1)S(1)} %fusion.2.rest_0_), channel_id=1, source_target_pairs={{0,4},{4,0},{8,12},{12,8},{1,5},{5,1},{9,13},{13,9},{2,6},{6,2},{1... | collective-permute-start | bytes 688136 | tf_op jit(solution)/shard_map/ppermute | solution.py:78
  14.2 13.2 %collective-permute-start.4 = (bf16[896,128]{1,0:T(8,128)(2,1)S(1)}, bf16[896,128]{1,0:T(8,128)(2,1)S(1)}, u32[]{:S(2)}, u32[]{:S(2)}) collective-permute-start(bf16[896,128]{1,0:T(8,128)(2,1)S(1)} %fusion.2.rest_0_), channel_id=1, source_target_pairs={{0,8},{4,12},{8,0},{12,4},{1,9},{5,13},{9,1},{13,5},{2,10},{6,14},... | collective-permute-start | bytes 688136 | tf_op jit(solution)/shard_map/ppermute | solution.py:78
  16.1 16.1 %collective-permute-start.9 = (bf16[32,2688]{1,0:T(8,128)(2,1)S(1)}, bf16[32,2688]{1,0:T(8,128)(2,1)S(1)}, u32[]{:S(2)}, u32[]{:S(2)}) collective-permute-start(bf16[32,2688]{1,0:T(8,128)(2,1)S(1)} %fusion.5.rest_3_), channel_id=1, source_target_pairs={{0,4},{4,0},{8,12},{12,8},{1,5},{5,1},{9,13},{13,9},{2,6},{6,2},{1... | collective-permute-start | bytes 516104 | tf_op jit(solution)/shard_map/ppermute | solution.py:78
  17.8 17.0 %collective-permute-start.10 = (bf16[32,2688]{1,0:T(8,128)(2,1)S(1)}, bf16[32,2688]{1,0:T(8,128)(2,1)S(1)}, u32[]{:S(2)}, u32[]{:S(2)}) collective-permute-start(bf16[32,2688]{1,0:T(8,128)(2,1)S(1)} %fusion.5.rest_3_), channel_id=1, source_target_pairs={{0,8},{4,12},{8,0},{12,4},{1,9},{5,13},{9,1},{13,5},{2,10},{6,14},... | collective-permute-start | bytes 516104 | tf_op jit(solution)/shard_map/ppermute | solution.py:78
  27.4 12.0 %collective-permute-start.6 = (bf16[896,128]{1,0:T(8,128)(2,1)S(1)}, bf16[896,128]{1,0:T(8,128)(2,1)S(1)}, u32[]{:S(2)}, u32[]{:S(2)}) collective-permute-start(bf16[896,128]{1,0:T(8,128)(2,1)S(1)} %collective-permute-done.4.rest_2_), channel_id=1, source_target_pairs={{0,4},{4,0},{8,12},{12,8},{1,5},{5,1},{9,13},{13,9},{2,6},{6,2},{1... | collective-permute-start | bytes 688136 | tf_op jit(solution)/shard_map/ppermute | solution.py:303
  34.8 7.8 %collective-permute-start.11 = (bf16[32,2688]{1,0:T(8,128)(2,1)S(1)}, bf16[32,2688]{1,0:T(8,128)(2,1)S(1)}, u32[]{:S(2)}, u32[]{:S(2)}) collective-permute-start(bf16[32,2688]{1,0:T(8,128)(2,1)S(1)} %collective-permute-done.10.rest_5_), channel_id=1, source_target_pairs={{0,4},{4,0},{8,12},{12,8},{1,5},{5,1},{9,13},{13,9},{2,6},{6,2},{1... | collective-permute-start | bytes 516104 | tf_op jit(solution)/shard_map/ppermute | solution.py:305
  34.8 10.0 %collective-permute-start.12 = (bf16[128,768]{1,0:T(8,128)(2,1)S(1)}, bf16[128,768]{1,0:T(8,128)(2,1)S(1)}, u32[]{:S(2)}, u32[]{:S(2)}) collective-permute-start(bf16[128,768]{1,0:T(8,128)(2,1)S(1)} %collective-permute-done.5.rest_2_), channel_id=1, source_target_pairs={{0,0},{4,4},{8,12},{12,8},{1,1},{5,5},{9,13},{13,9},{2,2},{6,6},{1... | collective-permute-start | bytes 589832 | tf_op jit(solution)/shard_map/ppermute | solution.py:307

commit v2 on v1

--- a/solution.py
+++ b/solution.py
@@ -299,11 +299,11 @@
     down_one, down_two = spread(down)
     up = keep_up[0] + near_up[0] + far_up
     up_one, up_two = spread(up)
-    down_two = lax.optimization_barrier((down_two, down_one, kv_two))[0]
+    down_two = lax.optimization_barrier((down_two, kv_two))[0]
     down_three = lax.ppermute(down_two, "ctx", ONE)
-    up_two = lax.optimization_barrier((up_two, up_one))[0]
+    up_two = lax.optimization_barrier((up_two, down_one))[0]
     up_three = lax.ppermute(up_two, "ctx", ONE)
-    kv_last = lax.optimization_barrier((kv_two, up_two))[0]
+    kv_last = lax.optimization_barrier((kv_two, up_two, up_one))[0]
     kv_three = lax.ppermute(kv_last, "ctx", LAST)
     downs = [down, down_one, down_two, down_three]
     ups = [up, up_one, up_two, up_three]

time: 47.3 us -> 47.4 us (level)
  Pallas kernels: 5.11 us -> 6.15 us
  waiting for transfers between devices: 22.1 us -> 21.5 us
    ppermute x1, starting transfers between devices: 0.01 us -> 2.3 us  [body(): up_three = lax.ppermute(up_two, 'ctx', ONE)]
    ppermute x6, waiting for transfers between devices: 12.8 us -> 10.7 us  [spread(): return (lax.ppermute(shard, 'ctx', ONE), lax.ppermute(shard, 'ctx', TWO))]
    ppermute x1, waiting for transfers between devices: 0.01 us -> 1.07 us  [body(): down_three = lax.ppermute(down_two, 'ctx', ONE)]
    pallas_call x1, Pallas kernels: 0.81 us -> 1.86 us  [select(): pl.pallas_call(functools.partial(select_kernel, requests=ids.shape[0]), o...]
    ppermute x1, starting transfers between devices: 3.92 us -> 2.87 us  [body(): kv_three = lax.ppermute(kv_last, 'ctx', LAST)]
    ppermute x1, starting transfers between devices: 0.77 us -> 1.76 us  [body(): far_up = lax.ppermute(keep_up[1] + near_up[1], 'req', ACROSS)]
    ppermute x1, starting transfers between devices: 1.39 us -> 0.4 us  [body(): far_down = lax.ppermute(keep_down[1] + near_down[1], 'req', ACROSS)]
    ppermute x1, starting transfers between devices: 3.27 us -> 2.36 us  [body(): down_three = lax.ppermute(down_two, 'ctx', ONE)]
where the time goes in v2:
time: 47.4 us; the launch traced here: 46.7 us
  waiting for transfers between devices  21.5 us (45%)
  starting transfers between devices  17.4 us (37%)
  Pallas kernels  6.15 us (13%)
  other arithmetic  0.89 us (2%)
  between operations  0.73 us (2%)
    ppermute x6, waiting for transfers between devices, spread(): return (lax.ppermute(shard, 'ctx', ONE), lax.ppermute(shard, 'ctx', TWO))  10.7 us
    ppermute x6, starting transfers between devices, spread(): return (lax.ppermute(shard, 'ctx', ONE), lax.ppermute(shard, 'ctx', TWO))  7.12 us
    ppermute x1, waiting for transfers between devices, body(): far_down = lax.ppermute(keep_down[1] + near_down[1], 'req', ACROSS)  6.41 us
    ppermute x1, starting transfers between devices, body(): kv_three = lax.ppermute(kv_last, 'ctx', LAST)  2.87 us
    ppermute x1, waiting for transfers between devices, body(): up_three = lax.ppermute(up_two, 'ctx', ONE)  2.7 us
    ppermute x1, starting transfers between devices, body(): down_three = lax.ppermute(down_two, 'ctx', ONE)  2.36 us
    ppermute x1, starting transfers between devices, body(): up_three = lax.ppermute(up_two, 'ctx', ONE)  2.3 us
    pallas_call x1, Pallas kernels, select(): pl.pallas_call(functools.partial(select_kernel, requests=ids.shape[0]), o...  1.86 us
  transfers between devices with their start and end apart: 13, of which 7 were waited for; matrix products, arithmetic and copies ran while one was open for 0% of the time, Pallas kernels for 5%

profile of v2, /device:TPU:18, one launch (start us, length us, event | category | flops | bytes accessed | tf_op | source)
XLA Modules:
  0.0 46.7 jit_solution(2758154227149365439)
XLA Ops:
  0.0 0.7 %pad_add_fusion.table = s32[68]{0:T(128)S(1)} fusion(s32[64]{0:T(128)} %param.15, s32[4]{0:T(128)} %ids.1), kind=kLoop, calls=%fused_computation.10 | loop fusion | flops 68 | bytes 544 | tf_op jit(solution)/shard_map/concatenate | solution.py:67
  0.7 0.0 copy-start.4
  0.7 1.9 %shard_map.91 = (bf16[2,896,128]{2,1,0:T(8,128)(2,1)S(1)}, bf16[2,896,128]{2,1,0:T(8,128)(2,1)S(1)}, bf16[2,32,2688]{2,1,0:T(8,128)(2,1)S(1)}, bf16[2,32,2688]{2,1,0:T(8,128)(2,1)S(1)}) custom-call(s32[68]{0:T(128)S(1)} %pad_add_fusion.table, bf16[16,896,128]{2,1,0:T(8,128)(2,1)} %rest_0_.1, bf16[16,32,2688]{2,1,0:T(8,128)(2,1)} %rest_1_.1), custom_call_target="tpu_custom_call" | custom-call | tf_op jit(solution)/shard_map/pallas_call | solution.py:60
  2.6 0.1 collective-permute-start
  2.7 0.5 %collective-permute-start.7 = (bf16[2,32,2688]{2,1,0:T(8,128)(2,1)S(1)}, bf16[2,32,2688]{2,1,0:T(8,128)(2,1)S(1)}, u32[]{:S(2)}, u32[]{:S(2)}) collective-permute-start(bf16[2,32,2688]{2,1,0:T(8,128)(2,1)S(1)} %get-tuple-element.25), channel_id=1, source_target_pairs={{0,1},{1,0},{2,3},{3,2},{4,5},{5,4},{6,7},{7,6},{8,9},{9,8},{10,11... | collective-permute-start | bytes 1032200 | tf_op jit(solution)/shard_map/ppermute | solution.py:294
  3.2 0.0 copy-done.4
  3.2 1.6 %collective-permute-start.2 = (bf16[128,768]{1,0:T(8,128)(2,1)S(1)}, bf16[128,768]{1,0:T(8,128)(2,1)S(1)}, u32[]{:S(2)}, u32[]{:S(2)}) collective-permute-start(bf16[128,768]{1,0:T(8,128)(2,1)S(1)} %bitcast.18), channel_id=1, source_target_pairs={{0,4},{4,0},{8,12},{12,8},{1,5},{5,1},{9,13},{13,9},{2,6},{6,2},{1... | collective-permute-start | bytes 589832 | tf_op jit(solution)/shard_map/ppermute | solution.py:78
  4.8 0.3 collective-permute-start.5
  5.1 0.0 collective-permute-done
  5.1 0.0 copy-start
  5.1 0.0 copy-start.1
  5.1 0.0 copy-start.2
  5.2 0.4 collective-permute-start.1
  5.6 0.0 collective-permute-done.7
  5.6 1.8 %collective-permute-start.8 = (bf16[32,2688]{1,0:T(8,128)(2,1)S(1)}, bf16[32,2688]{1,0:T(8,128)(2,1)S(1)}, u32[]{:S(2)}, u32[]{:S(2)}) collective-permute-start(bf16[32,2688]{1,0:T(8,128)(2,1)S(1)} %fusion.3), channel_id=1, source_target_pairs={{0,2},{1,3},{2,0},{3,1},{4,6},{5,7},{6,4},{7,5},{8,10},{9,11},{10,... | collective-permute-start | bytes 516104 | tf_op jit(solution)/shard_map/ppermute | solution.py:296
  7.4 6.4 %collective-permute-done.1 = bf16[896,128]{1,0:T(8,128)(2,1)S(1)} collective-permute-done((bf16[896,128]{1,0:T(8,128)(2,1)S(1)}, bf16[896,128]{1,0:T(8,128)(2,1)S(1)}, u32[]{:S(2)}, u32[]{:S(2)}) %collective-permute-start.1) | collective-permute-done | bytes 229408 | tf_op jit(solution)/shard_map/ppermute | solution.py:295
  13.8 0.0 copy-start.3
  13.8 0.0 collective-permute-done.2.rest_1_
  13.8 2.7 %collective-permute-start.4 = (bf16[896,128]{1,0:T(8,128)(2,1)S(1)}, bf16[896,128]{1,0:T(8,128)(2,1)S(1)}, u32[]{:S(2)}, u32[]{:S(2)}) collective-permute-start(bf16[896,128]{1,0:T(8,128)(2,1)S(1)} %fusion.2.rest_0_), channel_id=1, source_target_pairs={{0,8},{4,12},{8,0},{12,4},{1,9},{5,13},{9,1},{13,5},{2,10},{6,14},... | collective-permute-start | bytes 688136 | tf_op jit(solution)/shard_map/ppermute | solution.py:78
  16.5 0.4 collective-permute-start.3
  16.9 0.0 collective-permute-done.8
  17.0 1.7 %collective-permute-start.10 = (bf16[32,2688]{1,0:T(8,128)(2,1)S(1)}, bf16[32,2688]{1,0:T(8,128)(2,1)S(1)}, u32[]{:S(2)}, u32[]{:S(2)}) collective-permute-start(bf16[32,2688]{1,0:T(8,128)(2,1)S(1)} %fusion.5.rest_3_), channel_id=1, source_target_pairs={{0,8},{4,12},{8,0},{12,4},{1,9},{5,13},{9,1},{13,5},{2,10},{6,14},... | collective-permute-start | bytes 516104 | tf_op jit(solution)/shard_map/ppermute | solution.py:78
  18.6 0.4 collective-permute-start.9
  19.1 0.0 collective-permute-done.5.rest_2_
  19.1 7.8 %collective-permute-done.4.rest_2_ = bf16[896,128]{1,0:T(8,128)(2,1)S(1)} collective-permute-done((bf16[896,128]{1,0:T(8,128)(2,1)S(1)}, bf16[896,128]{1,0:T(8,128)(2,1)S(1)}, u32[]{:S(2)}, u32[]{:S(2)}) %collective-permute-start.4) | collective-permute-done | bytes 229408 | tf_op jit(solution)/shard_map/ppermute | solution.py:78
  26.9 2.4 %collective-permute-start.6 = (bf16[896,128]{1,0:T(8,128)(2,1)S(1)}, bf16[896,128]{1,0:T(8,128)(2,1)S(1)}, u32[]{:S(2)}, u32[]{:S(2)}) collective-permute-start(bf16[896,128]{1,0:T(8,128)(2,1)S(1)} %collective-permute-done.4.rest_2_), channel_id=1, source_target_pairs={{0,4},{4,0},{8,12},{12,8},{1,5},{5,1},{9,13},{13,9},{2,6},{6,2},{1... | collective-permute-start | bytes 688136 | tf_op jit(solution)/shard_map/ppermute | solution.py:303
  29.2 2.8 %collective-permute-done.10.rest_5_ = bf16[32,2688]{1,0:T(8,128)(2,1)S(1)} collective-permute-done((bf16[32,2688]{1,0:T(8,128)(2,1)S(1)}, bf16[32,2688]{1,0:T(8,128)(2,1)S(1)}, u32[]{:S(2)}, u32[]{:S(2)}) %collective-permute-start.10) | collective-permute-done | bytes 172064 | tf_op jit(solution)/shard_map/ppermute | solution.py:78
  32.0 0.0 collective-permute-done.3.rest_1_
  32.0 2.3 %collective-permute-start.11 = (bf16[32,2688]{1,0:T(8,128)(2,1)S(1)}, bf16[32,2688]{1,0:T(8,128)(2,1)S(1)}, u32[]{:S(2)}, u32[]{:S(2)}) collective-permute-start(bf16[32,2688]{1,0:T(8,128)(2,1)S(1)} %collective-permute-done.10.rest_5_), channel_id=1, source_target_pairs={{0,4},{4,0},{8,12},{12,8},{1,5},{5,1},{9,13},{13,9},{2,6},{6,2},{1... | collective-permute-start | bytes 516104 | tf_op jit(solution)/shard_map/ppermute | solution.py:305
  34.3 0.2 collective-permute-done.9.rest_4_
  34.5 2.9 %collective-permute-start.12 = (bf16[128,768]{1,0:T(8,128)(2,1)S(1)}, bf16[128,768]{1,0:T(8,128)(2,1)S(1)}, u32[]{:S(2)}, u32[]{:S(2)}) collective-permute-start(bf16[128,768]{1,0:T(8,128)(2,1)S(1)} %collective-permute-done.5.rest_2_), channel_id=1, source_target_pairs={{0,0},{4,4},{8,12},{12,8},{1,1},{5,5},{9,13},{13,9},{2,2},{6,6},{1... | collective-permute-start | bytes 589832 | tf_op jit(solution)/shard_map/ppermute | solution.py:307
  38.0 1.1 %collective-permute-done.6.rest_3_ = bf16[896,128]{1,0:T(8,128)(2,1)S(1)} collective-permute-done((bf16[896,128]{1,0:T(8,128)(2,1)S(1)}, bf16[896,128]{1,0:T(8,128)(2,1)S(1)}, u32[]{:S(2)}, u32[]{:S(2)}) %collective-permute-start.6) | collective-permute-done | bytes 229408 | tf_op jit(solution)/shard_map/ppermute | solution.py:303
  39.1 0.0 copy-done
  39.1 0.0 copy-done.1
  39.1 0.0 copy-done.2
  39.1 0.9 %shard_map.92.low = bf16[128,128]{1,0:T(8,128)(2,1)S(1)} custom-call(s32[4]{0:T(128)S(1)} %copy-done.1, s32[64]{0:T(128)S(1)} %copy-done.2, bf16[128,3584]{1,0:T(8,128)(2,1)S(1)} %bitcast.16, bf16[896,128]{1,0:T(8,128)(2,1)S(1)} %fusion.2.rest_0_, bf16[896,128]{1,0:T(8,128)(2,1)S(1)} %collective-permute-done.3.rest_1_, ...), custom_call_target="tpu_custom_call" | custom-call | flops 134217728 | bytes 4194304 | tf_op jit(solution)/shard_map/pallas_call | solution.py:97
  40.0 2.7 %collective-permute-done.11.rest_6_ = bf16[32,2688]{1,0:T(8,128)(2,1)S(1)} collective-permute-done((bf16[32,2688]{1,0:T(8,128)(2,1)S(1)}, bf16[32,2688]{1,0:T(8,128)(2,1)S(1)}, u32[]{:S(2)}, u32[]{:S(2)}) %collective-permute-start.11) | collective-permute-done | bytes 172064 | tf_op jit(solution)/shard_map/ppermute | solution.py:305
  42.7 0.0 copy-done.3
  42.7 1.5 %shard_map.93 = (bf16[128,2688]{1,0:T(8,128)(2,1)}, bf16[2688,128]{1,0:T(8,128)(2,1)S(1)}, f32[2688,128]{1,0:T(8,128)S(1)}, f32[2688,128]{1,0:T(8,128)S(1)}, f32[2688,128]{1,0:T(8,128)S(1)}) custom-call(s32[1]{0:T(128)S(6)} %copy.12.lengths, bf16[128,2688]{1,0:T(8,128)(2,1)S(1)} %bitcast.17, bf16[128,128]{1,0:T(8,128)(2,1)S(1)} %shard_map.92.low, ...), custom_call_target="tpu_custom_call" | custom-call | flops 1073741824 | bytes 4194304 | tf_op jit(solution)/shard_map/pallas_call | solution.py:207
  44.3 0.6 %collective-permute-done.12.kv = bf16[128,768]{1,0:T(8,128)(2,1)S(1)} collective-permute-done((bf16[128,768]{1,0:T(8,128)(2,1)S(1)}, bf16[128,768]{1,0:T(8,128)(2,1)S(1)}, u32[]{:S(2)}, u32[]{:S(2)}) %collective-permute-start.12) | collective-permute-done | bytes 196640 | tf_op jit(solution)/shard_map/ppermute | solution.py:307
  44.8 1.8 %shard_map.94 = bf16[128,2688]{1,0:T(8,128)(2,1)} custom-call(s32[1]{0:T(128)S(6)} %copy.12.lengths, bf16[128,2688]{1,0:T(8,128)(2,1)} %get-tuple-element.27.so_far, bf16[2688,128]{1,0:T(8,128)(2,1)S(1)} %get-tuple-element.28.queries, f32[2688,128]{1,0:T(8,128)S(1)} %get-tuple-element.29.sums, ...), custom_call_target="tpu_custom_call", output_to_operand_aliasing={{}: (1, {})} | custom-call | flops 268435456 | bytes 2097152 | tf_op jit(solution)/shard_map/pallas_call | solution.py:260
  (4 shorter events, 0.1 us)
Async XLA Ops:
  0.7 2.5 %copy-start.4 = (bf16[1,128,768]{2,1,0:T(8,128)(2,1)S(1)}, bf16[1,128,768]{2,1,0:T(8,128)(2,1)}, u32[]{:S(2)}) copy-start(bf16[1,128,768]{2,1,0:T(8,128)(2,1)} %param.11) | copy-start | bytes 589828
  2.6 2.5 %collective-permute-start = (bf16[2,896,128]{2,1,0:T(8,128)(2,1)S(1)}, bf16[2,896,128]{2,1,0:T(8,128)(2,1)S(1)}, u32[]{:S(2)}, u32[]{:S(2)}) collective-permute-start(bf16[2,896,128]{2,1,0:T(8,128)(2,1)S(1)} %get-tuple-element.20), channel_id=1, source_target_pairs={{0,1},{1,0},{2,3},{3,2},{4,5},{5,4},{6,7},{7,6},{8,9},{9,8},{10,11... | collective-permute-start | bytes 1376264 | tf_op jit(solution)/shard_map/ppermute | solution.py:293
  2.7 2.9 %collective-permute-start.7 = (bf16[2,32,2688]{2,1,0:T(8,128)(2,1)S(1)}, bf16[2,32,2688]{2,1,0:T(8,128)(2,1)S(1)}, u32[]{:S(2)}, u32[]{:S(2)}) collective-permute-start(bf16[2,32,2688]{2,1,0:T(8,128)(2,1)S(1)} %get-tuple-element.25), channel_id=1, source_target_pairs={{0,1},{1,0},{2,3},{3,2},{4,5},{5,4},{6,7},{7,6},{8,9},{9,8},{10,11... | collective-permute-start | bytes 1032200 | tf_op jit(solution)/shard_map/ppermute | solution.py:294
  3.2 10.6 %collective-permute-start.2 = (bf16[128,768]{1,0:T(8,128)(2,1)S(1)}, bf16[128,768]{1,0:T(8,128)(2,1)S(1)}, u32[]{:S(2)}, u32[]{:S(2)}) collective-permute-start(bf16[128,768]{1,0:T(8,128)(2,1)S(1)} %bitcast.18), channel_id=1, source_target_pairs={{0,4},{4,0},{8,12},{12,8},{1,5},{5,1},{9,13},{13,9},{2,6},{6,2},{1... | collective-permute-start | bytes 589832 | tf_op jit(solution)/shard_map/ppermute | solution.py:78
  4.8 14.3 %collective-permute-start.5 = (bf16[128,768]{1,0:T(8,128)(2,1)S(1)}, bf16[128,768]{1,0:T(8,128)(2,1)S(1)}, u32[]{:S(2)}, u32[]{:S(2)}) collective-permute-start(bf16[128,768]{1,0:T(8,128)(2,1)S(1)} %bitcast.19), channel_id=1, source_target_pairs={{0,8},{4,12},{8,0},{12,4},{1,9},{5,13},{9,1},{13,5},{2,10},{6,14},... | collective-permute-start | bytes 589832 | tf_op jit(solution)/shard_map/ppermute | solution.py:78
  5.1 34.0 %copy-start = (bf16[1,128,3584]{2,1,0:T(8,128)(2,1)S(1)}, bf16[1,128,3584]{2,1,0:T(8,128)(2,1)}, u32[]{:S(2)}) copy-start(bf16[1,128,3584]{2,1,0:T(8,128)(2,1)} %param.9) | copy-start | bytes 2752516
  5.1 34.0 %copy-start.1 = (s32[4]{0:T(128)S(1)}, s32[4]{0:T(128)}, u32[]{:S(2)}) copy-start(s32[4]{0:T(128)} %ids.1) | copy-start | bytes 52
  5.1 34.0 %copy-start.2 = (s32[64]{0:T(128)S(1)}, s32[64]{0:T(128)}, u32[]{:S(2)}) copy-start(s32[64]{0:T(128)} %ranks.1) | copy-start | bytes 772
  5.2 8.6 %collective-permute-start.1 = (bf16[896,128]{1,0:T(8,128)(2,1)S(1)}, bf16[896,128]{1,0:T(8,128)(2,1)S(1)}, u32[]{:S(2)}, u32[]{:S(2)}) collective-permute-start(bf16[896,128]{1,0:T(8,128)(2,1)S(1)} %fusion), channel_id=1, source_target_pairs={{0,2},{1,3},{2,0},{3,1},{4,6},{5,7},{6,4},{7,5},{8,10},{9,11},{10,... | collective-permute-start | bytes 688136 | tf_op jit(solution)/shard_map/ppermute | solution.py:295
  5.6 11.3 %collective-permute-start.8 = (bf16[32,2688]{1,0:T(8,128)(2,1)S(1)}, bf16[32,2688]{1,0:T(8,128)(2,1)S(1)}, u32[]{:S(2)}, u32[]{:S(2)}) collective-permute-start(bf16[32,2688]{1,0:T(8,128)(2,1)S(1)} %fusion.3), channel_id=1, source_target_pairs={{0,2},{1,3},{2,0},{3,1},{4,6},{5,7},{6,4},{7,5},{8,10},{9,11},{10,... | collective-permute-start | bytes 516104 | tf_op jit(solution)/shard_map/ppermute | solution.py:296
  13.8 28.9 %copy-start.3 = (bf16[1,128,2688]{2,1,0:T(8,128)(2,1)S(1)}, bf16[1,128,2688]{2,1,0:T(8,128)(2,1)}, u32[]{:S(2)}) copy-start(bf16[1,128,2688]{2,1,0:T(8,128)(2,1)} %param.10) | copy-start | bytes 2064388
  13.8 13.0 %collective-permute-start.4 = (bf16[896,128]{1,0:T(8,128)(2,1)S(1)}, bf16[896,128]{1,0:T(8,128)(2,1)S(1)}, u32[]{:S(2)}, u32[]{:S(2)}) collective-permute-start(bf16[896,128]{1,0:T(8,128)(2,1)S(1)} %fusion.2.rest_0_), channel_id=1, source_target_pairs={{0,8},{4,12},{8,0},{12,4},{1,9},{5,13},{9,1},{13,5},{2,10},{6,14},... | collective-permute-start | bytes 688136 | tf_op jit(solution)/shard_map/ppermute | solution.py:78
  16.5 15.5 %collective-permute-start.3 = (bf16[896,128]{1,0:T(8,128)(2,1)S(1)}, bf16[896,128]{1,0:T(8,128)(2,1)S(1)}, u32[]{:S(2)}, u32[]{:S(2)}) collective-permute-start(bf16[896,128]{1,0:T(8,128)(2,1)S(1)} %fusion.2.rest_0_), channel_id=1, source_target_pairs={{0,4},{4,0},{8,12},{12,8},{1,5},{5,1},{9,13},{13,9},{2,6},{6,2},{1... | collective-permute-start | bytes 688136 | tf_op jit(solution)/shard_map/ppermute | solution.py:78
  17.0 15.0 %collective-permute-start.10 = (bf16[32,2688]{1,0:T(8,128)(2,1)S(1)}, bf16[32,2688]{1,0:T(8,128)(2,1)S(1)}, u32[]{:S(2)}, u32[]{:S(2)}) collective-permute-start(bf16[32,2688]{1,0:T(8,128)(2,1)S(1)} %fusion.5.rest_3_), channel_id=1, source_target_pairs={{0,8},{4,12},{8,0},{12,4},{1,9},{5,13},{9,1},{13,5},{2,10},{6,14},... | collective-permute-start | bytes 516104 | tf_op jit(solution)/shard_map/ppermute | solution.py:78
  18.6 15.8 %collective-permute-start.9 = (bf16[32,2688]{1,0:T(8,128)(2,1)S(1)}, bf16[32,2688]{1,0:T(8,128)(2,1)S(1)}, u32[]{:S(2)}, u32[]{:S(2)}) collective-permute-start(bf16[32,2688]{1,0:T(8,128)(2,1)S(1)} %fusion.5.rest_3_), channel_id=1, source_target_pairs={{0,4},{4,0},{8,12},{12,8},{1,5},{5,1},{9,13},{13,9},{2,6},{6,2},{1... | collective-permute-start | bytes 516104 | tf_op jit(solution)/shard_map/ppermute | solution.py:78
  26.9 12.2 %collective-permute-start.6 = (bf16[896,128]{1,0:T(8,128)(2,1)S(1)}, bf16[896,128]{1,0:T(8,128)(2,1)S(1)}, u32[]{:S(2)}, u32[]{:S(2)}) collective-permute-start(bf16[896,128]{1,0:T(8,128)(2,1)S(1)} %collective-permute-done.4.rest_2_), channel_id=1, source_target_pairs={{0,4},{4,0},{8,12},{12,8},{1,5},{5,1},{9,13},{13,9},{2,6},{6,2},{1... | collective-permute-start | bytes 688136 | tf_op jit(solution)/shard_map/ppermute | solution.py:303
  32.0 10.7 %collective-permute-start.11 = (bf16[32,2688]{1,0:T(8,128)(2,1)S(1)}, bf16[32,2688]{1,0:T(8,128)(2,1)S(1)}, u32[]{:S(2)}, u32[]{:S(2)}) collective-permute-start(bf16[32,2688]{1,0:T(8,128)(2,1)S(1)} %collective-permute-done.10.rest_5_), channel_id=1, source_target_pairs={{0,4},{4,0},{8,12},{12,8},{1,5},{5,1},{9,13},{13,9},{2,6},{6,2},{1... | collective-permute-start | bytes 516104 | tf_op jit(solution)/shard_map/ppermute | solution.py:305
  34.5 10.4 %collective-permute-start.12 = (bf16[128,768]{1,0:T(8,128)(2,1)S(1)}, bf16[128,768]{1,0:T(8,128)(2,1)S(1)}, u32[]{:S(2)}, u32[]{:S(2)}) collective-permute-start(bf16[128,768]{1,0:T(8,128)(2,1)S(1)} %collective-permute-done.5.rest_2_), channel_id=1, source_target_pairs={{0,0},{4,4},{8,12},{12,8},{1,1},{5,5},{9,13},{13,9},{2,2},{6,6},{1... | collective-permute-start | bytes 589832 | tf_op jit(solution)/shard_map/ppermute | solution.py:307

commit v3 on v2

--- a/solution.py
+++ b/solution.py
@@ -289,20 +289,23 @@
         adapter_ids, adapter_slots, adapter_down, adapter_up
     )
     kv = kv_base[0]
-    kv_one, kv_two = spread(kv)
+    kv_two = lax.ppermute(kv, "ctx", TWO)
     near_down = lax.ppermute(give_down, "req", SIBLING)
     near_up = lax.ppermute(give_up, "req", SIBLING)
-    far_down = lax.ppermute(keep_down[1] + near_down[1], "req", ACROSS)
+    pass_down = keep_down[1] + near_down[1]
+    later = lax.optimization_barrier((kv, pass_down))[0]
+    kv_one = lax.ppermute(later, "ctx", ONE)
+    far_down = lax.ppermute(pass_down, "req", ACROSS)
     far_up = lax.ppermute(keep_up[1] + near_up[1], "req", ACROSS)
     down = keep_down[0] + near_down[0] + far_down
-    down, kv_one = lax.optimization_barrier((down, kv_one))
     down_one, down_two = spread(down)
     up = keep_up[0] + near_up[0] + far_up
+    up = lax.optimization_barrier((up, kv_one))[0]
     up_one, up_two = spread(up)
-    down_two = lax.optimization_barrier((down_two, kv_two))[0]
-    down_three = lax.ppermute(down_two, "ctx", ONE)
-    up_two = lax.optimization_barrier((up_two, down_one))[0]
-    up_three = lax.ppermute(up_two, "ctx", ONE)
+    ready = lax.optimization_barrier((down_two, kv_two))[0]
+    down_three = lax.ppermute(ready, "ctx", ONE)
+    ready = lax.optimization_barrier((up_two, down_one))[0]
+    up_three = lax.ppermute(ready, "ctx", ONE)
     kv_last = lax.optimization_barrier((kv_two, up_two, up_one))[0]
     kv_three = lax.ppermute(kv_last, "ctx", LAST)
     downs = [down, down_one, down_two, down_three]

time: 47.4 us -> 49.2 us (1.038)
  the two profiles are of different devices: /device:TPU:18 before, /device:TPU:25 now
where the time goes in v3:
time: 49.2 us; the launch traced here: 48.2 us
  waiting for transfers between devices  34.1 us (69%)
  starting transfers between devices  6.98 us (14%)
  Pallas kernels  5.54 us (11%)
  other arithmetic  0.89 us (2%)
  between operations  0.72 us (1%)
    ppermute x4, waiting for transfers between devices, spread(): return (lax.ppermute(shard, 'ctx', ONE), lax.ppermute(shard, 'ctx', TWO))  17.1 us
    ppermute x1, waiting for transfers between devices, body(): far_down = lax.ppermute(pass_down, 'req', ACROSS)  4.96 us
    ppermute x1, waiting for transfers between devices, body(): far_up = lax.ppermute(keep_up[1] + near_up[1], 'req', ACROSS)  2.77 us
    ppermute x1, waiting for transfers between devices, body(): up_three = lax.ppermute(ready, 'ctx', ONE)  2.73 us
    ppermute x1, starting transfers between devices, body(): kv_three = lax.ppermute(kv_last, 'ctx', LAST)  2.29 us
    ppermute x1, waiting for transfers between devices, body(): kv_three = lax.ppermute(kv_last, 'ctx', LAST)  2.24 us
    ppermute x1, waiting for transfers between devices, body(): down_three = lax.ppermute(ready, 'ctx', ONE)  1.97 us
    pallas_call x1, Pallas kernels, attend(): pl.pallas_call(attend_kernel, out_shape=shapes, in_specs=[spec(SMEM)] + [...  1.96 us
  transfers between devices with their start and end apart: 13, of which 10 were waited for; matrix products, arithmetic and copies ran while one was open for 0% of the time, Pallas kernels for 6%

profile of v3, /device:TPU:25, one launch (start us, length us, event | category | flops | bytes accessed | tf_op | source)
XLA Modules:
  0.0 48.2 jit_solution(16585366036592676452)
XLA Ops:
  0.0 0.7 %pad_add_fusion.table = s32[68]{0:T(128)S(1)} fusion(s32[64]{0:T(128)} %param.15, s32[4]{0:T(128)} %ids.1), kind=kLoop, calls=%fused_computation.10 | loop fusion | flops 68 | bytes 544 | tf_op jit(solution)/shard_map/concatenate | solution.py:67
  0.7 0.0 copy-start.4
  0.7 0.8 %shard_map.91 = (bf16[2,896,128]{2,1,0:T(8,128)(2,1)S(1)}, bf16[2,896,128]{2,1,0:T(8,128)(2,1)S(1)}, bf16[2,32,2688]{2,1,0:T(8,128)(2,1)S(1)}, bf16[2,32,2688]{2,1,0:T(8,128)(2,1)S(1)}) custom-call(s32[68]{0:T(128)S(1)} %pad_add_fusion.table, bf16[16,896,128]{2,1,0:T(8,128)(2,1)} %rest_0_.1, bf16[16,32,2688]{2,1,0:T(8,128)(2,1)} %rest_1_.1), custom_call_target="tpu_custom_call" | custom-call | tf_op jit(solution)/shard_map/pallas_call | solution.py:60
  1.6 1.8 %collective-permute-start = (bf16[2,896,128]{2,1,0:T(8,128)(2,1)S(1)}, bf16[2,896,128]{2,1,0:T(8,128)(2,1)S(1)}, u32[]{:S(2)}, u32[]{:S(2)}) collective-permute-start(bf16[2,896,128]{2,1,0:T(8,128)(2,1)S(1)} %get-tuple-element.20), channel_id=1, source_target_pairs={{0,1},{1,0},{2,3},{3,2},{4,5},{5,4},{6,7},{7,6},{8,9},{9,8},{10,11... | collective-permute-start | bytes 1376264 | tf_op jit(solution)/shard_map/ppermute | solution.py:293
  3.4 0.1 collective-permute-start.7
  3.4 0.0 copy-done.4
  3.4 0.1 collective-permute-start.4
  3.5 1.3 %collective-permute-done = bf16[2,896,128]{2,1,0:T(8,128)(2,1)S(1)} collective-permute-done((bf16[2,896,128]{2,1,0:T(8,128)(2,1)S(1)}, bf16[2,896,128]{2,1,0:T(8,128)(2,1)S(1)}, u32[]{:S(2)}, u32[]{:S(2)}) %collective-permute-start) | collective-permute-done | bytes 458784 | tf_op jit(solution)/shard_map/ppermute | solution.py:293
  4.8 0.0 copy-start
  4.8 0.0 copy-start.1
  4.8 0.0 copy-start.2
  4.8 1.3 %collective-permute-start.1 = (bf16[896,128]{1,0:T(8,128)(2,1)S(1)}, bf16[896,128]{1,0:T(8,128)(2,1)S(1)}, u32[]{:S(2)}, u32[]{:S(2)}) collective-permute-start(bf16[896,128]{1,0:T(8,128)(2,1)S(1)} %fusion), channel_id=1, source_target_pairs={{0,2},{1,3},{2,0},{3,1},{4,6},{5,7},{6,4},{7,5},{8,10},{9,11},{10,... | collective-permute-start | bytes 688136 | tf_op jit(solution)/shard_map/ppermute | solution.py:298
  6.1 0.0 collective-permute-done.7
  6.1 0.4 collective-permute-start.8
  6.6 0.2 collective-permute-start.6
  6.8 5.0 %collective-permute-done.1 = bf16[896,128]{1,0:T(8,128)(2,1)S(1)} collective-permute-done((bf16[896,128]{1,0:T(8,128)(2,1)S(1)}, bf16[896,128]{1,0:T(8,128)(2,1)S(1)}, u32[]{:S(2)}, u32[]{:S(2)}) %collective-permute-start.1) | collective-permute-done | bytes 229408 | tf_op jit(solution)/shard_map/ppermute | solution.py:298
  11.8 0.0 copy-start.3
  11.8 0.7 %collective-permute-start.3 = (bf16[896,128]{1,0:T(8,128)(2,1)S(1)}, bf16[896,128]{1,0:T(8,128)(2,1)S(1)}, u32[]{:S(2)}, u32[]{:S(2)}) collective-permute-start(bf16[896,128]{1,0:T(8,128)(2,1)S(1)} %fusion.2.rest_0_), channel_id=1, source_target_pairs={{0,8},{4,12},{8,0},{12,4},{1,9},{5,13},{9,1},{13,5},{2,10},{6,14},... | collective-permute-start | bytes 688136 | tf_op jit(solution)/shard_map/ppermute | solution.py:78
  12.5 0.2 collective-permute-start.2
  12.6 2.8 %collective-permute-done.8 = bf16[32,2688]{1,0:T(8,128)(2,1)S(1)} collective-permute-done((bf16[32,2688]{1,0:T(8,128)(2,1)S(1)}, bf16[32,2688]{1,0:T(8,128)(2,1)S(1)}, u32[]{:S(2)}, u32[]{:S(2)}) %collective-permute-start.8) | collective-permute-done | bytes 172064 | tf_op jit(solution)/shard_map/ppermute | solution.py:299
  15.5 1.0 %collective-permute-done.6.rest_1_ = bf16[128,768]{1,0:T(8,128)(2,1)S(1)} collective-permute-done((bf16[128,768]{1,0:T(8,128)(2,1)S(1)}, bf16[128,768]{1,0:T(8,128)(2,1)S(1)}, u32[]{:S(2)}, u32[]{:S(2)}) %collective-permute-start.6) | collective-permute-done | bytes 196640 | tf_op jit(solution)/shard_map/ppermute | solution.py:297
  16.5 0.0 collective-permute-start.10
  16.5 0.0 collective-permute-start.9
  16.5 0.0 collective-permute-done.4.rest_2_
  16.5 10.5 %collective-permute-done.3.rest_2_ = bf16[896,128]{1,0:T(8,128)(2,1)S(1)} collective-permute-done((bf16[896,128]{1,0:T(8,128)(2,1)S(1)}, bf16[896,128]{1,0:T(8,128)(2,1)S(1)}, u32[]{:S(2)}, u32[]{:S(2)}) %collective-permute-start.3) | collective-permute-done | bytes 229408 | tf_op jit(solution)/shard_map/ppermute | solution.py:78
  27.0 0.0 collective-permute-start.5
  27.0 5.5 %collective-permute-done.10.rest_5_ = bf16[32,2688]{1,0:T(8,128)(2,1)S(1)} collective-permute-done((bf16[32,2688]{1,0:T(8,128)(2,1)S(1)}, bf16[32,2688]{1,0:T(8,128)(2,1)S(1)}, u32[]{:S(2)}, u32[]{:S(2)}) %collective-permute-start.10) | collective-permute-done | bytes 172064 | tf_op jit(solution)/shard_map/ppermute | solution.py:78
  32.5 0.0 collective-permute-done.2.rest_1_
  32.5 0.0 collective-permute-start.11
  32.5 1.1 %collective-permute-done.9.rest_4_ = bf16[32,2688]{1,0:T(8,128)(2,1)S(1)} collective-permute-done((bf16[32,2688]{1,0:T(8,128)(2,1)S(1)}, bf16[32,2688]{1,0:T(8,128)(2,1)S(1)}, u32[]{:S(2)}, u32[]{:S(2)}) %collective-permute-start.9) | collective-permute-done | bytes 172064 | tf_op jit(solution)/shard_map/ppermute | solution.py:78
  33.6 2.3 %collective-permute-start.12 = (bf16[128,768]{1,0:T(8,128)(2,1)S(1)}, bf16[128,768]{1,0:T(8,128)(2,1)S(1)}, u32[]{:S(2)}, u32[]{:S(2)}) collective-permute-start(bf16[128,768]{1,0:T(8,128)(2,1)S(1)} %collective-permute-done.4.rest_2_), channel_id=1, source_target_pairs={{0,0},{4,4},{8,12},{12,8},{1,1},{5,5},{9,13},{13,9},{2,2},{6,6},{1... | collective-permute-start | bytes 589832 | tf_op jit(solution)/shard_map/ppermute | solution.py:310
  36.5 2.0 %collective-permute-done.5.rest_3_ = bf16[896,128]{1,0:T(8,128)(2,1)S(1)} collective-permute-done((bf16[896,128]{1,0:T(8,128)(2,1)S(1)}, bf16[896,128]{1,0:T(8,128)(2,1)S(1)}, u32[]{:S(2)}, u32[]{:S(2)}) %collective-permute-start.5) | collective-permute-done | bytes 229408 | tf_op jit(solution)/shard_map/ppermute | solution.py:306
  38.5 0.0 copy-done
  38.5 0.0 copy-done.1
  38.5 0.0 copy-done.2
  38.5 0.9 %shard_map.92.low = bf16[128,128]{1,0:T(8,128)(2,1)S(1)} custom-call(s32[4]{0:T(128)S(1)} %copy-done.1, s32[64]{0:T(128)S(1)} %copy-done.2, bf16[128,3584]{1,0:T(8,128)(2,1)S(1)} %bitcast.16, bf16[896,128]{1,0:T(8,128)(2,1)S(1)} %fusion.2.rest_0_, bf16[896,128]{1,0:T(8,128)(2,1)S(1)} %collective-permute-done.2.rest_1_, ...), custom_call_target="tpu_custom_call" | custom-call | flops 134217728 | bytes 4194304 | tf_op jit(solution)/shard_map/pallas_call | solution.py:97
  39.5 2.7 %collective-permute-done.11.rest_6_ = bf16[32,2688]{1,0:T(8,128)(2,1)S(1)} collective-permute-done((bf16[32,2688]{1,0:T(8,128)(2,1)S(1)}, bf16[32,2688]{1,0:T(8,128)(2,1)S(1)}, u32[]{:S(2)}, u32[]{:S(2)}) %collective-permute-start.11) | collective-permute-done | bytes 172064 | tf_op jit(solution)/shard_map/ppermute | solution.py:308
  42.2 0.0 copy-done.3
  42.2 2.0 %shard_map.93 = (bf16[128,2688]{1,0:T(8,128)(2,1)}, bf16[2688,128]{1,0:T(8,128)(2,1)S(1)}, f32[2688,128]{1,0:T(8,128)S(1)}, f32[2688,128]{1,0:T(8,128)S(1)}, f32[2688,128]{1,0:T(8,128)S(1)}) custom-call(s32[1]{0:T(128)S(6)} %copy.12.lengths, bf16[128,2688]{1,0:T(8,128)(2,1)S(1)} %bitcast.17, bf16[128,128]{1,0:T(8,128)(2,1)S(1)} %shard_map.92.low, ...), custom_call_target="tpu_custom_call" | custom-call | flops 1073741824 | bytes 4194304 | tf_op jit(solution)/shard_map/pallas_call | solution.py:207
  44.2 2.2 %collective-permute-done.12.kv = bf16[128,768]{1,0:T(8,128)(2,1)S(1)} collective-permute-done((bf16[128,768]{1,0:T(8,128)(2,1)S(1)}, bf16[128,768]{1,0:T(8,128)(2,1)S(1)}, u32[]{:S(2)}, u32[]{:S(2)}) %collective-permute-start.12) | collective-permute-done | bytes 196640 | tf_op jit(solution)/shard_map/ppermute | solution.py:310
  46.4 1.8 %shard_map.94 = bf16[128,2688]{1,0:T(8,128)(2,1)} custom-call(s32[1]{0:T(128)S(6)} %copy.12.lengths, bf16[128,2688]{1,0:T(8,128)(2,1)} %get-tuple-element.27.so_far, bf16[2688,128]{1,0:T(8,128)(2,1)S(1)} %get-tuple-element.28.queries, f32[2688,128]{1,0:T(8,128)S(1)} %get-tuple-element.29.sums, ...), custom_call_target="tpu_custom_call", output_to_operand_aliasing={{}: (1, {})} | custom-call | flops 268435456 | bytes 2097152 | tf_op jit(solution)/shard_map/pallas_call | solution.py:260
  (4 shorter events, 0.1 us)
Async XLA Ops:
  0.7 2.7 %copy-start.4 = (bf16[1,128,768]{2,1,0:T(8,128)(2,1)S(1)}, bf16[1,128,768]{2,1,0:T(8,128)(2,1)}, u32[]{:S(2)}) copy-start(bf16[1,128,768]{2,1,0:T(8,128)(2,1)} %param.11) | copy-start | bytes 589828
  1.6 3.2 %collective-permute-start = (bf16[2,896,128]{2,1,0:T(8,128)(2,1)S(1)}, bf16[2,896,128]{2,1,0:T(8,128)(2,1)S(1)}, u32[]{:S(2)}, u32[]{:S(2)}) collective-permute-start(bf16[2,896,128]{2,1,0:T(8,128)(2,1)S(1)} %get-tuple-element.20), channel_id=1, source_target_pairs={{0,1},{1,0},{2,3},{3,2},{4,5},{5,4},{6,7},{7,6},{8,9},{9,8},{10,11... | collective-permute-start | bytes 1376264 | tf_op jit(solution)/shard_map/ppermute | solution.py:293
  3.4 2.8 %collective-permute-start.7 = (bf16[2,32,2688]{2,1,0:T(8,128)(2,1)S(1)}, bf16[2,32,2688]{2,1,0:T(8,128)(2,1)S(1)}, u32[]{:S(2)}, u32[]{:S(2)}) collective-permute-start(bf16[2,32,2688]{2,1,0:T(8,128)(2,1)S(1)} %get-tuple-element.24), channel_id=1, source_target_pairs={{0,1},{1,0},{2,3},{3,2},{4,5},{5,4},{6,7},{7,6},{8,9},{9,8},{10,11... | collective-permute-start | bytes 1032200 | tf_op jit(solution)/shard_map/ppermute | solution.py:294
  3.4 13.1 %collective-permute-start.4 = (bf16[128,768]{1,0:T(8,128)(2,1)S(1)}, bf16[128,768]{1,0:T(8,128)(2,1)S(1)}, u32[]{:S(2)}, u32[]{:S(2)}) collective-permute-start(bf16[128,768]{1,0:T(8,128)(2,1)S(1)} %bitcast.18), channel_id=1, source_target_pairs={{0,8},{4,12},{8,0},{12,4},{1,9},{5,13},{9,1},{13,5},{2,10},{6,14},... | collective-permute-start | bytes 589832 | tf_op jit(solution)/shard_map/ppermute | solution.py:292
  4.8 33.7 %copy-start = (bf16[1,128,3584]{2,1,0:T(8,128)(2,1)S(1)}, bf16[1,128,3584]{2,1,0:T(8,128)(2,1)}, u32[]{:S(2)}) copy-start(bf16[1,128,3584]{2,1,0:T(8,128)(2,1)} %param.9) | copy-start | bytes 2752516
  4.8 33.7 %copy-start.1 = (s32[4]{0:T(128)S(1)}, s32[4]{0:T(128)}, u32[]{:S(2)}) copy-start(s32[4]{0:T(128)} %ids.1) | copy-start | bytes 52
  4.8 33.7 %copy-start.2 = (s32[64]{0:T(128)S(1)}, s32[64]{0:T(128)}, u32[]{:S(2)}) copy-start(s32[64]{0:T(128)} %ranks.1) | copy-start | bytes 772
  4.8 6.9 %collective-permute-start.1 = (bf16[896,128]{1,0:T(8,128)(2,1)S(1)}, bf16[896,128]{1,0:T(8,128)(2,1)S(1)}, u32[]{:S(2)}, u32[]{:S(2)}) collective-permute-start(bf16[896,128]{1,0:T(8,128)(2,1)S(1)} %fusion), channel_id=1, source_target_pairs={{0,2},{1,3},{2,0},{3,1},{4,6},{5,7},{6,4},{7,5},{8,10},{9,11},{10,... | collective-permute-start | bytes 688136 | tf_op jit(solution)/shard_map/ppermute | solution.py:298
  6.1 9.3 %collective-permute-start.8 = (bf16[32,2688]{1,0:T(8,128)(2,1)S(1)}, bf16[32,2688]{1,0:T(8,128)(2,1)S(1)}, u32[]{:S(2)}, u32[]{:S(2)}) collective-permute-start(bf16[32,2688]{1,0:T(8,128)(2,1)S(1)} %fusion.3), channel_id=1, source_target_pairs={{0,2},{1,3},{2,0},{3,1},{4,6},{5,7},{6,4},{7,5},{8,10},{9,11},{10,... | collective-permute-start | bytes 516104 | tf_op jit(solution)/shard_map/ppermute | solution.py:299
  6.6 9.9 %collective-permute-start.6 = (bf16[128,768]{1,0:T(8,128)(2,1)S(1)}, bf16[128,768]{1,0:T(8,128)(2,1)S(1)}, u32[]{:S(2)}, u32[]{:S(2)}) collective-permute-start(bf16[128,768]{1,0:T(8,128)(2,1)S(1)} %bitcast.19), channel_id=1, source_target_pairs={{0,4},{4,0},{8,12},{12,8},{1,5},{5,1},{9,13},{13,9},{2,6},{6,2},{1... | collective-permute-start | bytes 589832 | tf_op jit(solution)/shard_map/ppermute | solution.py:297
  11.8 30.4 %copy-start.3 = (bf16[1,128,2688]{2,1,0:T(8,128)(2,1)S(1)}, bf16[1,128,2688]{2,1,0:T(8,128)(2,1)}, u32[]{:S(2)}) copy-start(bf16[1,128,2688]{2,1,0:T(8,128)(2,1)} %param.10) | copy-start | bytes 2064388
  11.8 15.2 %collective-permute-start.3 = (bf16[896,128]{1,0:T(8,128)(2,1)S(1)}, bf16[896,128]{1,0:T(8,128)(2,1)S(1)}, u32[]{:S(2)}, u32[]{:S(2)}) collective-permute-start(bf16[896,128]{1,0:T(8,128)(2,1)S(1)} %fusion.2.rest_0_), channel_id=1, source_target_pairs={{0,8},{4,12},{8,0},{12,4},{1,9},{5,13},{9,1},{13,5},{2,10},{6,14},... | collective-permute-start | bytes 688136 | tf_op jit(solution)/shard_map/ppermute | solution.py:78
  12.5 20.0 %collective-permute-start.2 = (bf16[896,128]{1,0:T(8,128)(2,1)S(1)}, bf16[896,128]{1,0:T(8,128)(2,1)S(1)}, u32[]{:S(2)}, u32[]{:S(2)}) collective-permute-start(bf16[896,128]{1,0:T(8,128)(2,1)S(1)} %fusion.2.rest_0_), channel_id=1, source_target_pairs={{0,4},{4,0},{8,12},{12,8},{1,5},{5,1},{9,13},{13,9},{2,6},{6,2},{1... | collective-permute-start | bytes 688136 | tf_op jit(solution)/shard_map/ppermute | solution.py:78
  16.5 16.0 %collective-permute-start.10 = (bf16[32,2688]{1,0:T(8,128)(2,1)S(1)}, bf16[32,2688]{1,0:T(8,128)(2,1)S(1)}, u32[]{:S(2)}, u32[]{:S(2)}) collective-permute-start(bf16[32,2688]{1,0:T(8,128)(2,1)S(1)} %fusion.5.rest_3_), channel_id=1, source_target_pairs={{0,8},{4,12},{8,0},{12,4},{1,9},{5,13},{9,1},{13,5},{2,10},{6,14},... | collective-permute-start | bytes 516104 | tf_op jit(solution)/shard_map/ppermute | solution.py:78
  16.5 17.1 %collective-permute-start.9 = (bf16[32,2688]{1,0:T(8,128)(2,1)S(1)}, bf16[32,2688]{1,0:T(8,128)(2,1)S(1)}, u32[]{:S(2)}, u32[]{:S(2)}) collective-permute-start(bf16[32,2688]{1,0:T(8,128)(2,1)S(1)} %fusion.5.rest_3_), channel_id=1, source_target_pairs={{0,4},{4,0},{8,12},{12,8},{1,5},{5,1},{9,13},{13,9},{2,6},{6,2},{1... | collective-permute-start | bytes 516104 | tf_op jit(solution)/shard_map/ppermute | solution.py:78
  27.0 11.5 %collective-permute-start.5 = (bf16[896,128]{1,0:T(8,128)(2,1)S(1)}, bf16[896,128]{1,0:T(8,128)(2,1)S(1)}, u32[]{:S(2)}, u32[]{:S(2)}) collective-permute-start(bf16[896,128]{1,0:T(8,128)(2,1)S(1)} %collective-permute-done.3.rest_2_), channel_id=1, source_target_pairs={{0,4},{4,0},{8,12},{12,8},{1,5},{5,1},{9,13},{13,9},{2,6},{6,2},{1... | collective-permute-start | bytes 688136 | tf_op jit(solution)/shard_map/ppermute | solution.py:306
  32.5 9.7 %collective-permute-start.11 = (bf16[32,2688]{1,0:T(8,128)(2,1)S(1)}, bf16[32,2688]{1,0:T(8,128)(2,1)S(1)}, u32[]{:S(2)}, u32[]{:S(2)}) collective-permute-start(bf16[32,2688]{1,0:T(8,128)(2,1)S(1)} %collective-permute-done.10.rest_5_), channel_id=1, source_target_pairs={{0,4},{4,0},{8,12},{12,8},{1,5},{5,1},{9,13},{13,9},{2,6},{6,2},{1... | collective-permute-start | bytes 516104 | tf_op jit(solution)/shard_map/ppermute | solution.py:308
  33.6 12.8 %collective-permute-start.12 = (bf16[128,768]{1,0:T(8,128)(2,1)S(1)}, bf16[128,768]{1,0:T(8,128)(2,1)S(1)}, u32[]{:S(2)}, u32[]{:S(2)}) collective-permute-start(bf16[128,768]{1,0:T(8,128)(2,1)S(1)} %collective-permute-done.4.rest_2_), channel_id=1, source_target_pairs={{0,0},{4,4},{8,12},{12,8},{1,1},{5,5},{9,13},{13,9},{2,2},{6,6},{1... | collective-permute-start | bytes 589832 | tf_op jit(solution)/shard_map/ppermute | solution.py:310

commit v4 on v2

--- a/solution.py
+++ b/solution.py
@@ -148,23 +148,30 @@
     def _():
         for flip, piece in enumerate(ups):
             upper[pl.ds(pl.multiple_of((z ^ flip) * rows, rows), rows), :] = piece[...]
-        for j in range(HEADS):
-            columns = slice(j * HD, (j + 1) * HD)
-            delta = jnp.dot(low[...], upper[:, columns], preferred_element_type=jnp.float32)
-            queries[j * tokens : (j + 1) * tokens, :] = (
-                base[:, columns].astype(jnp.float32) + delta
-            ).astype(jnp.bfloat16)
 
     query_pos = lax.broadcasted_iota(jnp.int32, (tokens, tokens), 0)
     key_pos = lax.broadcasted_iota(jnp.int32, (tokens, tokens), 1)
     causal = key_pos <= query_pos
+
+    def scores_of(h, blocks):
+        columns = slice(h * GROUP * HD, (h + 1) * GROUP * HD)
+        delta = jnp.dot(low[...], upper[:, columns], preferred_element_type=jnp.float32)
+        query = (base[:, columns].astype(jnp.float32) + delta).astype(jnp.bfloat16)
+        query = [query[:, g * HD : (g + 1) * HD] for g in range(GROUP)]
+        query = jnp.concatenate(query, axis=0)
+        keys, values = head_columns(blocks, h)
+        return query, dot_keys(query, keys), values
+
     for mine, needed in enumerate(((0,), (0, 1), (0, 2), (0, 1, 2))):
 
         @pl.when(live & (z == mine))
         def _():
+            blocks = [kvs[i] for i in needed]
+            ahead = scores_of(0, blocks)
             for h in range(KVH):
-                keys, values = head_columns([kvs[i] for i in needed], h)
-                scores = dot_keys(queries[h * block : (h + 1) * block, :], keys)
+                query, scores, values = ahead
+                if h + 1 < KVH:
+                    ahead = scores_of(h + 1, blocks)
                 weights, tops, totals = [], [], []
                 for g in range(GROUP):
                     score = scores[g * tokens : (g + 1) * tokens, :]
@@ -185,6 +192,7 @@
                         ).astype(jnp.bfloat16)
                     copies[h].start()
                 else:
+                    queries[h * block : (h + 1) * block, :] = query
                     sums[h * block : (h + 1) * block, :] = product
                     for g in range(GROUP):
                         at = slice(h * block + g * tokens, h * block + (g + 1) * tokens)
@@ -230,9 +238,12 @@
 
     @pl.when((z * tokens < lengths[0]) & (z >= 2))
     def _():
+        heads = [head_columns([kv], h) for h in range(KVH)]
+        all_scores = [
+            dot_keys(queries[h * block : (h + 1) * block, :], heads[h][0]) for h in range(KVH)
+        ]
         for h in range(KVH):
-            keys, values = head_columns([kv], h)
-            scores = dot_keys(queries[h * block : (h + 1) * block, :], keys)
+            scores, values = all_scores[h], heads[h][1]
             weights, factors, totals = [], [], []
             for g in range(GROUP):
                 at = slice(h * block + g * tokens, h * block + (g + 1) * tokens)

time: 47.4 us -> 47.7 us (level)
  transfers between devices with their start and end apart: 13 -> 13, of which waited for: 7 -> 7; matrix products, arithmetic and copies ran while one was open for 0% -> 0% of each run, Pallas kernels for 5% -> 6%
where the time goes in v4:
time: 47.7 us; the launch traced here: 46.8 us
  waiting for transfers between devices  21.3 us (45%)
  starting transfers between devices  17.4 us (36%)
  Pallas kernels  6.56 us (14%)
  other arithmetic  0.89 us (2%)
  between operations  0.73 us (2%)
    ppermute x6, waiting for transfers between devices, spread(): return (lax.ppermute(shard, 'ctx', ONE), lax.ppermute(shard, 'ctx', TWO))  10.7 us
    ppermute x6, starting transfers between devices, spread(): return (lax.ppermute(shard, 'ctx', ONE), lax.ppermute(shard, 'ctx', TWO))  7.12 us
    ppermute x1, waiting for transfers between devices, body(): far_down = lax.ppermute(keep_down[1] + near_down[1], 'req', ACROSS)  6.41 us
    ppermute x1, starting transfers between devices, body(): kv_three = lax.ppermute(kv_last, 'ctx', LAST)  2.87 us
    ppermute x1, waiting for transfers between devices, body(): up_three = lax.ppermute(up_two, 'ctx', ONE)  2.7 us
    ppermute x1, starting transfers between devices, body(): down_three = lax.ppermute(down_two, 'ctx', ONE)  2.36 us
    ppermute x1, starting transfers between devices, body(): up_three = lax.ppermute(up_two, 'ctx', ONE)  2.3 us
    pallas_call x1, Pallas kernels, finish(): pl.pallas_call(finish_kernel, out_shape=jax.ShapeDtypeStruct(so_far.shape...  2.02 us
  transfers between devices with their start and end apart: 13, of which 7 were waited for; matrix products, arithmetic and copies ran while one was open for 0% of the time, Pallas kernels for 6%

profile of v4, /device:TPU:18, one launch (start us, length us, event | category | flops | bytes accessed | tf_op | source)
XLA Modules:
  0.0 46.8 jit_solution(6387060489261474525)
XLA Ops:
  0.0 0.7 %pad_add_fusion.table = s32[68]{0:T(128)S(1)} fusion(s32[64]{0:T(128)} %param.15, s32[4]{0:T(128)} %ids.1), kind=kLoop, calls=%fused_computation.10 | loop fusion | flops 68 | bytes 544 | tf_op jit(solution)/shard_map/concatenate | solution.py:67
  0.7 0.0 copy-start.4
  0.7 1.9 %shard_map.91 = (bf16[2,896,128]{2,1,0:T(8,128)(2,1)S(1)}, bf16[2,896,128]{2,1,0:T(8,128)(2,1)S(1)}, bf16[2,32,2688]{2,1,0:T(8,128)(2,1)S(1)}, bf16[2,32,2688]{2,1,0:T(8,128)(2,1)S(1)}) custom-call(s32[68]{0:T(128)S(1)} %pad_add_fusion.table, bf16[16,896,128]{2,1,0:T(8,128)(2,1)} %rest_0_.1, bf16[16,32,2688]{2,1,0:T(8,128)(2,1)} %rest_1_.1), custom_call_target="tpu_custom_call" | custom-call | tf_op jit(solution)/shard_map/pallas_call | solution.py:60
  2.6 0.1 collective-permute-start
  2.7 0.5 %collective-permute-start.7 = (bf16[2,32,2688]{2,1,0:T(8,128)(2,1)S(1)}, bf16[2,32,2688]{2,1,0:T(8,128)(2,1)S(1)}, u32[]{:S(2)}, u32[]{:S(2)}) collective-permute-start(bf16[2,32,2688]{2,1,0:T(8,128)(2,1)S(1)} %get-tuple-element.25), channel_id=1, source_target_pairs={{0,1},{1,0},{2,3},{3,2},{4,5},{5,4},{6,7},{7,6},{8,9},{9,8},{10,11... | collective-permute-start | bytes 1032200 | tf_op jit(solution)/shard_map/ppermute | solution.py:305
  3.2 0.0 copy-done.4
  3.2 1.6 %collective-permute-start.2 = (bf16[128,768]{1,0:T(8,128)(2,1)S(1)}, bf16[128,768]{1,0:T(8,128)(2,1)S(1)}, u32[]{:S(2)}, u32[]{:S(2)}) collective-permute-start(bf16[128,768]{1,0:T(8,128)(2,1)S(1)} %bitcast.18), channel_id=1, source_target_pairs={{0,4},{4,0},{8,12},{12,8},{1,5},{5,1},{9,13},{13,9},{2,6},{6,2},{1... | collective-permute-start | bytes 589832 | tf_op jit(solution)/shard_map/ppermute | solution.py:78
  4.8 0.3 collective-permute-start.5
  5.1 0.0 collective-permute-done
  5.1 0.0 copy-start
  5.1 0.0 copy-start.1
  5.1 0.0 copy-start.2
  5.2 0.4 collective-permute-start.1
  5.6 0.0 collective-permute-done.7
  5.6 1.8 %collective-permute-start.8 = (bf16[32,2688]{1,0:T(8,128)(2,1)S(1)}, bf16[32,2688]{1,0:T(8,128)(2,1)S(1)}, u32[]{:S(2)}, u32[]{:S(2)}) collective-permute-start(bf16[32,2688]{1,0:T(8,128)(2,1)S(1)} %fusion.3), channel_id=1, source_target_pairs={{0,2},{1,3},{2,0},{3,1},{4,6},{5,7},{6,4},{7,5},{8,10},{9,11},{10,... | collective-permute-start | bytes 516104 | tf_op jit(solution)/shard_map/ppermute | solution.py:307
  7.3 6.4 %collective-permute-done.1 = bf16[896,128]{1,0:T(8,128)(2,1)S(1)} collective-permute-done((bf16[896,128]{1,0:T(8,128)(2,1)S(1)}, bf16[896,128]{1,0:T(8,128)(2,1)S(1)}, u32[]{:S(2)}, u32[]{:S(2)}) %collective-permute-start.1) | collective-permute-done | bytes 229408 | tf_op jit(solution)/shard_map/ppermute | solution.py:306
  13.8 0.0 copy-start.3
  13.8 0.0 collective-permute-done.2.rest_1_
  13.8 2.7 %collective-permute-start.4 = (bf16[896,128]{1,0:T(8,128)(2,1)S(1)}, bf16[896,128]{1,0:T(8,128)(2,1)S(1)}, u32[]{:S(2)}, u32[]{:S(2)}) collective-permute-start(bf16[896,128]{1,0:T(8,128)(2,1)S(1)} %fusion.2.rest_0_), channel_id=1, source_target_pairs={{0,8},{4,12},{8,0},{12,4},{1,9},{5,13},{9,1},{13,5},{2,10},{6,14},... | collective-permute-start | bytes 688136 | tf_op jit(solution)/shard_map/ppermute | solution.py:78
  16.5 0.4 collective-permute-start.3
  16.9 0.0 collective-permute-done.8
  17.0 1.7 %collective-permute-start.10 = (bf16[32,2688]{1,0:T(8,128)(2,1)S(1)}, bf16[32,2688]{1,0:T(8,128)(2,1)S(1)}, u32[]{:S(2)}, u32[]{:S(2)}) collective-permute-start(bf16[32,2688]{1,0:T(8,128)(2,1)S(1)} %fusion.5.rest_3_), channel_id=1, source_target_pairs={{0,8},{4,12},{8,0},{12,4},{1,9},{5,13},{9,1},{13,5},{2,10},{6,14},... | collective-permute-start | bytes 516104 | tf_op jit(solution)/shard_map/ppermute | solution.py:78
  18.6 0.4 collective-permute-start.9
  19.1 0.0 collective-permute-done.5.rest_2_
  19.1 7.8 %collective-permute-done.4.rest_2_ = bf16[896,128]{1,0:T(8,128)(2,1)S(1)} collective-permute-done((bf16[896,128]{1,0:T(8,128)(2,1)S(1)}, bf16[896,128]{1,0:T(8,128)(2,1)S(1)}, u32[]{:S(2)}, u32[]{:S(2)}) %collective-permute-start.4) | collective-permute-done | bytes 229408 | tf_op jit(solution)/shard_map/ppermute | solution.py:78
  26.9 2.4 %collective-permute-start.6 = (bf16[896,128]{1,0:T(8,128)(2,1)S(1)}, bf16[896,128]{1,0:T(8,128)(2,1)S(1)}, u32[]{:S(2)}, u32[]{:S(2)}) collective-permute-start(bf16[896,128]{1,0:T(8,128)(2,1)S(1)} %collective-permute-done.4.rest_2_), channel_id=1, source_target_pairs={{0,4},{4,0},{8,12},{12,8},{1,5},{5,1},{9,13},{13,9},{2,6},{6,2},{1... | collective-permute-start | bytes 688136 | tf_op jit(solution)/shard_map/ppermute | solution.py:314
  29.2 2.8 %collective-permute-done.10.rest_5_ = bf16[32,2688]{1,0:T(8,128)(2,1)S(1)} collective-permute-done((bf16[32,2688]{1,0:T(8,128)(2,1)S(1)}, bf16[32,2688]{1,0:T(8,128)(2,1)S(1)}, u32[]{:S(2)}, u32[]{:S(2)}) %collective-permute-start.10) | collective-permute-done | bytes 172064 | tf_op jit(solution)/shard_map/ppermute | solution.py:78
  32.0 0.0 collective-permute-done.3.rest_1_
  32.0 2.3 %collective-permute-start.11 = (bf16[32,2688]{1,0:T(8,128)(2,1)S(1)}, bf16[32,2688]{1,0:T(8,128)(2,1)S(1)}, u32[]{:S(2)}, u32[]{:S(2)}) collective-permute-start(bf16[32,2688]{1,0:T(8,128)(2,1)S(1)} %collective-permute-done.10.rest_5_), channel_id=1, source_target_pairs={{0,4},{4,0},{8,12},{12,8},{1,5},{5,1},{9,13},{13,9},{2,6},{6,2},{1... | collective-permute-start | bytes 516104 | tf_op jit(solution)/shard_map/ppermute | solution.py:316
  34.3 0.2 collective-permute-done.9.rest_4_
  34.5 2.9 %collective-permute-start.12 = (bf16[128,768]{1,0:T(8,128)(2,1)S(1)}, bf16[128,768]{1,0:T(8,128)(2,1)S(1)}, u32[]{:S(2)}, u32[]{:S(2)}) collective-permute-start(bf16[128,768]{1,0:T(8,128)(2,1)S(1)} %collective-permute-done.5.rest_2_), channel_id=1, source_target_pairs={{0,0},{4,4},{8,12},{12,8},{1,1},{5,5},{9,13},{13,9},{2,2},{6,6},{1... | collective-permute-start | bytes 589832 | tf_op jit(solution)/shard_map/ppermute | solution.py:318
  38.0 1.1 %collective-permute-done.6.rest_3_ = bf16[896,128]{1,0:T(8,128)(2,1)S(1)} collective-permute-done((bf16[896,128]{1,0:T(8,128)(2,1)S(1)}, bf16[896,128]{1,0:T(8,128)(2,1)S(1)}, u32[]{:S(2)}, u32[]{:S(2)}) %collective-permute-start.6) | collective-permute-done | bytes 229408 | tf_op jit(solution)/shard_map/ppermute | solution.py:314
  39.1 0.0 copy-done
  39.1 0.0 copy-done.1
  39.1 0.0 copy-done.2
  39.1 0.9 %shard_map.92.low = bf16[128,128]{1,0:T(8,128)(2,1)S(1)} custom-call(s32[4]{0:T(128)S(1)} %copy-done.1, s32[64]{0:T(128)S(1)} %copy-done.2, bf16[128,3584]{1,0:T(8,128)(2,1)S(1)} %bitcast.16, bf16[896,128]{1,0:T(8,128)(2,1)S(1)} %fusion.2.rest_0_, bf16[896,128]{1,0:T(8,128)(2,1)S(1)} %collective-permute-done.3.rest_1_, ...), custom_call_target="tpu_custom_call" | custom-call | flops 134217728 | bytes 4194304 | tf_op jit(solution)/shard_map/pallas_call | solution.py:97
  40.0 2.7 %collective-permute-done.11.rest_6_ = bf16[32,2688]{1,0:T(8,128)(2,1)S(1)} collective-permute-done((bf16[32,2688]{1,0:T(8,128)(2,1)S(1)}, bf16[32,2688]{1,0:T(8,128)(2,1)S(1)}, u32[]{:S(2)}, u32[]{:S(2)}) %collective-permute-start.11) | collective-permute-done | bytes 172064 | tf_op jit(solution)/shard_map/ppermute | solution.py:316
  42.7 0.0 copy-done.3
  42.7 1.7 %shard_map.93 = (bf16[128,2688]{1,0:T(8,128)(2,1)}, bf16[2688,128]{1,0:T(8,128)(2,1)S(1)}, f32[2688,128]{1,0:T(8,128)S(1)}, f32[2688,128]{1,0:T(8,128)S(1)}, f32[2688,128]{1,0:T(8,128)S(1)}) custom-call(s32[1]{0:T(128)S(6)} %copy.12.lengths, bf16[128,2688]{1,0:T(8,128)(2,1)S(1)} %bitcast.17, bf16[128,128]{1,0:T(8,128)(2,1)S(1)} %shard_map.92.low, ...), custom_call_target="tpu_custom_call" | custom-call | flops 1073741824 | bytes 4194304 | tf_op jit(solution)/shard_map/pallas_call | solution.py:215
  44.5 0.3 collective-permute-done.12.kv
  44.8 2.0 %shard_map.94 = bf16[128,2688]{1,0:T(8,128)(2,1)} custom-call(s32[1]{0:T(128)S(6)} %copy.12.lengths, bf16[128,2688]{1,0:T(8,128)(2,1)} %get-tuple-element.27.so_far, bf16[2688,128]{1,0:T(8,128)(2,1)S(1)} %get-tuple-element.28.queries, f32[2688,128]{1,0:T(8,128)S(1)} %get-tuple-element.29.sums, ...), custom_call_target="tpu_custom_call", output_to_operand_aliasing={{}: (1, {})} | custom-call | flops 268435456 | bytes 2097152 | tf_op jit(solution)/shard_map/pallas_call | solution.py:271
  (4 shorter events, 0.1 us)
Async XLA Ops:
  0.7 2.4 %copy-start.4 = (bf16[1,128,768]{2,1,0:T(8,128)(2,1)S(1)}, bf16[1,128,768]{2,1,0:T(8,128)(2,1)}, u32[]{:S(2)}) copy-start(bf16[1,128,768]{2,1,0:T(8,128)(2,1)} %param.11) | copy-start | bytes 589828
  2.6 2.5 %collective-permute-start = (bf16[2,896,128]{2,1,0:T(8,128)(2,1)S(1)}, bf16[2,896,128]{2,1,0:T(8,128)(2,1)S(1)}, u32[]{:S(2)}, u32[]{:S(2)}) collective-permute-start(bf16[2,896,128]{2,1,0:T(8,128)(2,1)S(1)} %get-tuple-element.20), channel_id=1, source_target_pairs={{0,1},{1,0},{2,3},{3,2},{4,5},{5,4},{6,7},{7,6},{8,9},{9,8},{10,11... | collective-permute-start | bytes 1376264 | tf_op jit(solution)/shard_map/ppermute | solution.py:304
  2.7 2.9 %collective-permute-start.7 = (bf16[2,32,2688]{2,1,0:T(8,128)(2,1)S(1)}, bf16[2,32,2688]{2,1,0:T(8,128)(2,1)S(1)}, u32[]{:S(2)}, u32[]{:S(2)}) collective-permute-start(bf16[2,32,2688]{2,1,0:T(8,128)(2,1)S(1)} %get-tuple-element.25), channel_id=1, source_target_pairs={{0,1},{1,0},{2,3},{3,2},{4,5},{5,4},{6,7},{7,6},{8,9},{9,8},{10,11... | collective-permute-start | bytes 1032200 | tf_op jit(solution)/shard_map/ppermute | solution.py:305
  3.2 10.6 %collective-permute-start.2 = (bf16[128,768]{1,0:T(8,128)(2,1)S(1)}, bf16[128,768]{1,0:T(8,128)(2,1)S(1)}, u32[]{:S(2)}, u32[]{:S(2)}) collective-permute-start(bf16[128,768]{1,0:T(8,128)(2,1)S(1)} %bitcast.18), channel_id=1, source_target_pairs={{0,4},{4,0},{8,12},{12,8},{1,5},{5,1},{9,13},{13,9},{2,6},{6,2},{1... | collective-permute-start | bytes 589832 | tf_op jit(solution)/shard_map/ppermute | solution.py:78
  4.8 14.3 %collective-permute-start.5 = (bf16[128,768]{1,0:T(8,128)(2,1)S(1)}, bf16[128,768]{1,0:T(8,128)(2,1)S(1)}, u32[]{:S(2)}, u32[]{:S(2)}) collective-permute-start(bf16[128,768]{1,0:T(8,128)(2,1)S(1)} %bitcast.19), channel_id=1, source_target_pairs={{0,8},{4,12},{8,0},{12,4},{1,9},{5,13},{9,1},{13,5},{2,10},{6,14},... | collective-permute-start | bytes 589832 | tf_op jit(solution)/shard_map/ppermute | solution.py:78
  5.1 34.0 %copy-start = (bf16[1,128,3584]{2,1,0:T(8,128)(2,1)S(1)}, bf16[1,128,3584]{2,1,0:T(8,128)(2,1)}, u32[]{:S(2)}) copy-start(bf16[1,128,3584]{2,1,0:T(8,128)(2,1)} %param.9) | copy-start | bytes 2752516
  5.1 34.0 %copy-start.1 = (s32[4]{0:T(128)S(1)}, s32[4]{0:T(128)}, u32[]{:S(2)}) copy-start(s32[4]{0:T(128)} %ids.1) | copy-start | bytes 52
  5.1 34.0 %copy-start.2 = (s32[64]{0:T(128)S(1)}, s32[64]{0:T(128)}, u32[]{:S(2)}) copy-start(s32[64]{0:T(128)} %ranks.1) | copy-start | bytes 772
  5.2 8.6 %collective-permute-start.1 = (bf16[896,128]{1,0:T(8,128)(2,1)S(1)}, bf16[896,128]{1,0:T(8,128)(2,1)S(1)}, u32[]{:S(2)}, u32[]{:S(2)}) collective-permute-start(bf16[896,128]{1,0:T(8,128)(2,1)S(1)} %fusion), channel_id=1, source_target_pairs={{0,2},{1,3},{2,0},{3,1},{4,6},{5,7},{6,4},{7,5},{8,10},{9,11},{10,... | collective-permute-start | bytes 688136 | tf_op jit(solution)/shard_map/ppermute | solution.py:306
  5.6 11.3 %collective-permute-start.8 = (bf16[32,2688]{1,0:T(8,128)(2,1)S(1)}, bf16[32,2688]{1,0:T(8,128)(2,1)S(1)}, u32[]{:S(2)}, u32[]{:S(2)}) collective-permute-start(bf16[32,2688]{1,0:T(8,128)(2,1)S(1)} %fusion.3), channel_id=1, source_target_pairs={{0,2},{1,3},{2,0},{3,1},{4,6},{5,7},{6,4},{7,5},{8,10},{9,11},{10,... | collective-permute-start | bytes 516104 | tf_op jit(solution)/shard_map/ppermute | solution.py:307
  13.8 28.9 %copy-start.3 = (bf16[1,128,2688]{2,1,0:T(8,128)(2,1)S(1)}, bf16[1,128,2688]{2,1,0:T(8,128)(2,1)}, u32[]{:S(2)}) copy-start(bf16[1,128,2688]{2,1,0:T(8,128)(2,1)} %param.10) | copy-start | bytes 2064388
  13.8 13.0 %collective-permute-start.4 = (bf16[896,128]{1,0:T(8,128)(2,1)S(1)}, bf16[896,128]{1,0:T(8,128)(2,1)S(1)}, u32[]{:S(2)}, u32[]{:S(2)}) collective-permute-start(bf16[896,128]{1,0:T(8,128)(2,1)S(1)} %fusion.2.rest_0_), channel_id=1, source_target_pairs={{0,8},{4,12},{8,0},{12,4},{1,9},{5,13},{9,1},{13,5},{2,10},{6,14},... | collective-permute-start | bytes 688136 | tf_op jit(solution)/shard_map/ppermute | solution.py:78
  16.5 15.5 %collective-permute-start.3 = (bf16[896,128]{1,0:T(8,128)(2,1)S(1)}, bf16[896,128]{1,0:T(8,128)(2,1)S(1)}, u32[]{:S(2)}, u32[]{:S(2)}) collective-permute-start(bf16[896,128]{1,0:T(8,128)(2,1)S(1)} %fusion.2.rest_0_), channel_id=1, source_target_pairs={{0,4},{4,0},{8,12},{12,8},{1,5},{5,1},{9,13},{13,9},{2,6},{6,2},{1... | collective-permute-start | bytes 688136 | tf_op jit(solution)/shard_map/ppermute | solution.py:78
  17.0 15.0 %collective-permute-start.10 = (bf16[32,2688]{1,0:T(8,128)(2,1)S(1)}, bf16[32,2688]{1,0:T(8,128)(2,1)S(1)}, u32[]{:S(2)}, u32[]{:S(2)}) collective-permute-start(bf16[32,2688]{1,0:T(8,128)(2,1)S(1)} %fusion.5.rest_3_), channel_id=1, source_target_pairs={{0,8},{4,12},{8,0},{12,4},{1,9},{5,13},{9,1},{13,5},{2,10},{6,14},... | collective-permute-start | bytes 516104 | tf_op jit(solution)/shard_map/ppermute | solution.py:78
  18.6 15.8 %collective-permute-start.9 = (bf16[32,2688]{1,0:T(8,128)(2,1)S(1)}, bf16[32,2688]{1,0:T(8,128)(2,1)S(1)}, u32[]{:S(2)}, u32[]{:S(2)}) collective-permute-start(bf16[32,2688]{1,0:T(8,128)(2,1)S(1)} %fusion.5.rest_3_), channel_id=1, source_target_pairs={{0,4},{4,0},{8,12},{12,8},{1,5},{5,1},{9,13},{13,9},{2,6},{6,2},{1... | collective-permute-start | bytes 516104 | tf_op jit(solution)/shard_map/ppermute | solution.py:78
  26.9 12.2 %collective-permute-start.6 = (bf16[896,128]{1,0:T(8,128)(2,1)S(1)}, bf16[896,128]{1,0:T(8,128)(2,1)S(1)}, u32[]{:S(2)}, u32[]{:S(2)}) collective-permute-start(bf16[896,128]{1,0:T(8,128)(2,1)S(1)} %collective-permute-done.4.rest_2_), channel_id=1, source_target_pairs={{0,4},{4,0},{8,12},{12,8},{1,5},{5,1},{9,13},{13,9},{2,6},{6,2},{1... | collective-permute-start | bytes 688136 | tf_op jit(solution)/shard_map/ppermute | solution.py:314
  32.0 10.7 %collective-permute-start.11 = (bf16[32,2688]{1,0:T(8,128)(2,1)S(1)}, bf16[32,2688]{1,0:T(8,128)(2,1)S(1)}, u32[]{:S(2)}, u32[]{:S(2)}) collective-permute-start(bf16[32,2688]{1,0:T(8,128)(2,1)S(1)} %collective-permute-done.10.rest_5_), channel_id=1, source_target_pairs={{0,4},{4,0},{8,12},{12,8},{1,5},{5,1},{9,13},{13,9},{2,6},{6,2},{1... | collective-permute-start | bytes 516104 | tf_op jit(solution)/shard_map/ppermute | solution.py:316
  34.5 10.4 %collective-permute-start.12 = (bf16[128,768]{1,0:T(8,128)(2,1)S(1)}, bf16[128,768]{1,0:T(8,128)(2,1)S(1)}, u32[]{:S(2)}, u32[]{:S(2)}) collective-permute-start(bf16[128,768]{1,0:T(8,128)(2,1)S(1)} %collective-permute-done.5.rest_2_), channel_id=1, source_target_pairs={{0,0},{4,4},{8,12},{12,8},{1,1},{5,5},{9,13},{13,9},{2,2},{6,6},{1... | collective-permute-start | bytes 589832 | tf_op jit(solution)/shard_map/ppermute | solution.py:318

commit v5 on v4

--- a/solution.py
+++ b/solution.py
@@ -238,12 +238,9 @@
 
     @pl.when((z * tokens < lengths[0]) & (z >= 2))
     def _():
-        heads = [head_columns([kv], h) for h in range(KVH)]
-        all_scores = [
-            dot_keys(queries[h * block : (h + 1) * block, :], heads[h][0]) for h in range(KVH)
-        ]
         for h in range(KVH):
-            scores, values = all_scores[h], heads[h][1]
+            keys, values = head_columns([kv], h)
+            scores = dot_keys(queries[h * block : (h + 1) * block, :], keys)
             weights, factors, totals = [], [], []
             for g in range(GROUP):
                 at = slice(h * block + g * tokens, h * block + (g + 1) * tokens)
@@ -300,20 +297,22 @@
         adapter_ids, adapter_slots, adapter_down, adapter_up
     )
     kv = kv_base[0]
-    kv_one, kv_two = spread(kv)
+    kv_two = lax.ppermute(kv, "ctx", TWO)
     near_down = lax.ppermute(give_down, "req", SIBLING)
     near_up = lax.ppermute(give_up, "req", SIBLING)
-    far_down = lax.ppermute(keep_down[1] + near_down[1], "req", ACROSS)
+    pass_down = keep_down[1] + near_down[1]
+    later = lax.optimization_barrier((kv, pass_down))[0]
+    kv_one = lax.ppermute(later, "ctx", ONE)
+    far_down = lax.ppermute(pass_down, "req", ACROSS)
     far_up = lax.ppermute(keep_up[1] + near_up[1], "req", ACROSS)
     down = keep_down[0] + near_down[0] + far_down
-    down, kv_one = lax.optimization_barrier((down, kv_one))
     down_one, down_two = spread(down)
     up = keep_up[0] + near_up[0] + far_up
     up_one, up_two = spread(up)
-    down_two = lax.optimization_barrier((down_two, kv_two))[0]
-    down_three = lax.ppermute(down_two, "ctx", ONE)
-    up_two = lax.optimization_barrier((up_two, down_one))[0]
-    up_three = lax.ppermute(up_two, "ctx", ONE)
+    ready = lax.optimization_barrier((down_two, kv_two))[0]
+    down_three = lax.ppermute(ready, "ctx", ONE)
+    ready = lax.optimization_barrier((up_two, down_one, kv_one))[0]
+    up_three = lax.ppermute(ready, "ctx", ONE)
     kv_last = lax.optimization_barrier((kv_two, up_two, up_one))[0]
     kv_three = lax.ppermute(kv_last, "ctx", LAST)
     downs = [down, down_one, down_two, down_three]

time: 47.7 us -> 49 us (1.027)
  the two profiles are of different devices: /device:TPU:18 before, /device:TPU:29 now
where the time goes in v5:
time: 49 us; the launch traced here: 48.1 us
  waiting for transfers between devices  33.2 us (68%)
  starting transfers between devices  6.88 us (14%)
  Pallas kernels  6.44 us (13%)
  other arithmetic  0.89 us (2%)
  between operations  0.71 us (1%)
    ppermute x4, waiting for transfers between devices, spread(): return (lax.ppermute(shard, 'ctx', ONE), lax.ppermute(shard, 'ctx', TWO))  17 us
    ppermute x1, waiting for transfers between devices, body(): far_down = lax.ppermute(pass_down, 'req', ACROSS)  5.08 us
    ppermute x1, waiting for transfers between devices, body(): far_up = lax.ppermute(keep_up[1] + near_up[1], 'req', ACROSS)  2.77 us
    ppermute x1, waiting for transfers between devices, body(): up_three = lax.ppermute(ready, 'ctx', ONE)  2.73 us
    ppermute x1, starting transfers between devices, body(): kv_three = lax.ppermute(kv_last, 'ctx', LAST)  2.55 us
    ppermute x1, waiting for transfers between devices, body(): kv_three = lax.ppermute(kv_last, 'ctx', LAST)  2.21 us
    pallas_call x1, Pallas kernels, attend(): pl.pallas_call(attend_kernel, out_shape=shapes, in_specs=[spec(SMEM)] + [...  1.99 us
    pallas_call x1, Pallas kernels, finish(): pl.pallas_call(finish_kernel, out_shape=jax.ShapeDtypeStruct(so_far.shape...  1.83 us
  transfers between devices with their start and end apart: 13, of which 10 were waited for; matrix products, arithmetic and copies ran while one was open for 0% of the time, Pallas kernels for 6%

profile of v5, /device:TPU:29, one launch (start us, length us, event | category | flops | bytes accessed | tf_op | source)
XLA Modules:
  0.0 48.1 jit_solution(18384551241780077878)
XLA Ops:
  0.0 0.7 %pad_add_fusion.table = s32[68]{0:T(128)S(1)} fusion(s32[64]{0:T(128)} %param.15, s32[4]{0:T(128)} %ids.1), kind=kLoop, calls=%fused_computation.10 | loop fusion | flops 68 | bytes 544 | tf_op jit(solution)/shard_map/concatenate | solution.py:67
  0.7 0.0 copy-start.4
  0.7 1.7 %shard_map.91 = (bf16[2,896,128]{2,1,0:T(8,128)(2,1)S(1)}, bf16[2,896,128]{2,1,0:T(8,128)(2,1)S(1)}, bf16[2,32,2688]{2,1,0:T(8,128)(2,1)S(1)}, bf16[2,32,2688]{2,1,0:T(8,128)(2,1)S(1)}) custom-call(s32[68]{0:T(128)S(1)} %pad_add_fusion.table, bf16[16,896,128]{2,1,0:T(8,128)(2,1)} %rest_0_.1, bf16[16,32,2688]{2,1,0:T(8,128)(2,1)} %rest_1_.1), custom_call_target="tpu_custom_call" | custom-call | tf_op jit(solution)/shard_map/pallas_call | solution.py:60
  2.4 1.1 %collective-permute-start = (bf16[2,896,128]{2,1,0:T(8,128)(2,1)S(1)}, bf16[2,896,128]{2,1,0:T(8,128)(2,1)S(1)}, u32[]{:S(2)}, u32[]{:S(2)}) collective-permute-start(bf16[2,896,128]{2,1,0:T(8,128)(2,1)S(1)} %get-tuple-element.19), channel_id=1, source_target_pairs={{0,1},{1,0},{2,3},{3,2},{4,5},{5,4},{6,7},{7,6},{8,9},{9,8},{10,11... | collective-permute-start | bytes 1376264 | tf_op jit(solution)/shard_map/ppermute | solution.py:301
  3.5 0.1 collective-permute-start.7
  3.6 0.0 copy-done.4
  3.6 0.1 collective-permute-start.4
  3.6 1.3 %collective-permute-done = bf16[2,896,128]{2,1,0:T(8,128)(2,1)S(1)} collective-permute-done((bf16[2,896,128]{2,1,0:T(8,128)(2,1)S(1)}, bf16[2,896,128]{2,1,0:T(8,128)(2,1)S(1)}, u32[]{:S(2)}, u32[]{:S(2)}) %collective-permute-start) | collective-permute-done | bytes 458784 | tf_op jit(solution)/shard_map/ppermute | solution.py:301
  4.9 0.0 copy-start
  4.9 0.0 copy-start.1
  4.9 0.0 copy-start.2
  5.0 0.1 collective-permute-start.1
  5.1 0.3 collective-permute-done.7
  5.4 1.1 %collective-permute-start.8 = (bf16[32,2688]{1,0:T(8,128)(2,1)S(1)}, bf16[32,2688]{1,0:T(8,128)(2,1)S(1)}, u32[]{:S(2)}, u32[]{:S(2)}) collective-permute-start(bf16[32,2688]{1,0:T(8,128)(2,1)S(1)} %fusion.3), channel_id=1, source_target_pairs={{0,2},{1,3},{2,0},{3,1},{4,6},{5,7},{6,4},{7,5},{8,10},{9,11},{10,... | collective-permute-start | bytes 516104 | tf_op jit(solution)/shard_map/ppermute | solution.py:307
  6.6 0.2 collective-permute-start.6
  6.8 5.1 %collective-permute-done.1 = bf16[896,128]{1,0:T(8,128)(2,1)S(1)} collective-permute-done((bf16[896,128]{1,0:T(8,128)(2,1)S(1)}, bf16[896,128]{1,0:T(8,128)(2,1)S(1)}, u32[]{:S(2)}, u32[]{:S(2)}) %collective-permute-start.1) | collective-permute-done | bytes 229408 | tf_op jit(solution)/shard_map/ppermute | solution.py:306
  11.9 0.0 copy-start.3
  11.9 0.7 %collective-permute-start.3 = (bf16[896,128]{1,0:T(8,128)(2,1)S(1)}, bf16[896,128]{1,0:T(8,128)(2,1)S(1)}, u32[]{:S(2)}, u32[]{:S(2)}) collective-permute-start(bf16[896,128]{1,0:T(8,128)(2,1)S(1)} %fusion.2.rest_0_), channel_id=1, source_target_pairs={{0,8},{4,12},{8,0},{12,4},{1,9},{5,13},{9,1},{13,5},{2,10},{6,14},... | collective-permute-start | bytes 688136 | tf_op jit(solution)/shard_map/ppermute | solution.py:78
  12.6 0.2 collective-permute-start.2
  12.8 2.8 %collective-permute-done.8 = bf16[32,2688]{1,0:T(8,128)(2,1)S(1)} collective-permute-done((bf16[32,2688]{1,0:T(8,128)(2,1)S(1)}, bf16[32,2688]{1,0:T(8,128)(2,1)S(1)}, u32[]{:S(2)}, u32[]{:S(2)}) %collective-permute-start.8) | collective-permute-done | bytes 172064 | tf_op jit(solution)/shard_map/ppermute | solution.py:307
  15.6 0.7 %collective-permute-start.10 = (bf16[32,2688]{1,0:T(8,128)(2,1)S(1)}, bf16[32,2688]{1,0:T(8,128)(2,1)S(1)}, u32[]{:S(2)}, u32[]{:S(2)}) collective-permute-start(bf16[32,2688]{1,0:T(8,128)(2,1)S(1)} %fusion.5.rest_3_), channel_id=1, source_target_pairs={{0,8},{4,12},{8,0},{12,4},{1,9},{5,13},{9,1},{13,5},{2,10},{6,14},... | collective-permute-start | bytes 516104 | tf_op jit(solution)/shard_map/ppermute | solution.py:78
  16.3 0.0 collective-permute-done.4.rest_2_
  16.3 0.2 collective-permute-start.9
  16.4 10.7 %collective-permute-done.3.rest_2_ = bf16[896,128]{1,0:T(8,128)(2,1)S(1)} collective-permute-done((bf16[896,128]{1,0:T(8,128)(2,1)S(1)}, bf16[896,128]{1,0:T(8,128)(2,1)S(1)}, u32[]{:S(2)}, u32[]{:S(2)}) %collective-permute-start.3) | collective-permute-done | bytes 229408 | tf_op jit(solution)/shard_map/ppermute | solution.py:78
  27.1 0.0 collective-permute-start.5
  27.1 0.0 collective-permute-done.6.rest_1_
  27.1 5.5 %collective-permute-done.10.rest_5_ = bf16[32,2688]{1,0:T(8,128)(2,1)S(1)} collective-permute-done((bf16[32,2688]{1,0:T(8,128)(2,1)S(1)}, bf16[32,2688]{1,0:T(8,128)(2,1)S(1)}, u32[]{:S(2)}, u32[]{:S(2)}) %collective-permute-start.10) | collective-permute-done | bytes 172064 | tf_op jit(solution)/shard_map/ppermute | solution.py:78
  32.6 0.0 collective-permute-done.2.rest_1_
  32.6 0.0 collective-permute-start.11
  32.6 0.8 %collective-permute-done.9.rest_4_ = bf16[32,2688]{1,0:T(8,128)(2,1)S(1)} collective-permute-done((bf16[32,2688]{1,0:T(8,128)(2,1)S(1)}, bf16[32,2688]{1,0:T(8,128)(2,1)S(1)}, u32[]{:S(2)}, u32[]{:S(2)}) %collective-permute-start.9) | collective-permute-done | bytes 172064 | tf_op jit(solution)/shard_map/ppermute | solution.py:78
  33.5 2.5 %collective-permute-start.12 = (bf16[128,768]{1,0:T(8,128)(2,1)S(1)}, bf16[128,768]{1,0:T(8,128)(2,1)S(1)}, u32[]{:S(2)}, u32[]{:S(2)}) collective-permute-start(bf16[128,768]{1,0:T(8,128)(2,1)S(1)} %collective-permute-done.4.rest_2_), channel_id=1, source_target_pairs={{0,0},{4,4},{8,12},{12,8},{1,1},{5,5},{9,13},{13,9},{2,2},{6,6},{1... | collective-permute-start | bytes 589832 | tf_op jit(solution)/shard_map/ppermute | solution.py:317
  36.7 1.7 %collective-permute-done.5.rest_3_ = bf16[896,128]{1,0:T(8,128)(2,1)S(1)} collective-permute-done((bf16[896,128]{1,0:T(8,128)(2,1)S(1)}, bf16[896,128]{1,0:T(8,128)(2,1)S(1)}, u32[]{:S(2)}, u32[]{:S(2)}) %collective-permute-start.5) | collective-permute-done | bytes 229408 | tf_op jit(solution)/shard_map/ppermute | solution.py:313
  38.4 0.0 copy-done
  38.4 0.0 copy-done.1
  38.4 0.0 copy-done.2
  38.4 0.9 %shard_map.92.low = bf16[128,128]{1,0:T(8,128)(2,1)S(1)} custom-call(s32[4]{0:T(128)S(1)} %copy-done.1, s32[64]{0:T(128)S(1)} %copy-done.2, bf16[128,3584]{1,0:T(8,128)(2,1)S(1)} %bitcast.16, bf16[896,128]{1,0:T(8,128)(2,1)S(1)} %fusion.2.rest_0_, bf16[896,128]{1,0:T(8,128)(2,1)S(1)} %collective-permute-done.2.rest_1_, ...), custom_call_target="tpu_custom_call" | custom-call | flops 134217728 | bytes 4194304 | tf_op jit(solution)/shard_map/pallas_call | solution.py:97
  39.3 2.7 %collective-permute-done.11.rest_6_ = bf16[32,2688]{1,0:T(8,128)(2,1)S(1)} collective-permute-done((bf16[32,2688]{1,0:T(8,128)(2,1)S(1)}, bf16[32,2688]{1,0:T(8,128)(2,1)S(1)}, u32[]{:S(2)}, u32[]{:S(2)}) %collective-permute-start.11) | collective-permute-done | bytes 172064 | tf_op jit(solution)/shard_map/ppermute | solution.py:315
  42.1 0.0 copy-done.3
  42.1 2.0 %shard_map.93 = (bf16[128,2688]{1,0:T(8,128)(2,1)}, bf16[2688,128]{1,0:T(8,128)(2,1)S(1)}, f32[2688,128]{1,0:T(8,128)S(1)}, f32[2688,128]{1,0:T(8,128)S(1)}, f32[2688,128]{1,0:T(8,128)S(1)}) custom-call(s32[1]{0:T(128)S(6)} %copy.12.lengths, bf16[128,2688]{1,0:T(8,128)(2,1)S(1)} %bitcast.17, bf16[128,128]{1,0:T(8,128)(2,1)S(1)} %shard_map.92.low, ...), custom_call_target="tpu_custom_call" | custom-call | flops 1073741824 | bytes 4194304 | tf_op jit(solution)/shard_map/pallas_call | solution.py:215
  44.1 2.2 %collective-permute-done.12.kv = bf16[128,768]{1,0:T(8,128)(2,1)S(1)} collective-permute-done((bf16[128,768]{1,0:T(8,128)(2,1)S(1)}, bf16[128,768]{1,0:T(8,128)(2,1)S(1)}, u32[]{:S(2)}, u32[]{:S(2)}) %collective-permute-start.12) | collective-permute-done | bytes 196640 | tf_op jit(solution)/shard_map/ppermute | solution.py:317
  46.3 1.8 %shard_map.94 = bf16[128,2688]{1,0:T(8,128)(2,1)} custom-call(s32[1]{0:T(128)S(6)} %copy.12.lengths, bf16[128,2688]{1,0:T(8,128)(2,1)} %get-tuple-element.25.so_far, bf16[2688,128]{1,0:T(8,128)(2,1)S(1)} %get-tuple-element.26.queries, f32[2688,128]{1,0:T(8,128)S(1)} %get-tuple-element.27.sums, ...), custom_call_target="tpu_custom_call", output_to_operand_aliasing={{}: (1, {})} | custom-call | flops 268435456 | bytes 2097152 | tf_op jit(solution)/shard_map/pallas_call | solution.py:268
  (4 shorter events, 0.1 us)
Async XLA Ops:
  0.7 2.8 %copy-start.4 = (bf16[1,128,768]{2,1,0:T(8,128)(2,1)S(1)}, bf16[1,128,768]{2,1,0:T(8,128)(2,1)}, u32[]{:S(2)}) copy-start(bf16[1,128,768]{2,1,0:T(8,128)(2,1)} %param.11) | copy-start | bytes 589828
  2.4 2.5 %collective-permute-start = (bf16[2,896,128]{2,1,0:T(8,128)(2,1)S(1)}, bf16[2,896,128]{2,1,0:T(8,128)(2,1)S(1)}, u32[]{:S(2)}, u32[]{:S(2)}) collective-permute-start(bf16[2,896,128]{2,1,0:T(8,128)(2,1)S(1)} %get-tuple-element.19), channel_id=1, source_target_pairs={{0,1},{1,0},{2,3},{3,2},{4,5},{5,4},{6,7},{7,6},{8,9},{9,8},{10,11... | collective-permute-start | bytes 1376264 | tf_op jit(solution)/shard_map/ppermute | solution.py:301
  3.5 1.9 %collective-permute-start.7 = (bf16[2,32,2688]{2,1,0:T(8,128)(2,1)S(1)}, bf16[2,32,2688]{2,1,0:T(8,128)(2,1)S(1)}, u32[]{:S(2)}, u32[]{:S(2)}) collective-permute-start(bf16[2,32,2688]{2,1,0:T(8,128)(2,1)S(1)} %get-tuple-element.23), channel_id=1, source_target_pairs={{0,1},{1,0},{2,3},{3,2},{4,5},{5,4},{6,7},{7,6},{8,9},{9,8},{10,11... | collective-permute-start | bytes 1032200 | tf_op jit(solution)/shard_map/ppermute | solution.py:302
  3.6 12.7 %collective-permute-start.4 = (bf16[128,768]{1,0:T(8,128)(2,1)S(1)}, bf16[128,768]{1,0:T(8,128)(2,1)S(1)}, u32[]{:S(2)}, u32[]{:S(2)}) collective-permute-start(bf16[128,768]{1,0:T(8,128)(2,1)S(1)} %bitcast.18), channel_id=1, source_target_pairs={{0,8},{4,12},{8,0},{12,4},{1,9},{5,13},{9,1},{13,5},{2,10},{6,14},... | collective-permute-start | bytes 589832 | tf_op jit(solution)/shard_map/ppermute | solution.py:300
  4.9 33.5 %copy-start = (bf16[1,128,3584]{2,1,0:T(8,128)(2,1)S(1)}, bf16[1,128,3584]{2,1,0:T(8,128)(2,1)}, u32[]{:S(2)}) copy-start(bf16[1,128,3584]{2,1,0:T(8,128)(2,1)} %param.9) | copy-start | bytes 2752516
  4.9 33.5 %copy-start.1 = (s32[4]{0:T(128)S(1)}, s32[4]{0:T(128)}, u32[]{:S(2)}) copy-start(s32[4]{0:T(128)} %ids.1) | copy-start | bytes 52
  4.9 33.5 %copy-start.2 = (s32[64]{0:T(128)S(1)}, s32[64]{0:T(128)}, u32[]{:S(2)}) copy-start(s32[64]{0:T(128)} %ranks.1) | copy-start | bytes 772
  5.0 6.9 %collective-permute-start.1 = (bf16[896,128]{1,0:T(8,128)(2,1)S(1)}, bf16[896,128]{1,0:T(8,128)(2,1)S(1)}, u32[]{:S(2)}, u32[]{:S(2)}) collective-permute-start(bf16[896,128]{1,0:T(8,128)(2,1)S(1)} %fusion), channel_id=1, source_target_pairs={{0,2},{1,3},{2,0},{3,1},{4,6},{5,7},{6,4},{7,5},{8,10},{9,11},{10,... | collective-permute-start | bytes 688136 | tf_op jit(solution)/shard_map/ppermute | solution.py:306
  5.4 10.1 %collective-permute-start.8 = (bf16[32,2688]{1,0:T(8,128)(2,1)S(1)}, bf16[32,2688]{1,0:T(8,128)(2,1)S(1)}, u32[]{:S(2)}, u32[]{:S(2)}) collective-permute-start(bf16[32,2688]{1,0:T(8,128)(2,1)S(1)} %fusion.3), channel_id=1, source_target_pairs={{0,2},{1,3},{2,0},{3,1},{4,6},{5,7},{6,4},{7,5},{8,10},{9,11},{10,... | collective-permute-start | bytes 516104 | tf_op jit(solution)/shard_map/ppermute | solution.py:307
  6.6 20.5 %collective-permute-start.6 = (bf16[128,768]{1,0:T(8,128)(2,1)S(1)}, bf16[128,768]{1,0:T(8,128)(2,1)S(1)}, u32[]{:S(2)}, u32[]{:S(2)}) collective-permute-start(bf16[128,768]{1,0:T(8,128)(2,1)S(1)} %bitcast.19), channel_id=1, source_target_pairs={{0,4},{4,0},{8,12},{12,8},{1,5},{5,1},{9,13},{13,9},{2,6},{6,2},{1... | collective-permute-start | bytes 589832 | tf_op jit(solution)/shard_map/ppermute | solution.py:305
  11.9 30.2 %copy-start.3 = (bf16[1,128,2688]{2,1,0:T(8,128)(2,1)S(1)}, bf16[1,128,2688]{2,1,0:T(8,128)(2,1)}, u32[]{:S(2)}) copy-start(bf16[1,128,2688]{2,1,0:T(8,128)(2,1)} %param.10) | copy-start | bytes 2064388
  11.9 15.2 %collective-permute-start.3 = (bf16[896,128]{1,0:T(8,128)(2,1)S(1)}, bf16[896,128]{1,0:T(8,128)(2,1)S(1)}, u32[]{:S(2)}, u32[]{:S(2)}) collective-permute-start(bf16[896,128]{1,0:T(8,128)(2,1)S(1)} %fusion.2.rest_0_), channel_id=1, source_target_pairs={{0,8},{4,12},{8,0},{12,4},{1,9},{5,13},{9,1},{13,5},{2,10},{6,14},... | collective-permute-start | bytes 688136 | tf_op jit(solution)/shard_map/ppermute | solution.py:78
  12.6 20.0 %collective-permute-start.2 = (bf16[896,128]{1,0:T(8,128)(2,1)S(1)}, bf16[896,128]{1,0:T(8,128)(2,1)S(1)}, u32[]{:S(2)}, u32[]{:S(2)}) collective-permute-start(bf16[896,128]{1,0:T(8,128)(2,1)S(1)} %fusion.2.rest_0_), channel_id=1, source_target_pairs={{0,4},{4,0},{8,12},{12,8},{1,5},{5,1},{9,13},{13,9},{2,6},{6,2},{1... | collective-permute-start | bytes 688136 | tf_op jit(solution)/shard_map/ppermute | solution.py:78
  15.6 17.1 %collective-permute-start.10 = (bf16[32,2688]{1,0:T(8,128)(2,1)S(1)}, bf16[32,2688]{1,0:T(8,128)(2,1)S(1)}, u32[]{:S(2)}, u32[]{:S(2)}) collective-permute-start(bf16[32,2688]{1,0:T(8,128)(2,1)S(1)} %fusion.5.rest_3_), channel_id=1, source_target_pairs={{0,8},{4,12},{8,0},{12,4},{1,9},{5,13},{9,1},{13,5},{2,10},{6,14},... | collective-permute-start | bytes 516104 | tf_op jit(solution)/shard_map/ppermute | solution.py:78
  16.3 17.2 %collective-permute-start.9 = (bf16[32,2688]{1,0:T(8,128)(2,1)S(1)}, bf16[32,2688]{1,0:T(8,128)(2,1)S(1)}, u32[]{:S(2)}, u32[]{:S(2)}) collective-permute-start(bf16[32,2688]{1,0:T(8,128)(2,1)S(1)} %fusion.5.rest_3_), channel_id=1, source_target_pairs={{0,4},{4,0},{8,12},{12,8},{1,5},{5,1},{9,13},{13,9},{2,6},{6,2},{1... | collective-permute-start | bytes 516104 | tf_op jit(solution)/shard_map/ppermute | solution.py:78
  27.1 11.3 %collective-permute-start.5 = (bf16[896,128]{1,0:T(8,128)(2,1)S(1)}, bf16[896,128]{1,0:T(8,128)(2,1)S(1)}, u32[]{:S(2)}, u32[]{:S(2)}) collective-permute-start(bf16[896,128]{1,0:T(8,128)(2,1)S(1)} %collective-permute-done.3.rest_2_), channel_id=1, source_target_pairs={{0,4},{4,0},{8,12},{12,8},{1,5},{5,1},{9,13},{13,9},{2,6},{6,2},{1... | collective-permute-start | bytes 688136 | tf_op jit(solution)/shard_map/ppermute | solution.py:313
  32.6 9.4 %collective-permute-start.11 = (bf16[32,2688]{1,0:T(8,128)(2,1)S(1)}, bf16[32,2688]{1,0:T(8,128)(2,1)S(1)}, u32[]{:S(2)}, u32[]{:S(2)}) collective-permute-start(bf16[32,2688]{1,0:T(8,128)(2,1)S(1)} %collective-permute-done.10.rest_5_), channel_id=1, source_target_pairs={{0,4},{4,0},{8,12},{12,8},{1,5},{5,1},{9,13},{13,9},{2,6},{6,2},{1... | collective-permute-start | bytes 516104 | tf_op jit(solution)/shard_map/ppermute | solution.py:315
  33.5 12.8 %collective-permute-start.12 = (bf16[128,768]{1,0:T(8,128)(2,1)S(1)}, bf16[128,768]{1,0:T(8,128)(2,1)S(1)}, u32[]{:S(2)}, u32[]{:S(2)}) collective-permute-start(bf16[128,768]{1,0:T(8,128)(2,1)S(1)} %collective-permute-done.4.rest_2_), channel_id=1, source_target_pairs={{0,0},{4,4},{8,12},{12,8},{1,1},{5,5},{9,13},{13,9},{2,2},{6,6},{1... | collective-permute-start | bytes 589832 | tf_op jit(solution)/shard_map/ppermute | solution.py:317

commit v6 on v5

--- a/solution.py
+++ b/solution.py
@@ -78,31 +78,44 @@
     return lax.ppermute(shard, "ctx", ONE), lax.ppermute(shard, "ctx", TWO)
 
 
-def low_rank_kernel(ids, ranks, hidden, *rest):
-    pieces, out, accum = rest[:-2], rest[-2], rest[-1]
+def product_kernel(features, piece, out):
+    rows = piece.shape[0]
+    out[...] = jnp.dot(features[:, -rows:], piece[...], preferred_element_type=jnp.float32)
+
+
+def product(features, piece):
+    return pl.pallas_call(
+        product_kernel,
+        out_shape=jax.ShapeDtypeStruct((features.shape[0], piece.shape[1]), jnp.float32),
+        in_specs=[spec(VMEM)] * 2,
+        out_specs=spec(VMEM),
+        compiler_params=PARAMS,
+        cost_estimate=pl.CostEstimate(flops=1 << 25, bytes_accessed=1 << 19, transcendentals=0),
+    )(features, piece)
+
+
+def low_rank_kernel(ids, ranks, hidden, partial, *rest):
+    pieces, out = rest[:-1], rest[-1]
     rows = pieces[0].shape[0]
     rank = ranks[ids[lax.axis_index("req")]]
-    accum[...] = jnp.zeros_like(accum)
-    for flip, piece in enumerate(pieces):
+    total = partial[...]
+    for flip, piece in zip((0, 2, 3), pieces):
         place = lax.axis_index("ctx") ^ flip
         columns = pl.ds(pl.multiple_of(place * rows, HD), rows)
-        accum[...] += jnp.dot(hidden[:, columns], piece[...], preferred_element_type=jnp.float32)
-
-    column = lax.broadcasted_iota(jnp.int32, accum.shape, 1)
-    out[...] = jnp.where(column < rank, accum[...], 0.0).astype(jnp.bfloat16)
-
-
-def low_rank(ids, ranks, hidden, pieces):
-    shape = (hidden.shape[0], pieces[0].shape[1])
+        total += jnp.dot(hidden[:, columns], piece[...], preferred_element_type=jnp.float32)
+    column = lax.broadcasted_iota(jnp.int32, total.shape, 1)
+    out[...] = jnp.where(column < rank, total, 0.0).astype(jnp.bfloat16)
+
+
+def low_rank(ids, ranks, hidden, partial, pieces):
     return pl.pallas_call(
         low_rank_kernel,
-        out_shape=jax.ShapeDtypeStruct(shape, jnp.bfloat16),
-        in_specs=[spec(SMEM)] * 2 + [spec(VMEM)] * (1 + len(pieces)),
+        out_shape=jax.ShapeDtypeStruct(partial.shape, jnp.bfloat16),
+        in_specs=[spec(SMEM)] * 2 + [spec(VMEM)] * (2 + len(pieces)),
         out_specs=spec(VMEM),
-        scratch_shapes=[VMEM(shape, jnp.float32)],
         compiler_params=PARAMS,
         cost_estimate=pl.CostEstimate(flops=1 << 27, bytes_accessed=1 << 22, transcendentals=0),
-    )(ids, ranks, hidden, *pieces)
+    )(ids, ranks, hidden, partial, *pieces)
 
 
 FACTOR = LOG2E / math.sqrt(HD)
@@ -296,28 +309,30 @@
     keep_down, give_down, keep_up, give_up = select(
         adapter_ids, adapter_slots, adapter_down, adapter_up
     )
-    kv = kv_base[0]
+    kv, hidden = kv_base[0], hidden_states[0]
+    rows = adapter_down.shape[1]
+    start = (lax.axis_index("ctx") ^ 1) * rows
+    columns = lax.dynamic_slice_in_dim(hidden, start, rows, 1)
+    kv_one = lax.ppermute(jnp.concatenate([kv, columns], axis=1), "ctx", ONE)
     kv_two = lax.ppermute(kv, "ctx", TWO)
     near_down = lax.ppermute(give_down, "req", SIBLING)
     near_up = lax.ppermute(give_up, "req", SIBLING)
-    pass_down = keep_down[1] + near_down[1]
-    later = lax.optimization_barrier((kv, pass_down))[0]
-    kv_one = lax.ppermute(later, "ctx", ONE)
-    far_down = lax.ppermute(pass_down, "req", ACROSS)
+    far_down = lax.ppermute(keep_down[1] + near_down[1], "req", ACROSS)
     far_up = lax.ppermute(keep_up[1] + near_up[1], "req", ACROSS)
     down = keep_down[0] + near_down[0] + far_down
-    down_one, down_two = spread(down)
+    down_two = lax.ppermute(down, "ctx", TWO)
+    partial = lax.ppermute(product(kv_one, down), "ctx", ONE)
     up = keep_up[0] + near_up[0] + far_up
     up_one, up_two = spread(up)
-    ready = lax.optimization_barrier((down_two, kv_two))[0]
+    ready = lax.optimization_barrier((down_two, kv_two, partial))[0]
     down_three = lax.ppermute(ready, "ctx", ONE)
-    ready = lax.optimization_barrier((up_two, down_one, kv_one))[0]
+    ready = up_two
     up_three = lax.ppermute(ready, "ctx", ONE)
     kv_last = lax.optimization_barrier((kv_two, up_two, up_one))[0]
     kv_three = lax.ppermute(kv_last, "ctx", LAST)
-    downs = [down, down_one, down_two, down_three]
+    downs = [down, down_two, down_three]
     ups = [up, up_one, up_two, up_three]
-    low = low_rank(adapter_ids, rank_buckets, hidden_states[0], downs)
+    low = low_rank(adapter_ids, rank_buckets, hidden, partial, downs)
     parts = attend(lengths, queries_base[0], low, [kv, kv_one, kv_two], ups)
     return finish(lengths, *parts, kv_three)[None]
 

time: 49 us -> 50.6 us (1.033)
  the two profiles are of different devices: /device:TPU:29 before, /device:TPU:28 now
where the time goes in v6:
time: 50.6 us; the launch traced here: 50.4 us
  waiting for transfers between devices  27 us (53%)
  starting transfers between devices  14.2 us (28%)
  Pallas kernels  5.7 us (11%)
  other arithmetic  2.76 us (5%)
  between operations  0.75 us (1%)
    ppermute x1, waiting for transfers between devices, body(): partial = lax.ppermute(product(kv_one, down), 'ctx', ONE)  7.05 us
    ppermute x1, waiting for transfers between devices, body(): far_down = lax.ppermute(keep_down[1] + near_down[1], 'req', ACROSS)  5.32 us
    ppermute x1, waiting for transfers between devices, body(): kv_one = lax.ppermute(jnp.concatenate([kv, columns], axis=1), 'ctx', ONE)  5.19 us
    ppermute x2, starting transfers between devices, spread(): return (lax.ppermute(shard, 'ctx', ONE), lax.ppermute(shard, 'ctx', TWO))  4 us
    ppermute x1, waiting for transfers between devices, body(): up_three = lax.ppermute(ready, 'ctx', ONE)  2.8 us
    ppermute x1, waiting for transfers between devices, body(): down_three = lax.ppermute(ready, 'ctx', ONE)  2.35 us
    ppermute x1, starting transfers between devices, body(): down_two = lax.ppermute(down, 'ctx', TWO)  2.14 us
    ppermute x1, starting transfers between devices, body(): up_three = lax.ppermute(ready, 'ctx', ONE)  2.02 us
  transfers between devices with their start and end apart: 13, of which 9 were waited for; matrix products, arithmetic and copies ran while one was open for 4% of the time, Pallas kernels for 6%

profile of v6, /device:TPU:28, one launch (start us, length us, event | category | flops | bytes accessed | tf_op | source)
XLA Modules:
  0.0 50.4 jit_solution(706144523141907071)
XLA Ops:
  0.0 0.7 %pad_add_fusion.table = s32[68]{0:T(128)S(1)} fusion(s32[64]{0:T(128)} %param.15, s32[4]{0:T(128)} %ids.1), kind=kLoop, calls=%fused_computation.12 | loop fusion | flops 68 | bytes 544 | tf_op jit(solution)/shard_map/concatenate | solution.py:67
  0.7 0.0 copy-start.1
  0.7 0.0 copy-start
  0.8 0.8 %shard_map.91 = (bf16[2,896,128]{2,1,0:T(8,128)(2,1)S(1)}, bf16[2,896,128]{2,1,0:T(8,128)(2,1)S(1)}, bf16[2,32,2688]{2,1,0:T(8,128)(2,1)S(1)}, bf16[2,32,2688]{2,1,0:T(8,128)(2,1)S(1)}) custom-call(s32[68]{0:T(128)S(1)} %pad_add_fusion.table, bf16[16,896,128]{2,1,0:T(8,128)(2,1)} %rest_0_.1, bf16[16,32,2688]{2,1,0:T(8,128)(2,1)} %rest_1_.1), custom_call_target="tpu_custom_call" | custom-call | tf_op jit(solution)/shard_map/pallas_call | solution.py:60
  1.6 1.0 %collective-permute-start.1 = (bf16[2,896,128]{2,1,0:T(8,128)(2,1)S(1)}, bf16[2,896,128]{2,1,0:T(8,128)(2,1)S(1)}, u32[]{:S(2)}, u32[]{:S(2)}) collective-permute-start(bf16[2,896,128]{2,1,0:T(8,128)(2,1)S(1)} %get-tuple-element.17), channel_id=1, source_target_pairs={{0,1},{1,0},{2,3},{3,2},{4,5},{5,4},{6,7},{7,6},{8,9},{9,8},{10,11... | collective-permute-start | bytes 1376264 | tf_op jit(solution)/shard_map/ppermute | solution.py:318
  2.5 0.0 copy-done.1
  2.5 0.3 collective-permute-start.5
  2.9 0.0 collective-permute-start.7
  2.9 0.0 copy-done
  2.9 0.5 %collective-permute-start = (bf16[128,1664]{1,0:T(8,128)(2,1)S(1)}, bf16[128,1664]{1,0:T(8,128)(2,1)S(1)}, u32[]{:S(2)}, u32[]{:S(2)}) collective-permute-start(bf16[128,1664]{1,0:T(8,128)(2,1)S(1)} %pad_maximum_fusion), channel_id=1, source_target_pairs={{0,4},{4,0},{8,12},{12,8},{1,5},{5,1},{9,13},{13,9},{2,6},{6,2},{1... | collective-permute-start | bytes 1277960 | tf_op jit(solution)/shard_map/ppermute | solution.py:316
  3.4 0.5 %collective-permute-done.1 = bf16[2,896,128]{2,1,0:T(8,128)(2,1)S(1)} collective-permute-done((bf16[2,896,128]{2,1,0:T(8,128)(2,1)S(1)}, bf16[2,896,128]{2,1,0:T(8,128)(2,1)S(1)}, u32[]{:S(2)}, u32[]{:S(2)}) %collective-permute-start.1) | collective-permute-done | bytes 458784 | tf_op jit(solution)/shard_map/ppermute | solution.py:318
  4.0 1.6 %collective-permute-start.2 = (bf16[896,128]{1,0:T(8,128)(2,1)S(1)}, bf16[896,128]{1,0:T(8,128)(2,1)S(1)}, u32[]{:S(2)}, u32[]{:S(2)}) collective-permute-start(bf16[896,128]{1,0:T(8,128)(2,1)S(1)} %fusion), channel_id=1, source_target_pairs={{0,2},{1,3},{2,0},{3,1},{4,6},{5,7},{6,4},{7,5},{8,10},{9,11},{10,... | collective-permute-start | bytes 688136 | tf_op jit(solution)/shard_map/ppermute | solution.py:320
  5.6 0.0 collective-permute-done.7
  5.6 0.0 copy-start.2
  5.6 0.0 copy-start.3
  5.6 1.0 %fusion.3 = bf16[32,2688]{1,0:T(8,128)(2,1)S(1)} fusion(bf16[2,32,2688]{2,1,0:T(8,128)(2,1)} %collective-permute-done.7, bf16[2,32,2688]{2,1,0:T(8,128)(2,1)S(1)} %get-tuple-element.19), kind=kLoop, calls=%fused_computation.8 | loop fusion | flops 86016 | bytes 516096 | tf_op jit(solution)/shard_map/add | solution.py:321
  6.5 0.6 %collective-permute-start.8 = (bf16[32,2688]{1,0:T(8,128)(2,1)S(1)}, bf16[32,2688]{1,0:T(8,128)(2,1)S(1)}, u32[]{:S(2)}, u32[]{:S(2)}) collective-permute-start(bf16[32,2688]{1,0:T(8,128)(2,1)S(1)} %fusion.3), channel_id=1, source_target_pairs={{0,2},{1,3},{2,0},{3,1},{4,6},{5,7},{6,4},{7,5},{8,10},{9,11},{10,... | collective-permute-start | bytes 516104 | tf_op jit(solution)/shard_map/ppermute | solution.py:321
  7.2 5.3 %collective-permute-done.2 = bf16[896,128]{1,0:T(8,128)(2,1)S(1)} collective-permute-done((bf16[896,128]{1,0:T(8,128)(2,1)S(1)}, bf16[896,128]{1,0:T(8,128)(2,1)S(1)}, u32[]{:S(2)}, u32[]{:S(2)}) %collective-permute-start.2) | collective-permute-done | bytes 229408 | tf_op jit(solution)/shard_map/ppermute | solution.py:320
  12.5 2.1 %collective-permute-start.4 = (bf16[896,128]{1,0:T(8,128)(2,1)S(1)}, bf16[896,128]{1,0:T(8,128)(2,1)S(1)}, u32[]{:S(2)}, u32[]{:S(2)}) collective-permute-start(bf16[896,128]{1,0:T(8,128)(2,1)S(1)} %fusion.2.piece.rest_0_), channel_id=1, source_target_pairs={{0,8},{4,12},{8,0},{12,4},{1,9},{5,13},{9,1},{13,5},{2,10},{6,14},... | collective-permute-start | bytes 688136 | tf_op jit(solution)/shard_map/ppermute | solution.py:323
  14.7 1.0 %collective-permute-done.8 = bf16[32,2688]{1,0:T(8,128)(2,1)S(1)} collective-permute-done((bf16[32,2688]{1,0:T(8,128)(2,1)S(1)}, bf16[32,2688]{1,0:T(8,128)(2,1)S(1)}, u32[]{:S(2)}, u32[]{:S(2)}) %collective-permute-start.8) | collective-permute-done | bytes 172064 | tf_op jit(solution)/shard_map/ppermute | solution.py:321
  15.6 0.9 %fusion.5.rest_3_ = bf16[32,2688]{1,0:T(8,128)(2,1)S(1)} fusion(bf16[32,2688]{1,0:T(8,128)(2,1)S(1)} %collective-permute-done.8, bf16[2,32,2688]{2,1,0:T(8,128)(2,1)} %collective-permute-done.7, bf16[2,32,2688]{2,1,0:T(8,128)(2,1)S(1)} %get-tuple-element.19), kind=kLoop, calls=%fused_computation.11 | loop fusion | flops 172032 | bytes 688128 | tf_op jit(solution)/shard_map/add | solution.py:325
  16.6 0.0 copy-start.4
  16.6 2.0 %collective-permute-start.10 = (bf16[32,2688]{1,0:T(8,128)(2,1)S(1)}, bf16[32,2688]{1,0:T(8,128)(2,1)S(1)}, u32[]{:S(2)}, u32[]{:S(2)}) collective-permute-start(bf16[32,2688]{1,0:T(8,128)(2,1)S(1)} %fusion.5.rest_3_), channel_id=1, source_target_pairs={{0,8},{4,12},{8,0},{12,4},{1,9},{5,13},{9,1},{13,5},{2,10},{6,14},... | collective-permute-start | bytes 516104 | tf_op jit(solution)/shard_map/ppermute | solution.py:78
  18.6 5.2 %collective-permute-done.features.rest_1_ = bf16[128,1664]{1,0:T(8,128)(2,1)S(1)} collective-permute-done((bf16[128,1664]{1,0:T(8,128)(2,1)S(1)}, bf16[128,1664]{1,0:T(8,128)(2,1)S(1)}, u32[]{:S(2)}, u32[]{:S(2)}) %collective-permute-start) | collective-permute-done | bytes 426016 | tf_op jit(solution)/shard_map/ppermute | solution.py:316
  23.8 0.2 shard_map.92
  24.0 0.1 collective-permute-start.3
  24.1 2.0 %collective-permute-start.9 = (bf16[32,2688]{1,0:T(8,128)(2,1)S(1)}, bf16[32,2688]{1,0:T(8,128)(2,1)S(1)}, u32[]{:S(2)}, u32[]{:S(2)}) collective-permute-start(bf16[32,2688]{1,0:T(8,128)(2,1)S(1)} %fusion.5.rest_3_), channel_id=1, source_target_pairs={{0,4},{4,0},{8,12},{12,8},{1,5},{5,1},{9,13},{13,9},{2,6},{6,2},{1... | collective-permute-start | bytes 516104 | tf_op jit(solution)/shard_map/ppermute | solution.py:78
  26.1 0.0 collective-permute-done.5.rest_2_
  26.1 7.1 %collective-permute-done.3.partial = f32[128,128]{1,0:T(8,128)S(1)} collective-permute-done((f32[128,128]{1,0:T(8,128)S(1)}, f32[128,128]{1,0:T(8,128)S(1)}, u32[]{:S(2)}, u32[]{:S(2)}) %collective-permute-start.3) | collective-permute-done | bytes 65568 | tf_op jit(solution)/shard_map/ppermute | solution.py:324
  33.1 0.0 collective-permute-done.4.rest_1_
  33.1 0.0 collective-permute-start.6
  33.1 0.0 collective-permute-done.10.rest_5_
  33.2 2.0 %collective-permute-start.11 = (bf16[32,2688]{1,0:T(8,128)(2,1)S(1)}, bf16[32,2688]{1,0:T(8,128)(2,1)S(1)}, u32[]{:S(2)}, u32[]{:S(2)}) collective-permute-start(bf16[32,2688]{1,0:T(8,128)(2,1)S(1)} %collective-permute-done.10.rest_5_), channel_id=1, source_target_pairs={{0,4},{4,0},{8,12},{12,8},{1,5},{5,1},{9,13},{13,9},{2,6},{6,2},{1... | collective-permute-start | bytes 516104 | tf_op jit(solution)/shard_map/ppermute | solution.py:330
  35.2 1.7 %collective-permute-done.9.rest_4_ = bf16[32,2688]{1,0:T(8,128)(2,1)S(1)} collective-permute-done((bf16[32,2688]{1,0:T(8,128)(2,1)S(1)}, bf16[32,2688]{1,0:T(8,128)(2,1)S(1)}, u32[]{:S(2)}, u32[]{:S(2)}) %collective-permute-start.9) | collective-permute-done | bytes 172064 | tf_op jit(solution)/shard_map/ppermute | solution.py:78
  36.8 1.9 %collective-permute-start.12 = (bf16[128,768]{1,0:T(8,128)(2,1)S(1)}, bf16[128,768]{1,0:T(8,128)(2,1)S(1)}, u32[]{:S(2)}, u32[]{:S(2)}) collective-permute-start(bf16[128,768]{1,0:T(8,128)(2,1)S(1)} %collective-permute-done.5.rest_2_), channel_id=1, source_target_pairs={{0,0},{4,4},{8,12},{12,8},{1,1},{5,5},{9,13},{13,9},{2,2},{6,6},{1... | collective-permute-start | bytes 589832 | tf_op jit(solution)/shard_map/ppermute | solution.py:332
  39.4 2.4 %collective-permute-done.6.rest_2_ = bf16[896,128]{1,0:T(8,128)(2,1)S(1)} collective-permute-done((bf16[896,128]{1,0:T(8,128)(2,1)S(1)}, bf16[896,128]{1,0:T(8,128)(2,1)S(1)}, u32[]{:S(2)}, u32[]{:S(2)}) %collective-permute-start.6) | collective-permute-done | bytes 229408 | tf_op jit(solution)/shard_map/ppermute | solution.py:328
  41.7 0.0 copy-done.2
  41.7 0.0 copy-done.3
  41.7 0.9 %shard_map.93.low = bf16[128,128]{1,0:T(8,128)(2,1)S(1)} custom-call(s32[4]{0:T(128)S(1)} %copy-done.2, s32[64]{0:T(128)S(1)} %copy-done.3, bf16[128,3584]{1,0:T(8,128)(2,1)S(1)} %bitcast.18, f32[128,128]{1,0:T(8,128)S(1)} %collective-permute-done.3.partial, bf16[896,128]{1,0:T(8,128)(2,1)S(1)} %fusion.2.piece.rest_0_, ...), custom_call_target="tpu_custom_call" | custom-call | flops 134217728 | bytes 4194304 | tf_op jit(solution)/shard_map/pallas_call | solution.py:111
  42.6 2.8 %collective-permute-done.11.rest_6_ = bf16[32,2688]{1,0:T(8,128)(2,1)S(1)} collective-permute-done((bf16[32,2688]{1,0:T(8,128)(2,1)S(1)}, bf16[32,2688]{1,0:T(8,128)(2,1)S(1)}, u32[]{:S(2)}, u32[]{:S(2)}) %collective-permute-start.11) | collective-permute-done | bytes 172064 | tf_op jit(solution)/shard_map/ppermute | solution.py:330
  45.4 0.0 copy-done.4
  45.4 2.0 %shard_map.94 = (bf16[128,2688]{1,0:T(8,128)(2,1)}, bf16[2688,128]{1,0:T(8,128)(2,1)S(1)}, f32[2688,128]{1,0:T(8,128)S(1)}, f32[2688,128]{1,0:T(8,128)S(1)}, f32[2688,128]{1,0:T(8,128)S(1)}) custom-call(s32[1]{0:T(128)S(6)} %copy.12.lengths, bf16[128,2688]{1,0:T(8,128)(2,1)S(1)} %bitcast.22, bf16[128,128]{1,0:T(8,128)(2,1)S(1)} %shard_map.93.low, ...), custom_call_target="tpu_custom_call" | custom-call | flops 1073741824 | bytes 4194304 | tf_op jit(solution)/shard_map/pallas_call | solution.py:228
  47.4 1.2 %collective-permute-done.12.kv = bf16[128,768]{1,0:T(8,128)(2,1)S(1)} collective-permute-done((bf16[128,768]{1,0:T(8,128)(2,1)S(1)}, bf16[128,768]{1,0:T(8,128)(2,1)S(1)}, u32[]{:S(2)}, u32[]{:S(2)}) %collective-permute-start.12) | collective-permute-done | bytes 196640 | tf_op jit(solution)/shard_map/ppermute | solution.py:332
  48.6 1.8 %shard_map.95 = bf16[128,2688]{1,0:T(8,128)(2,1)} custom-call(s32[1]{0:T(128)S(6)} %copy.12.lengths, bf16[128,2688]{1,0:T(8,128)(2,1)} %get-tuple-element.21.so_far, bf16[2688,128]{1,0:T(8,128)(2,1)S(1)} %get-tuple-element.22.queries, f32[2688,128]{1,0:T(8,128)S(1)} %get-tuple-element.23.sums, ...), custom_call_target="tpu_custom_call", output_to_operand_aliasing={{}: (1, {})} | custom-call | flops 268435456 | bytes 2097152 | tf_op jit(solution)/shard_map/pallas_call | solution.py:281
  (4 shorter events, 0.1 us)
Async XLA Ops:
  0.7 1.8 %copy-start.1 = (bf16[1,128,768]{2,1,0:T(8,128)(2,1)S(1)}, bf16[1,128,768]{2,1,0:T(8,128)(2,1)}, u32[]{:S(2)}) copy-start(bf16[1,128,768]{2,1,0:T(8,128)(2,1)} %param.11) | copy-start | bytes 589828
  0.7 2.1 %copy-start = (bf16[1,128,3584]{2,1,0:T(8,128)(2,1)S(1)}, bf16[1,128,3584]{2,1,0:T(8,128)(2,1)}, u32[]{:S(2)}) copy-start(bf16[1,128,3584]{2,1,0:T(8,128)(2,1)} %param.9) | copy-start | bytes 2752516
  1.6 2.4 %collective-permute-start.1 = (bf16[2,896,128]{2,1,0:T(8,128)(2,1)S(1)}, bf16[2,896,128]{2,1,0:T(8,128)(2,1)S(1)}, u32[]{:S(2)}, u32[]{:S(2)}) collective-permute-start(bf16[2,896,128]{2,1,0:T(8,128)(2,1)S(1)} %get-tuple-element.17), channel_id=1, source_target_pairs={{0,1},{1,0},{2,3},{3,2},{4,5},{5,4},{6,7},{7,6},{8,9},{9,8},{10,11... | collective-permute-start | bytes 1376264 | tf_op jit(solution)/shard_map/ppermute | solution.py:318
  2.5 23.6 %collective-permute-start.5 = (bf16[128,768]{1,0:T(8,128)(2,1)S(1)}, bf16[128,768]{1,0:T(8,128)(2,1)S(1)}, u32[]{:S(2)}, u32[]{:S(2)}) collective-permute-start(bf16[128,768]{1,0:T(8,128)(2,1)S(1)} %bitcast.19), channel_id=1, source_target_pairs={{0,8},{4,12},{8,0},{12,4},{1,9},{5,13},{9,1},{13,5},{2,10},{6,14},... | collective-permute-start | bytes 589832 | tf_op jit(solution)/shard_map/ppermute | solution.py:317
  2.9 2.7 %collective-permute-start.7 = (bf16[2,32,2688]{2,1,0:T(8,128)(2,1)S(1)}, bf16[2,32,2688]{2,1,0:T(8,128)(2,1)}, u32[]{:S(2)}, u32[]{:S(2)}) collective-permute-start(bf16[2,32,2688]{2,1,0:T(8,128)(2,1)S(1)} %get-tuple-element.20), channel_id=1, source_target_pairs={{0,1},{1,0},{2,3},{3,2},{4,5},{5,4},{6,7},{7,6},{8,9},{9,8},{10,11... | collective-permute-start | bytes 1032200 | tf_op jit(solution)/shard_map/ppermute | solution.py:319
  2.9 20.8 %collective-permute-start = (bf16[128,1664]{1,0:T(8,128)(2,1)S(1)}, bf16[128,1664]{1,0:T(8,128)(2,1)S(1)}, u32[]{:S(2)}, u32[]{:S(2)}) collective-permute-start(bf16[128,1664]{1,0:T(8,128)(2,1)S(1)} %pad_maximum_fusion), channel_id=1, source_target_pairs={{0,4},{4,0},{8,12},{12,8},{1,5},{5,1},{9,13},{13,9},{2,6},{6,2},{1... | collective-permute-start | bytes 1277960 | tf_op jit(solution)/shard_map/ppermute | solution.py:316
  4.0 8.5 %collective-permute-start.2 = (bf16[896,128]{1,0:T(8,128)(2,1)S(1)}, bf16[896,128]{1,0:T(8,128)(2,1)S(1)}, u32[]{:S(2)}, u32[]{:S(2)}) collective-permute-start(bf16[896,128]{1,0:T(8,128)(2,1)S(1)} %fusion), channel_id=1, source_target_pairs={{0,2},{1,3},{2,0},{3,1},{4,6},{5,7},{6,4},{7,5},{8,10},{9,11},{10,... | collective-permute-start | bytes 688136 | tf_op jit(solution)/shard_map/ppermute | solution.py:320
  5.6 36.2 %copy-start.2 = (s32[4]{0:T(128)S(1)}, s32[4]{0:T(128)}, u32[]{:S(2)}) copy-start(s32[4]{0:T(128)} %ids.1) | copy-start | bytes 52
  5.6 36.2 %copy-start.3 = (s32[64]{0:T(128)S(1)}, s32[64]{0:T(128)}, u32[]{:S(2)}) copy-start(s32[64]{0:T(128)} %ranks.1) | copy-start | bytes 772
  6.5 9.1 %collective-permute-start.8 = (bf16[32,2688]{1,0:T(8,128)(2,1)S(1)}, bf16[32,2688]{1,0:T(8,128)(2,1)S(1)}, u32[]{:S(2)}, u32[]{:S(2)}) collective-permute-start(bf16[32,2688]{1,0:T(8,128)(2,1)S(1)} %fusion.3), channel_id=1, source_target_pairs={{0,2},{1,3},{2,0},{3,1},{4,6},{5,7},{6,4},{7,5},{8,10},{9,11},{10,... | collective-permute-start | bytes 516104 | tf_op jit(solution)/shard_map/ppermute | solution.py:321
  12.5 20.6 %collective-permute-start.4 = (bf16[896,128]{1,0:T(8,128)(2,1)S(1)}, bf16[896,128]{1,0:T(8,128)(2,1)S(1)}, u32[]{:S(2)}, u32[]{:S(2)}) collective-permute-start(bf16[896,128]{1,0:T(8,128)(2,1)S(1)} %fusion.2.piece.rest_0_), channel_id=1, source_target_pairs={{0,8},{4,12},{8,0},{12,4},{1,9},{5,13},{9,1},{13,5},{2,10},{6,14},... | collective-permute-start | bytes 688136 | tf_op jit(solution)/shard_map/ppermute | solution.py:323
  16.6 28.9 %copy-start.4 = (bf16[1,128,2688]{2,1,0:T(8,128)(2,1)S(1)}, bf16[1,128,2688]{2,1,0:T(8,128)(2,1)}, u32[]{:S(2)}) copy-start(bf16[1,128,2688]{2,1,0:T(8,128)(2,1)} %param.10) | copy-start | bytes 2064388
  16.6 16.6 %collective-permute-start.10 = (bf16[32,2688]{1,0:T(8,128)(2,1)S(1)}, bf16[32,2688]{1,0:T(8,128)(2,1)S(1)}, u32[]{:S(2)}, u32[]{:S(2)}) collective-permute-start(bf16[32,2688]{1,0:T(8,128)(2,1)S(1)} %fusion.5.rest_3_), channel_id=1, source_target_pairs={{0,8},{4,12},{8,0},{12,4},{1,9},{5,13},{9,1},{13,5},{2,10},{6,14},... | collective-permute-start | bytes 516104 | tf_op jit(solution)/shard_map/ppermute | solution.py:78
  24.0 9.1 %collective-permute-start.3 = (f32[128,128]{1,0:T(8,128)S(1)}, f32[128,128]{1,0:T(8,128)S(1)}, u32[]{:S(2)}, u32[]{:S(2)}) collective-permute-start(f32[128,128]{1,0:T(8,128)S(1)} %shard_map.92), channel_id=1, source_target_pairs={{0,4},{4,0},{8,12},{12,8},{1,5},{5,1},{9,13},{13,9},{2,6},{6,2},{1... | collective-permute-start | bytes 196616 | tf_op jit(solution)/shard_map/ppermute | solution.py:324
  24.1 12.8 %collective-permute-start.9 = (bf16[32,2688]{1,0:T(8,128)(2,1)S(1)}, bf16[32,2688]{1,0:T(8,128)(2,1)S(1)}, u32[]{:S(2)}, u32[]{:S(2)}) collective-permute-start(bf16[32,2688]{1,0:T(8,128)(2,1)S(1)} %fusion.5.rest_3_), channel_id=1, source_target_pairs={{0,4},{4,0},{8,12},{12,8},{1,5},{5,1},{9,13},{13,9},{2,6},{6,2},{1... | collective-permute-start | bytes 516104 | tf_op jit(solution)/shard_map/ppermute | solution.py:78
  33.1 8.6 %collective-permute-start.6 = (bf16[896,128]{1,0:T(8,128)(2,1)S(1)}, bf16[896,128]{1,0:T(8,128)(2,1)S(1)}, u32[]{:S(2)}, u32[]{:S(2)}) collective-permute-start(bf16[896,128]{1,0:T(8,128)(2,1)S(1)} %collective-permute-done.4.rest_1_), channel_id=1, source_target_pairs={{0,4},{4,0},{8,12},{12,8},{1,5},{5,1},{9,13},{13,9},{2,6},{6,2},{1... | collective-permute-start | bytes 688136 | tf_op jit(solution)/shard_map/ppermute | solution.py:328
  33.2 12.3 %collective-permute-start.11 = (bf16[32,2688]{1,0:T(8,128)(2,1)S(1)}, bf16[32,2688]{1,0:T(8,128)(2,1)S(1)}, u32[]{:S(2)}, u32[]{:S(2)}) collective-permute-start(bf16[32,2688]{1,0:T(8,128)(2,1)S(1)} %collective-permute-done.10.rest_5_), channel_id=1, source_target_pairs={{0,4},{4,0},{8,12},{12,8},{1,5},{5,1},{9,13},{13,9},{2,6},{6,2},{1... | collective-permute-start | bytes 516104 | tf_op jit(solution)/shard_map/ppermute | solution.py:330
  36.8 11.8 %collective-permute-start.12 = (bf16[128,768]{1,0:T(8,128)(2,1)S(1)}, bf16[128,768]{1,0:T(8,128)(2,1)S(1)}, u32[]{:S(2)}, u32[]{:S(2)}) collective-permute-start(bf16[128,768]{1,0:T(8,128)(2,1)S(1)} %collective-permute-done.5.rest_2_), channel_id=1, source_target_pairs={{0,0},{4,4},{8,12},{12,8},{1,1},{5,5},{9,13},{13,9},{2,2},{6,6},{1... | collective-permute-start | bytes 589832 | tf_op jit(solution)/shard_map/ppermute | solution.py:332

commit v7 on v6

--- a/solution.py
+++ b/solution.py
@@ -17,7 +17,7 @@
 HBM = pltpu.HBM
 LOG2E = 1.0 / math.log(2.0)
 PARAMS = pltpu.CompilerParams(vmem_limit_bytes=32 * 1024 * 1024)
-WHOLE = pltpu.CompilerParams(vmem_limit_bytes=52 * 1024 * 1024)
+WHOLE = pltpu.CompilerParams(vmem_limit_bytes=50 * 1024 * 1024)
 
 
 def spec(space):
@@ -321,12 +321,13 @@
     far_up = lax.ppermute(keep_up[1] + near_up[1], "req", ACROSS)
     down = keep_down[0] + near_down[0] + far_down
     down_two = lax.ppermute(down, "ctx", TWO)
-    partial = lax.ppermute(product(kv_one, down), "ctx", ONE)
+    mine = product(kv_one, down)
+    partial = lax.ppermute(mine, "ctx", ONE)
     up = keep_up[0] + near_up[0] + far_up
     up_one, up_two = spread(up)
-    ready = lax.optimization_barrier((down_two, kv_two, partial))[0]
+    ready = lax.optimization_barrier((down_two, kv_two))[0]
     down_three = lax.ppermute(ready, "ctx", ONE)
-    ready = up_two
+    ready = lax.optimization_barrier((up_two, mine))[0]
     up_three = lax.ppermute(ready, "ctx", ONE)
     kv_last = lax.optimization_barrier((kv_two, up_two, up_one))[0]
     kv_three = lax.ppermute(kv_last, "ctx", LAST)

time: 50.6 us -> 51 us (level)
  the two profiles are of different devices: /device:TPU:28 before, /device:TPU:27 now
where the time goes in v7:
time: 51 us; the launch traced here: 50.6 us
  waiting for transfers between devices  26.7 us (52%)
  starting transfers between devices  14.6 us (29%)
  Pallas kernels  5.74 us (11%)
  other arithmetic  2.76 us (5%)
  between operations  0.77 us (2%)
    ppermute x1, waiting for transfers between devices, body(): partial = lax.ppermute(mine, 'ctx', ONE)  9.42 us
    ppermute x2, waiting for transfers between devices, spread(): return (lax.ppermute(shard, 'ctx', ONE), lax.ppermute(shard, 'ctx', TWO))  7.06 us
    ppermute x1, waiting for transfers between devices, body(): far_down = lax.ppermute(keep_down[1] + near_down[1], 'req', ACROSS)  4.31 us
    ppermute x1, starting transfers between devices, body(): kv_three = lax.ppermute(kv_last, 'ctx', LAST)  3.36 us
    ppermute x1, starting transfers between devices, body(): down_three = lax.ppermute(ready, 'ctx', ONE)  3.21 us
    ppermute x2, starting transfers between devices, spread(): return (lax.ppermute(shard, 'ctx', ONE), lax.ppermute(shard, 'ctx', TWO))  2.88 us
    ppermute x1, waiting for transfers between devices, body(): down_two = lax.ppermute(down, 'ctx', TWO)  2.57 us
    ppermute x1, waiting for transfers between devices, body(): far_up = lax.ppermute(keep_up[1] + near_up[1], 'req', ACROSS)  2.06 us
  transfers between devices with their start and end apart: 13, of which 7 were waited for; matrix products, arithmetic and copies ran while one was open for 4% of the time, Pallas kernels for 6%

profile of v7, /device:TPU:27, one launch (start us, length us, event | category | flops | bytes accessed | tf_op | source)
XLA Modules:
  0.0 50.6 jit_solution(2493736581891985281)
XLA Ops:
  0.0 0.7 %pad_add_fusion.table = s32[68]{0:T(128)S(1)} fusion(s32[64]{0:T(128)} %param.15, s32[4]{0:T(128)} %ids.1), kind=kLoop, calls=%fused_computation.12 | loop fusion | flops 68 | bytes 544 | tf_op jit(solution)/shard_map/concatenate | solution.py:67
  0.7 0.0 copy-start.1
  0.7 0.0 copy-start
  0.8 0.8 %shard_map.91 = (bf16[2,896,128]{2,1,0:T(8,128)(2,1)S(1)}, bf16[2,896,128]{2,1,0:T(8,128)(2,1)S(1)}, bf16[2,32,2688]{2,1,0:T(8,128)(2,1)S(1)}, bf16[2,32,2688]{2,1,0:T(8,128)(2,1)S(1)}) custom-call(s32[68]{0:T(128)S(1)} %pad_add_fusion.table, bf16[16,896,128]{2,1,0:T(8,128)(2,1)} %rest_0_.1, bf16[16,32,2688]{2,1,0:T(8,128)(2,1)} %rest_1_.1), custom_call_target="tpu_custom_call" | custom-call | tf_op jit(solution)/shard_map/pallas_call | solution.py:60
  1.6 1.8 %collective-permute-start.1 = (bf16[2,896,128]{2,1,0:T(8,128)(2,1)S(1)}, bf16[2,896,128]{2,1,0:T(8,128)(2,1)S(1)}, u32[]{:S(2)}, u32[]{:S(2)}) collective-permute-start(bf16[2,896,128]{2,1,0:T(8,128)(2,1)S(1)} %get-tuple-element.18), channel_id=1, source_target_pairs={{0,1},{1,0},{2,3},{3,2},{4,5},{5,4},{6,7},{7,6},{8,9},{9,8},{10,11... | collective-permute-start | bytes 1376264 | tf_op jit(solution)/shard_map/ppermute | solution.py:318
  3.4 0.0 copy-done.1
  3.4 0.1 collective-permute-start.5
  3.4 0.4 collective-permute-start.7
  3.8 0.0 copy-done
  3.9 0.2 collective-permute-start
  4.1 0.7 %collective-permute-done.1 = bf16[2,896,128]{2,1,0:T(8,128)(2,1)S(1)} collective-permute-done((bf16[2,896,128]{2,1,0:T(8,128)(2,1)S(1)}, bf16[2,896,128]{2,1,0:T(8,128)(2,1)S(1)}, u32[]{:S(2)}, u32[]{:S(2)}) %collective-permute-start.1) | collective-permute-done | bytes 458784 | tf_op jit(solution)/shard_map/ppermute | solution.py:318
  4.8 0.1 collective-permute-start.2
  4.9 0.5 %collective-permute-done.7 = bf16[2,32,2688]{2,1,0:T(8,128)(2,1)} collective-permute-done((bf16[2,32,2688]{2,1,0:T(8,128)(2,1)S(1)}, bf16[2,32,2688]{2,1,0:T(8,128)(2,1)}, u32[]{:S(2)}, u32[]{:S(2)}) %collective-permute-start.7) | collective-permute-done | bytes 344096 | tf_op jit(solution)/shard_map/ppermute | solution.py:319
  5.4 0.0 copy-start.2
  5.4 0.0 copy-start.3
  5.4 1.0 %fusion.3 = bf16[32,2688]{1,0:T(8,128)(2,1)S(1)} fusion(bf16[2,32,2688]{2,1,0:T(8,128)(2,1)} %collective-permute-done.7, bf16[2,32,2688]{2,1,0:T(8,128)(2,1)S(1)} %get-tuple-element.20), kind=kLoop, calls=%fused_computation.8 | loop fusion | flops 86016 | bytes 516096 | tf_op jit(solution)/shard_map/add | solution.py:321
  6.4 1.0 %collective-permute-start.8 = (bf16[32,2688]{1,0:T(8,128)(2,1)S(1)}, bf16[32,2688]{1,0:T(8,128)(2,1)S(1)}, u32[]{:S(2)}, u32[]{:S(2)}) collective-permute-start(bf16[32,2688]{1,0:T(8,128)(2,1)S(1)} %fusion.3), channel_id=1, source_target_pairs={{0,2},{1,3},{2,0},{3,1},{4,6},{5,7},{6,4},{7,5},{8,10},{9,11},{10,... | collective-permute-start | bytes 516104 | tf_op jit(solution)/shard_map/ppermute | solution.py:321
  7.4 4.3 %collective-permute-done.2 = bf16[896,128]{1,0:T(8,128)(2,1)S(1)} collective-permute-done((bf16[896,128]{1,0:T(8,128)(2,1)S(1)}, bf16[896,128]{1,0:T(8,128)(2,1)S(1)}, u32[]{:S(2)}, u32[]{:S(2)}) %collective-permute-start.2) | collective-permute-done | bytes 229408 | tf_op jit(solution)/shard_map/ppermute | solution.py:320
  11.8 1.6 %collective-permute-start.4 = (bf16[896,128]{1,0:T(8,128)(2,1)S(1)}, bf16[896,128]{1,0:T(8,128)(2,1)S(1)}, u32[]{:S(2)}, u32[]{:S(2)}) collective-permute-start(bf16[896,128]{1,0:T(8,128)(2,1)S(1)} %fusion.2.piece.rest_0_), channel_id=1, source_target_pairs={{0,8},{4,12},{8,0},{12,4},{1,9},{5,13},{9,1},{13,5},{2,10},{6,14},... | collective-permute-start | bytes 688136 | tf_op jit(solution)/shard_map/ppermute | solution.py:323
  13.3 2.1 %collective-permute-done.8 = bf16[32,2688]{1,0:T(8,128)(2,1)S(1)} collective-permute-done((bf16[32,2688]{1,0:T(8,128)(2,1)S(1)}, bf16[32,2688]{1,0:T(8,128)(2,1)S(1)}, u32[]{:S(2)}, u32[]{:S(2)}) %collective-permute-start.8) | collective-permute-done | bytes 172064 | tf_op jit(solution)/shard_map/ppermute | solution.py:321
  15.4 0.9 %fusion.5.rest_3_ = bf16[32,2688]{1,0:T(8,128)(2,1)S(1)} fusion(bf16[32,2688]{1,0:T(8,128)(2,1)S(1)} %collective-permute-done.8, bf16[2,32,2688]{2,1,0:T(8,128)(2,1)} %collective-permute-done.7, bf16[2,32,2688]{2,1,0:T(8,128)(2,1)S(1)} %get-tuple-element.20), kind=kLoop, calls=%fused_computation.11 | loop fusion | flops 172032 | bytes 688128 | tf_op jit(solution)/shard_map/add | solution.py:326
  16.4 0.0 copy-start.4
  16.4 1.6 %collective-permute-start.10 = (bf16[32,2688]{1,0:T(8,128)(2,1)S(1)}, bf16[32,2688]{1,0:T(8,128)(2,1)S(1)}, u32[]{:S(2)}, u32[]{:S(2)}) collective-permute-start(bf16[32,2688]{1,0:T(8,128)(2,1)S(1)} %fusion.5.rest_3_), channel_id=1, source_target_pairs={{0,8},{4,12},{8,0},{12,4},{1,9},{5,13},{9,1},{13,5},{2,10},{6,14},... | collective-permute-start | bytes 516104 | tf_op jit(solution)/shard_map/ppermute | solution.py:78
  18.0 1.3 %collective-permute-start.9 = (bf16[32,2688]{1,0:T(8,128)(2,1)S(1)}, bf16[32,2688]{1,0:T(8,128)(2,1)S(1)}, u32[]{:S(2)}, u32[]{:S(2)}) collective-permute-start(bf16[32,2688]{1,0:T(8,128)(2,1)S(1)} %fusion.5.rest_3_), channel_id=1, source_target_pairs={{0,4},{4,0},{8,12},{12,8},{1,5},{5,1},{9,13},{13,9},{2,6},{6,2},{1... | collective-permute-start | bytes 516104 | tf_op jit(solution)/shard_map/ppermute | solution.py:78
  19.2 0.0 collective-permute-done.5.rest_2_
  19.3 2.6 %collective-permute-done.4.rest_1_ = bf16[896,128]{1,0:T(8,128)(2,1)S(1)} collective-permute-done((bf16[896,128]{1,0:T(8,128)(2,1)S(1)}, bf16[896,128]{1,0:T(8,128)(2,1)S(1)}, u32[]{:S(2)}, u32[]{:S(2)}) %collective-permute-start.4) | collective-permute-done | bytes 229408 | tf_op jit(solution)/shard_map/ppermute | solution.py:323
  21.8 3.2 %collective-permute-start.6 = (bf16[896,128]{1,0:T(8,128)(2,1)S(1)}, bf16[896,128]{1,0:T(8,128)(2,1)S(1)}, u32[]{:S(2)}, u32[]{:S(2)}) collective-permute-start(bf16[896,128]{1,0:T(8,128)(2,1)S(1)} %collective-permute-done.4.rest_1_), channel_id=1, source_target_pairs={{0,4},{4,0},{8,12},{12,8},{1,5},{5,1},{9,13},{13,9},{2,6},{6,2},{1... | collective-permute-start | bytes 688136 | tf_op jit(solution)/shard_map/ppermute | solution.py:329
  25.0 0.0 collective-permute-done.features.rest_1_
  25.0 0.2 shard_map.92
  25.3 7.1 %collective-permute-done.10.rest_5_ = bf16[32,2688]{1,0:T(8,128)(2,1)S(1)} collective-permute-done((bf16[32,2688]{1,0:T(8,128)(2,1)S(1)}, bf16[32,2688]{1,0:T(8,128)(2,1)S(1)}, u32[]{:S(2)}, u32[]{:S(2)}) %collective-permute-start.10) | collective-permute-done | bytes 172064 | tf_op jit(solution)/shard_map/ppermute | solution.py:78
  32.3 0.0 collective-permute-start.11
  32.3 0.0 collective-permute-done.9.rest_4_
  32.3 3.4 %collective-permute-start.12 = (bf16[128,768]{1,0:T(8,128)(2,1)S(1)}, bf16[128,768]{1,0:T(8,128)(2,1)S(1)}, u32[]{:S(2)}, u32[]{:S(2)}) collective-permute-start(bf16[128,768]{1,0:T(8,128)(2,1)S(1)} %collective-permute-done.5.rest_2_), channel_id=1, source_target_pairs={{0,0},{4,4},{8,12},{12,8},{1,1},{5,5},{9,13},{13,9},{2,2},{6,6},{1... | collective-permute-start | bytes 589832 | tf_op jit(solution)/shard_map/ppermute | solution.py:333
  35.7 0.1 collective-permute-start.3
  36.4 9.4 %collective-permute-done.3.partial = f32[128,128]{1,0:T(8,128)S(1)} collective-permute-done((f32[128,128]{1,0:T(8,128)S(1)}, f32[128,128]{1,0:T(8,128)S(1)}, u32[]{:S(2)}, u32[]{:S(2)}) %collective-permute-start.3) | collective-permute-done | bytes 65568 | tf_op jit(solution)/shard_map/ppermute | solution.py:325
  45.8 0.0 collective-permute-done.6.rest_2_
  45.9 0.0 copy-done.2
  45.9 0.0 copy-done.3
  45.9 0.9 %shard_map.93.low = bf16[128,128]{1,0:T(8,128)(2,1)S(1)} custom-call(s32[4]{0:T(128)S(1)} %copy-done.2, s32[64]{0:T(128)S(1)} %copy-done.3, bf16[128,3584]{1,0:T(8,128)(2,1)S(1)} %bitcast.18, f32[128,128]{1,0:T(8,128)S(1)} %collective-permute-done.3.partial, bf16[896,128]{1,0:T(8,128)(2,1)S(1)} %fusion.2.piece.rest_0_, ...), custom_call_target="tpu_custom_call" | custom-call | flops 134217728 | bytes 4194304 | tf_op jit(solution)/shard_map/pallas_call | solution.py:111
  46.7 0.0 collective-permute-done.11.rest_6_
  46.8 0.0 copy-done.4
  46.8 2.0 %shard_map.94 = (bf16[128,2688]{1,0:T(8,128)(2,1)}, bf16[2688,128]{1,0:T(8,128)(2,1)S(1)}, f32[2688,128]{1,0:T(8,128)S(1)}, f32[2688,128]{1,0:T(8,128)S(1)}, f32[2688,128]{1,0:T(8,128)S(1)}) custom-call(s32[1]{0:T(128)S(6)} %copy.12.lengths, bf16[128,2688]{1,0:T(8,128)(2,1)S(1)} %bitcast.22, bf16[128,128]{1,0:T(8,128)(2,1)S(1)} %shard_map.93.low, ...), custom_call_target="tpu_custom_call" | custom-call | flops 1073741824 | bytes 4194304 | tf_op jit(solution)/shard_map/pallas_call | solution.py:228
  48.8 0.0 collective-permute-done.12.kv
  48.8 1.9 %shard_map.95 = bf16[128,2688]{1,0:T(8,128)(2,1)} custom-call(s32[1]{0:T(128)S(6)} %copy.12.lengths, bf16[128,2688]{1,0:T(8,128)(2,1)} %get-tuple-element.23.so_far, bf16[2688,128]{1,0:T(8,128)(2,1)S(1)} %get-tuple-element.24.queries, f32[2688,128]{1,0:T(8,128)S(1)} %get-tuple-element.25.sums, ...), custom_call_target="tpu_custom_call", output_to_operand_aliasing={{}: (1, {})} | custom-call | flops 268435456 | bytes 2097152 | tf_op jit(solution)/shard_map/pallas_call | solution.py:281
  (4 shorter events, 0.1 us)
Async XLA Ops:
  0.7 2.6 %copy-start.1 = (bf16[1,128,768]{2,1,0:T(8,128)(2,1)S(1)}, bf16[1,128,768]{2,1,0:T(8,128)(2,1)}, u32[]{:S(2)}) copy-start(bf16[1,128,768]{2,1,0:T(8,128)(2,1)} %param.11) | copy-start | bytes 589828
  0.7 3.0 %copy-start = (bf16[1,128,3584]{2,1,0:T(8,128)(2,1)S(1)}, bf16[1,128,3584]{2,1,0:T(8,128)(2,1)}, u32[]{:S(2)}) copy-start(bf16[1,128,3584]{2,1,0:T(8,128)(2,1)} %param.9) | copy-start | bytes 2752516
  1.6 3.2 %collective-permute-start.1 = (bf16[2,896,128]{2,1,0:T(8,128)(2,1)S(1)}, bf16[2,896,128]{2,1,0:T(8,128)(2,1)S(1)}, u32[]{:S(2)}, u32[]{:S(2)}) collective-permute-start(bf16[2,896,128]{2,1,0:T(8,128)(2,1)S(1)} %get-tuple-element.18), channel_id=1, source_target_pairs={{0,1},{1,0},{2,3},{3,2},{4,5},{5,4},{6,7},{7,6},{8,9},{9,8},{10,11... | collective-permute-start | bytes 1376264 | tf_op jit(solution)/shard_map/ppermute | solution.py:318
  3.4 15.9 %collective-permute-start.5 = (bf16[128,768]{1,0:T(8,128)(2,1)S(1)}, bf16[128,768]{1,0:T(8,128)(2,1)S(1)}, u32[]{:S(2)}, u32[]{:S(2)}) collective-permute-start(bf16[128,768]{1,0:T(8,128)(2,1)S(1)} %bitcast.19), channel_id=1, source_target_pairs={{0,8},{4,12},{8,0},{12,4},{1,9},{5,13},{9,1},{13,5},{2,10},{6,14},... | collective-permute-start | bytes 589832 | tf_op jit(solution)/shard_map/ppermute | solution.py:317
  3.4 2.0 %collective-permute-start.7 = (bf16[2,32,2688]{2,1,0:T(8,128)(2,1)S(1)}, bf16[2,32,2688]{2,1,0:T(8,128)(2,1)}, u32[]{:S(2)}, u32[]{:S(2)}) collective-permute-start(bf16[2,32,2688]{2,1,0:T(8,128)(2,1)S(1)} %get-tuple-element.21), channel_id=1, source_target_pairs={{0,1},{1,0},{2,3},{3,2},{4,5},{5,4},{6,7},{7,6},{8,9},{9,8},{10,11... | collective-permute-start | bytes 1032200 | tf_op jit(solution)/shard_map/ppermute | solution.py:319
  3.9 21.2 %collective-permute-start = (bf16[128,1664]{1,0:T(8,128)(2,1)S(1)}, bf16[128,1664]{1,0:T(8,128)(2,1)S(1)}, u32[]{:S(2)}, u32[]{:S(2)}) collective-permute-start(bf16[128,1664]{1,0:T(8,128)(2,1)S(1)} %pad_maximum_fusion), channel_id=1, source_target_pairs={{0,4},{4,0},{8,12},{12,8},{1,5},{5,1},{9,13},{13,9},{2,6},{6,2},{1... | collective-permute-start | bytes 1277960 | tf_op jit(solution)/shard_map/ppermute | solution.py:316
  4.8 6.9 %collective-permute-start.2 = (bf16[896,128]{1,0:T(8,128)(2,1)S(1)}, bf16[896,128]{1,0:T(8,128)(2,1)S(1)}, u32[]{:S(2)}, u32[]{:S(2)}) collective-permute-start(bf16[896,128]{1,0:T(8,128)(2,1)S(1)} %fusion), channel_id=1, source_target_pairs={{0,2},{1,3},{2,0},{3,1},{4,6},{5,7},{6,4},{7,5},{8,10},{9,11},{10,... | collective-permute-start | bytes 688136 | tf_op jit(solution)/shard_map/ppermute | solution.py:320
  5.4 40.4 %copy-start.2 = (s32[4]{0:T(128)S(1)}, s32[4]{0:T(128)}, u32[]{:S(2)}) copy-start(s32[4]{0:T(128)} %ids.1) | copy-start | bytes 52
  5.4 40.4 %copy-start.3 = (s32[64]{0:T(128)S(1)}, s32[64]{0:T(128)}, u32[]{:S(2)}) copy-start(s32[64]{0:T(128)} %ranks.1) | copy-start | bytes 772
  6.4 9.0 %collective-permute-start.8 = (bf16[32,2688]{1,0:T(8,128)(2,1)S(1)}, bf16[32,2688]{1,0:T(8,128)(2,1)S(1)}, u32[]{:S(2)}, u32[]{:S(2)}) collective-permute-start(bf16[32,2688]{1,0:T(8,128)(2,1)S(1)} %fusion.3), channel_id=1, source_target_pairs={{0,2},{1,3},{2,0},{3,1},{4,6},{5,7},{6,4},{7,5},{8,10},{9,11},{10,... | collective-permute-start | bytes 516104 | tf_op jit(solution)/shard_map/ppermute | solution.py:321
  11.8 10.1 %collective-permute-start.4 = (bf16[896,128]{1,0:T(8,128)(2,1)S(1)}, bf16[896,128]{1,0:T(8,128)(2,1)S(1)}, u32[]{:S(2)}, u32[]{:S(2)}) collective-permute-start(bf16[896,128]{1,0:T(8,128)(2,1)S(1)} %fusion.2.piece.rest_0_), channel_id=1, source_target_pairs={{0,8},{4,12},{8,0},{12,4},{1,9},{5,13},{9,1},{13,5},{2,10},{6,14},... | collective-permute-start | bytes 688136 | tf_op jit(solution)/shard_map/ppermute | solution.py:323
  16.4 30.4 %copy-start.4 = (bf16[1,128,2688]{2,1,0:T(8,128)(2,1)S(1)}, bf16[1,128,2688]{2,1,0:T(8,128)(2,1)}, u32[]{:S(2)}) copy-start(bf16[1,128,2688]{2,1,0:T(8,128)(2,1)} %param.10) | copy-start | bytes 2064388
  16.4 16.0 %collective-permute-start.10 = (bf16[32,2688]{1,0:T(8,128)(2,1)S(1)}, bf16[32,2688]{1,0:T(8,128)(2,1)S(1)}, u32[]{:S(2)}, u32[]{:S(2)}) collective-permute-start(bf16[32,2688]{1,0:T(8,128)(2,1)S(1)} %fusion.5.rest_3_), channel_id=1, source_target_pairs={{0,8},{4,12},{8,0},{12,4},{1,9},{5,13},{9,1},{13,5},{2,10},{6,14},... | collective-permute-start | bytes 516104 | tf_op jit(solution)/shard_map/ppermute | solution.py:78
  18.0 14.4 %collective-permute-start.9 = (bf16[32,2688]{1,0:T(8,128)(2,1)S(1)}, bf16[32,2688]{1,0:T(8,128)(2,1)S(1)}, u32[]{:S(2)}, u32[]{:S(2)}) collective-permute-start(bf16[32,2688]{1,0:T(8,128)(2,1)S(1)} %fusion.5.rest_3_), channel_id=1, source_target_pairs={{0,4},{4,0},{8,12},{12,8},{1,5},{5,1},{9,13},{13,9},{2,6},{6,2},{1... | collective-permute-start | bytes 516104 | tf_op jit(solution)/shard_map/ppermute | solution.py:78
  21.8 24.0 %collective-permute-start.6 = (bf16[896,128]{1,0:T(8,128)(2,1)S(1)}, bf16[896,128]{1,0:T(8,128)(2,1)S(1)}, u32[]{:S(2)}, u32[]{:S(2)}) collective-permute-start(bf16[896,128]{1,0:T(8,128)(2,1)S(1)} %collective-permute-done.4.rest_1_), channel_id=1, source_target_pairs={{0,4},{4,0},{8,12},{12,8},{1,5},{5,1},{9,13},{13,9},{2,6},{6,2},{1... | collective-permute-start | bytes 688136 | tf_op jit(solution)/shard_map/ppermute | solution.py:329
  32.3 14.4 %collective-permute-start.11 = (bf16[32,2688]{1,0:T(8,128)(2,1)S(1)}, bf16[32,2688]{1,0:T(8,128)(2,1)S(1)}, u32[]{:S(2)}, u32[]{:S(2)}) collective-permute-start(bf16[32,2688]{1,0:T(8,128)(2,1)S(1)} %collective-permute-done.10.rest_5_), channel_id=1, source_target_pairs={{0,4},{4,0},{8,12},{12,8},{1,5},{5,1},{9,13},{13,9},{2,6},{6,2},{1... | collective-permute-start | bytes 516104 | tf_op jit(solution)/shard_map/ppermute | solution.py:331
  32.3 16.4 %collective-permute-start.12 = (bf16[128,768]{1,0:T(8,128)(2,1)S(1)}, bf16[128,768]{1,0:T(8,128)(2,1)S(1)}, u32[]{:S(2)}, u32[]{:S(2)}) collective-permute-start(bf16[128,768]{1,0:T(8,128)(2,1)S(1)} %collective-permute-done.5.rest_2_), channel_id=1, source_target_pairs={{0,0},{4,4},{8,12},{12,8},{1,1},{5,5},{9,13},{13,9},{2,2},{6,6},{1... | collective-permute-start | bytes 589832 | tf_op jit(solution)/shard_map/ppermute | solution.py:333
  35.7 10.2 %collective-permute-start.3 = (f32[128,128]{1,0:T(8,128)S(1)}, f32[128,128]{1,0:T(8,128)S(1)}, u32[]{:S(2)}, u32[]{:S(2)}) collective-permute-start(f32[128,128]{1,0:T(8,128)S(1)} %shard_map.92), channel_id=1, source_target_pairs={{0,4},{4,0},{8,12},{12,8},{1,5},{5,1},{9,13},{13,9},{2,6},{6,2},{1... | collective-permute-start | bytes 196616 | tf_op jit(solution)/shard_map/ppermute | solution.py:325

commit v8 on v4

--- a/solution.py
+++ b/solution.py
@@ -229,7 +229,7 @@
     )(lengths, base, low, *kvs, *ups)
 
 
-def finish_kernel(lengths, so_far, queries, sums, highs, counts, kv, out, result, sems):
+def finish_kernel(lengths, so_far, queries, sums, highs, counts, kv, out, result, sems, *, heads):
     del so_far
     tokens = result.shape[1]
     z = lax.axis_index("ctx")
@@ -238,12 +238,10 @@
 
     @pl.when((z * tokens < lengths[0]) & (z >= 2))
     def _():
-        heads = [head_columns([kv], h) for h in range(KVH)]
-        all_scores = [
-            dot_keys(queries[h * block : (h + 1) * block, :], heads[h][0]) for h in range(KVH)
-        ]
-        for h in range(KVH):
-            scores, values = all_scores[h], heads[h][1]
+        for i, h in enumerate(heads):
+            keys = kv[:, i * HD : (i + 1) * HD]
+            values = kv[:, (len(heads) + i) * HD : (len(heads) + i + 1) * HD]
+            scores = dot_keys(queries[h * block : (h + 1) * block, :], keys)
             weights, factors, totals = [], [], []
             for g in range(GROUP):
                 at = slice(h * block + g * tokens, h * block + (g + 1) * tokens)
@@ -262,14 +260,14 @@
                 whole = sums[at, :] * factors[g] + product[g * tokens : (g + 1) * tokens, :]
                 result[h, :, g * HD : (g + 1) * HD] = (whole / totals[g]).astype(jnp.bfloat16)
             copies[h].start()
-        for copy in copies:
-            copy.wait()
-
-
-def finish(lengths, so_far, queries, sums, highs, counts, kv):
+        for h in heads:
+            copies[h].wait()
+
+
+def finish(lengths, so_far, queries, sums, highs, counts, kv, heads):
     tokens = so_far.shape[0]
     return pl.pallas_call(
-        finish_kernel,
+        functools.partial(finish_kernel, heads=heads),
         out_shape=jax.ShapeDtypeStruct(so_far.shape, so_far.dtype),
         in_specs=[spec(SMEM), spec(HBM)] + [spec(VMEM)] * 5,
         out_specs=spec(HBM),
@@ -283,6 +281,11 @@
             flops=1 << 28, bytes_accessed=1 << 21, transcendentals=1 << 19
         ),
     )(lengths, so_far, queries, sums, highs, counts, kv)
+
+
+def pick_heads(kv, heads):
+    columns = [h for h in heads] + [KVH + h for h in heads]
+    return jnp.concatenate([kv[:, c * HD : (c + 1) * HD] for c in columns], axis=1)
 
 
 def body(
@@ -314,13 +317,18 @@
     down_three = lax.ppermute(down_two, "ctx", ONE)
     up_two = lax.optimization_barrier((up_two, down_one))[0]
     up_three = lax.ppermute(up_two, "ctx", ONE)
-    kv_last = lax.optimization_barrier((kv_two, up_two, up_one))[0]
-    kv_three = lax.ppermute(kv_last, "ctx", LAST)
+    kv_last = lax.optimization_barrier((kv_two, down_one))[0]
+    kv_last = [pick_heads(kv_last, heads) for heads in ((0, 1), (2,))]
+    kv_last = lax.optimization_barrier((*kv_last, up_two, up_one))[:2]
+    kv_three = [lax.ppermute(part, "ctx", LAST) for part in kv_last]
     downs = [down, down_one, down_two, down_three]
     ups = [up, up_one, up_two, up_three]
     low = low_rank(adapter_ids, rank_buckets, hidden_states[0], downs)
     parts = attend(lengths, queries_base[0], low, [kv, kv_one, kv_two], ups)
-    return finish(lengths, *parts, kv_three)[None]
+    output, *state = parts
+    for part, heads in zip(kv_three, ((0, 1), (2,))):
+        output = finish(lengths, output, *state, part, heads)
+    return output[None]
 
 
 def plain_body(

time: 47.7 us -> 49.5 us (1.038); the launches traced: 46.8 us -> 49.4 us
  starting transfers between devices: 17.4 us -> 21.5 us
  waiting for transfers between devices: 21.3 us -> 20 us
    ppermute x1 -> x2, starting transfers between devices: 2.87 us -> 5.83 us  [body(): kv_three = [lax.ppermute(part, 'ctx', LAST) for part in kv_last]]
    ppermute x1, waiting for transfers between devices: 2.7 us -> 1.12 us  [body(): up_three = lax.ppermute(up_two, 'ctx', ONE)]
    ppermute x6, waiting for transfers between devices: 10.7 us -> 12 us  [spread(): return (lax.ppermute(shard, 'ctx', ONE), lax.ppermute(shard, 'ctx', TWO))]
    ppermute x1, waiting for transfers between devices: 1.07 us -> 0.01 us  [body(): down_three = lax.ppermute(down_two, 'ctx', ONE)]
    pallas_call x1, Pallas kernels: 1.86 us -> 0.81 us  [select(): pl.pallas_call(functools.partial(select_kernel, requests=ids.shape[0]), o...]
    ppermute x1, starting transfers between devices: 0.07 us -> 0.95 us  [body(): near_down = lax.ppermute(give_down, 'req', SIBLING)]
    pallas_call x1 -> x2, Pallas kernels: 2.02 us -> 2.74 us  [finish(): pl.pallas_call(functools.partial(finish_kernel, heads=heads), out_shape=j...]
    ppermute x1, starting transfers between devices: 1.75 us -> 1.16 us  [body(): far_up = lax.ppermute(keep_up[1] + near_up[1], 'req', ACROSS)]
  transfers between devices with their start and end apart: 13 -> 14, of which waited for: 7 -> 7; matrix products, arithmetic and copies ran while one was open for 0% -> 0% of each run, Pallas kernels for 6% -> 9%
where the time goes in v8:
time: 49.5 us; the launch traced here: 49.4 us
  starting transfers between devices  21.5 us (43%)
  waiting for transfers between devices  20 us (40%)
  Pallas kernels  6.23 us (13%)
  other arithmetic  0.91 us (2%)
  between operations  0.8 us (2%)
    ppermute x6, waiting for transfers between devices, spread(): return (lax.ppermute(shard, 'ctx', ONE), lax.ppermute(shard, 'ctx', TWO))  12 us
    ppermute x6, starting transfers between devices, spread(): return (lax.ppermute(shard, 'ctx', ONE), lax.ppermute(shard, 'ctx', TWO))  6.93 us
    ppermute x1, waiting for transfers between devices, body(): far_down = lax.ppermute(keep_down[1] + near_down[1], 'req', ACROSS)  6.35 us
    ppermute x2, starting transfers between devices, body(): kv_three = [lax.ppermute(part, 'ctx', LAST) for part in kv_last]  5.83 us
    ppermute x1, starting transfers between devices, body(): up_three = lax.ppermute(up_two, 'ctx', ONE)  2.84 us
    pallas_call x2, Pallas kernels, finish(): pl.pallas_call(functools.partial(finish_kernel, heads=heads), out_shape=j...  2.74 us
    ppermute x1, starting transfers between devices, body(): down_three = lax.ppermute(down_two, 'ctx', ONE)  2.72 us
    pallas_call x1, Pallas kernels, attend(): pl.pallas_call(attend_kernel, out_shape=shapes, in_specs=[spec(SMEM)] + [...  1.74 us
  transfers between devices with their start and end apart: 14, of which 7 were waited for; matrix products, arithmetic and copies ran while one was open for 0% of the time, Pallas kernels for 9%

profile of v8, /device:TPU:18, one launch (start us, length us, event | category | flops | bytes accessed | tf_op | source)
XLA Modules:
  0.0 49.4 jit_solution(6142135488627266138)
XLA Ops:
  0.0 0.7 %pad_add_fusion.table = s32[68]{0:T(128)S(1)} fusion(s32[64]{0:T(128)} %param.15, s32[4]{0:T(128)} %ids.1), kind=kLoop, calls=%fused_computation.12 | loop fusion | flops 68 | bytes 544 | tf_op jit(solution)/shard_map/concatenate | solution.py:67
  0.7 0.0 copy-start.4
  0.7 0.8 %shard_map.91 = (bf16[2,896,128]{2,1,0:T(8,128)(2,1)S(1)}, bf16[2,896,128]{2,1,0:T(8,128)(2,1)S(1)}, bf16[2,32,2688]{2,1,0:T(8,128)(2,1)S(1)}, bf16[2,32,2688]{2,1,0:T(8,128)(2,1)S(1)}) custom-call(s32[68]{0:T(128)S(1)} %pad_add_fusion.table, bf16[16,896,128]{2,1,0:T(8,128)(2,1)} %rest_0_.1, bf16[16,32,2688]{2,1,0:T(8,128)(2,1)} %rest_1_.1), custom_call_target="tpu_custom_call" | custom-call | tf_op jit(solution)/shard_map/pallas_call | solution.py:60
  1.6 1.0 %collective-permute-start = (bf16[2,896,128]{2,1,0:T(8,128)(2,1)S(1)}, bf16[2,896,128]{2,1,0:T(8,128)(2,1)S(1)}, u32[]{:S(2)}, u32[]{:S(2)}) collective-permute-start(bf16[2,896,128]{2,1,0:T(8,128)(2,1)S(1)} %get-tuple-element.22), channel_id=1, source_target_pairs={{0,1},{1,0},{2,3},{3,2},{4,5},{5,4},{6,7},{7,6},{8,9},{9,8},{10,11... | collective-permute-start | bytes 1376264 | tf_op jit(solution)/shard_map/ppermute | solution.py:307
  2.5 0.1 collective-permute-start.7
  2.6 0.0 copy-done.4
  2.6 0.3 collective-permute-start.5
  2.9 1.6 %collective-permute-start.2 = (bf16[128,768]{1,0:T(8,128)(2,1)S(1)}, bf16[128,768]{1,0:T(8,128)(2,1)S(1)}, u32[]{:S(2)}, u32[]{:S(2)}) collective-permute-start(bf16[128,768]{1,0:T(8,128)(2,1)S(1)} %bitcast.19), channel_id=1, source_target_pairs={{0,4},{4,0},{8,12},{12,8},{1,5},{5,1},{9,13},{13,9},{2,6},{6,2},{1... | collective-permute-start | bytes 589832 | tf_op jit(solution)/shard_map/ppermute | solution.py:78
  4.5 0.0 collective-permute-done
  4.6 1.0 %collective-permute-start.1 = (bf16[896,128]{1,0:T(8,128)(2,1)S(1)}, bf16[896,128]{1,0:T(8,128)(2,1)S(1)}, u32[]{:S(2)}, u32[]{:S(2)}) collective-permute-start(bf16[896,128]{1,0:T(8,128)(2,1)S(1)} %fusion), channel_id=1, source_target_pairs={{0,2},{1,3},{2,0},{3,1},{4,6},{5,7},{6,4},{7,5},{8,10},{9,11},{10,... | collective-permute-start | bytes 688136 | tf_op jit(solution)/shard_map/ppermute | solution.py:309
  5.5 0.0 collective-permute-done.7
  5.6 0.0 copy-start
  5.6 0.0 copy-start.1
  5.6 0.0 copy-start.2
  5.6 1.2 %collective-permute-start.8 = (bf16[32,2688]{1,0:T(8,128)(2,1)S(1)}, bf16[32,2688]{1,0:T(8,128)(2,1)S(1)}, u32[]{:S(2)}, u32[]{:S(2)}) collective-permute-start(bf16[32,2688]{1,0:T(8,128)(2,1)S(1)} %fusion.3), channel_id=1, source_target_pairs={{0,2},{1,3},{2,0},{3,1},{4,6},{5,7},{6,4},{7,5},{8,10},{9,11},{10,... | collective-permute-start | bytes 516104 | tf_op jit(solution)/shard_map/ppermute | solution.py:310
  6.8 6.3 %collective-permute-done.1 = bf16[896,128]{1,0:T(8,128)(2,1)S(1)} collective-permute-done((bf16[896,128]{1,0:T(8,128)(2,1)S(1)}, bf16[896,128]{1,0:T(8,128)(2,1)S(1)}, u32[]{:S(2)}, u32[]{:S(2)}) %collective-permute-start.1) | collective-permute-done | bytes 229408 | tf_op jit(solution)/shard_map/ppermute | solution.py:309
  13.1 0.8 %collective-permute-done.2.rest_1_ = bf16[128,768]{1,0:T(8,128)(2,1)S(1)} collective-permute-done((bf16[128,768]{1,0:T(8,128)(2,1)S(1)}, bf16[128,768]{1,0:T(8,128)(2,1)S(1)}, u32[]{:S(2)}, u32[]{:S(2)}) %collective-permute-start.2) | collective-permute-done | bytes 196640 | tf_op jit(solution)/shard_map/ppermute | solution.py:78
  14.0 1.8 %collective-permute-start.4 = (bf16[896,128]{1,0:T(8,128)(2,1)S(1)}, bf16[896,128]{1,0:T(8,128)(2,1)S(1)}, u32[]{:S(2)}, u32[]{:S(2)}) collective-permute-start(bf16[896,128]{1,0:T(8,128)(2,1)S(1)} %fusion.2.rest_0_), channel_id=1, source_target_pairs={{0,8},{4,12},{8,0},{12,4},{1,9},{5,13},{9,1},{13,5},{2,10},{6,14},... | collective-permute-start | bytes 688136 | tf_op jit(solution)/shard_map/ppermute | solution.py:78
  15.8 1.2 %collective-permute-start.3 = (bf16[896,128]{1,0:T(8,128)(2,1)S(1)}, bf16[896,128]{1,0:T(8,128)(2,1)S(1)}, u32[]{:S(2)}, u32[]{:S(2)}) collective-permute-start(bf16[896,128]{1,0:T(8,128)(2,1)S(1)} %fusion.2.rest_0_), channel_id=1, source_target_pairs={{0,4},{4,0},{8,12},{12,8},{1,5},{5,1},{9,13},{13,9},{2,6},{6,2},{1... | collective-permute-start | bytes 688136 | tf_op jit(solution)/shard_map/ppermute | solution.py:78
  17.0 0.0 collective-permute-done.8
  17.1 0.0 copy-start.3
  17.1 1.3 %collective-permute-start.10 = (bf16[32,2688]{1,0:T(8,128)(2,1)S(1)}, bf16[32,2688]{1,0:T(8,128)(2,1)S(1)}, u32[]{:S(2)}, u32[]{:S(2)}) collective-permute-start(bf16[32,2688]{1,0:T(8,128)(2,1)S(1)} %fusion.5.rest_3_), channel_id=1, source_target_pairs={{0,8},{4,12},{8,0},{12,4},{1,9},{5,13},{9,1},{13,5},{2,10},{6,14},... | collective-permute-start | bytes 516104 | tf_op jit(solution)/shard_map/ppermute | solution.py:78
  18.4 0.7 %collective-permute-start.9 = (bf16[32,2688]{1,0:T(8,128)(2,1)S(1)}, bf16[32,2688]{1,0:T(8,128)(2,1)S(1)}, u32[]{:S(2)}, u32[]{:S(2)}) collective-permute-start(bf16[32,2688]{1,0:T(8,128)(2,1)S(1)} %fusion.5.rest_3_), channel_id=1, source_target_pairs={{0,4},{4,0},{8,12},{12,8},{1,5},{5,1},{9,13},{13,9},{2,6},{6,2},{1... | collective-permute-start | bytes 516104 | tf_op jit(solution)/shard_map/ppermute | solution.py:78
  19.1 0.0 collective-permute-done.5.rest_2_
  19.1 8.1 %collective-permute-done.4.rest_2_ = bf16[896,128]{1,0:T(8,128)(2,1)S(1)} collective-permute-done((bf16[896,128]{1,0:T(8,128)(2,1)S(1)}, bf16[896,128]{1,0:T(8,128)(2,1)S(1)}, u32[]{:S(2)}, u32[]{:S(2)}) %collective-permute-start.4) | collective-permute-done | bytes 229408 | tf_op jit(solution)/shard_map/ppermute | solution.py:78
  27.1 2.7 %collective-permute-start.6 = (bf16[896,128]{1,0:T(8,128)(2,1)S(1)}, bf16[896,128]{1,0:T(8,128)(2,1)S(1)}, u32[]{:S(2)}, u32[]{:S(2)}) collective-permute-start(bf16[896,128]{1,0:T(8,128)(2,1)S(1)} %collective-permute-done.4.rest_2_), channel_id=1, source_target_pairs={{0,4},{4,0},{8,12},{12,8},{1,5},{5,1},{9,13},{13,9},{2,6},{6,2},{1... | collective-permute-start | bytes 688136 | tf_op jit(solution)/shard_map/ppermute | solution.py:317
  29.8 0.0 collective-permute-done.3.rest_1_
  29.9 2.2 %collective-permute-done.10.rest_5_ = bf16[32,2688]{1,0:T(8,128)(2,1)S(1)} collective-permute-done((bf16[32,2688]{1,0:T(8,128)(2,1)S(1)}, bf16[32,2688]{1,0:T(8,128)(2,1)S(1)}, u32[]{:S(2)}, u32[]{:S(2)}) %collective-permute-start.10) | collective-permute-done | bytes 172064 | tf_op jit(solution)/shard_map/ppermute | solution.py:78
  32.1 2.8 %collective-permute-start.11 = (bf16[32,2688]{1,0:T(8,128)(2,1)S(1)}, bf16[32,2688]{1,0:T(8,128)(2,1)S(1)}, u32[]{:S(2)}, u32[]{:S(2)}) collective-permute-start(bf16[32,2688]{1,0:T(8,128)(2,1)S(1)} %collective-permute-done.10.rest_5_), channel_id=1, source_target_pairs={{0,4},{4,0},{8,12},{12,8},{1,5},{5,1},{9,13},{13,9},{2,6},{6,2},{1... | collective-permute-start | bytes 516104 | tf_op jit(solution)/shard_map/ppermute | solution.py:319
  34.9 0.9 %collective-permute-done.9.rest_4_ = bf16[32,2688]{1,0:T(8,128)(2,1)S(1)} collective-permute-done((bf16[32,2688]{1,0:T(8,128)(2,1)S(1)}, bf16[32,2688]{1,0:T(8,128)(2,1)S(1)}, u32[]{:S(2)}, u32[]{:S(2)}) %collective-permute-start.9) | collective-permute-done | bytes 172064 | tf_op jit(solution)/shard_map/ppermute | solution.py:78
  35.9 2.7 %collective-permute-start.12 = (bf16[128,512]{1,0:T(8,128)(2,1)S(1)}, bf16[128,512]{1,0:T(8,128)(2,1)S(1)}, u32[]{:S(2)}, u32[]{:S(2)}) collective-permute-start(bf16[128,512]{1,0:T(8,128)(2,1)S(1)} %pad_maximum_fusion), channel_id=1, source_target_pairs={{0,0},{4,4},{8,12},{12,8},{1,1},{5,5},{9,13},{13,9},{2,2},{6,6},{1... | collective-permute-start | bytes 393224 | tf_op jit(solution)/shard_map/ppermute | solution.py:323
  39.2 3.1 %collective-permute-start.13 = (bf16[128,256]{1,0:T(8,128)(2,1)S(1)}, bf16[128,256]{1,0:T(8,128)(2,1)S(1)}, u32[]{:S(2)}, u32[]{:S(2)}) collective-permute-start(bf16[128,256]{1,0:T(8,128)(2,1)S(1)} %pad_maximum_fusion.1), channel_id=1, source_target_pairs={{0,0},{4,4},{8,12},{12,8},{1,1},{5,5},{9,13},{13,9},{2,2},{6,6},{1... | collective-permute-start | bytes 196616 | tf_op jit(solution)/shard_map/ppermute | solution.py:323
  42.3 0.0 collective-permute-done.6.rest_3_
  42.4 0.0 copy-done
  42.4 0.0 copy-done.1
  42.4 0.0 copy-done.2
  42.4 0.9 %shard_map.92.low = bf16[128,128]{1,0:T(8,128)(2,1)S(1)} custom-call(s32[4]{0:T(128)S(1)} %copy-done.1, s32[64]{0:T(128)S(1)} %copy-done.2, bf16[128,3584]{1,0:T(8,128)(2,1)S(1)} %bitcast.16, bf16[896,128]{1,0:T(8,128)(2,1)S(1)} %fusion.2.rest_0_, bf16[896,128]{1,0:T(8,128)(2,1)S(1)} %collective-permute-done.3.rest_1_, ...), custom_call_target="tpu_custom_call" | custom-call | flops 134217728 | bytes 4194304 | tf_op jit(solution)/shard_map/pallas_call | solution.py:97
  43.3 1.1 %collective-permute-done.11.rest_6_ = bf16[32,2688]{1,0:T(8,128)(2,1)S(1)} collective-permute-done((bf16[32,2688]{1,0:T(8,128)(2,1)S(1)}, bf16[32,2688]{1,0:T(8,128)(2,1)S(1)}, u32[]{:S(2)}, u32[]{:S(2)}) %collective-permute-start.11) | collective-permute-done | bytes 172064 | tf_op jit(solution)/shard_map/ppermute | solution.py:319
  44.5 0.0 copy-done.3
  44.5 1.7 %shard_map.93 = (bf16[128,2688]{1,0:T(8,128)(2,1)}, bf16[2688,128]{1,0:T(8,128)(2,1)S(1)}, f32[2688,128]{1,0:T(8,128)S(1)}, f32[2688,128]{1,0:T(8,128)S(1)}, f32[2688,128]{1,0:T(8,128)S(1)}) custom-call(s32[1]{0:T(128)S(6)} %copy.14.lengths, bf16[128,2688]{1,0:T(8,128)(2,1)S(1)} %bitcast.17, bf16[128,128]{1,0:T(8,128)(2,1)S(1)} %shard_map.92.low, ...), custom_call_target="tpu_custom_call" | custom-call | flops 1073741824 | bytes 4194304 | tf_op jit(solution)/shard_map/pallas_call | solution.py:215
  46.2 0.5 collective-permute-done.12.kv
  46.7 1.5 %shard_map.94.so_far = bf16[128,2688]{1,0:T(8,128)(2,1)} custom-call(s32[1]{0:T(128)S(6)} %copy.14.lengths, bf16[128,2688]{1,0:T(8,128)(2,1)} %get-tuple-element.29.so_far, bf16[2688,128]{1,0:T(8,128)(2,1)S(1)} %get-tuple-element.30.queries, f32[2688,128]{1,0:T(8,128)S(1)} %get-tuple-element.31.sums, ...), custom_call_target="tpu_custom_call", output_to_operand_aliasing={{}: (1, {})} | custom-call | flops 268435456 | bytes 2097152 | tf_op jit(solution)/shard_map/pallas_call | solution.py:269
  48.2 0.0 collective-permute-done.13.kv
  48.2 1.2 %shard_map.95 = bf16[128,2688]{1,0:T(8,128)(2,1)} custom-call(s32[1]{0:T(128)S(6)} %copy.14.lengths, bf16[128,2688]{1,0:T(8,128)(2,1)} %shard_map.94.so_far, bf16[2688,128]{1,0:T(8,128)(2,1)S(1)} %get-tuple-element.30.queries, f32[2688,128]{1,0:T(8,128)S(1)} %get-tuple-element.31.sums, ...), custom_call_target="tpu_custom_call", output_to_operand_aliasing={{}: (1, {})} | custom-call | flops 268435456 | bytes 2097152 | tf_op jit(solution)/shard_map/pallas_call | solution.py:269
  (8 shorter events, 0.2 us)
Async XLA Ops:
  0.7 1.9 %copy-start.4 = (bf16[1,128,768]{2,1,0:T(8,128)(2,1)S(1)}, bf16[1,128,768]{2,1,0:T(8,128)(2,1)}, u32[]{:S(2)}) copy-start(bf16[1,128,768]{2,1,0:T(8,128)(2,1)} %param.11) | copy-start | bytes 589828
  1.6 3.0 %collective-permute-start = (bf16[2,896,128]{2,1,0:T(8,128)(2,1)S(1)}, bf16[2,896,128]{2,1,0:T(8,128)(2,1)S(1)}, u32[]{:S(2)}, u32[]{:S(2)}) collective-permute-start(bf16[2,896,128]{2,1,0:T(8,128)(2,1)S(1)} %get-tuple-element.22), channel_id=1, source_target_pairs={{0,1},{1,0},{2,3},{3,2},{4,5},{5,4},{6,7},{7,6},{8,9},{9,8},{10,11... | collective-permute-start | bytes 1376264 | tf_op jit(solution)/shard_map/ppermute | solution.py:307
  2.5 3.0 %collective-permute-start.7 = (bf16[2,32,2688]{2,1,0:T(8,128)(2,1)S(1)}, bf16[2,32,2688]{2,1,0:T(8,128)(2,1)S(1)}, u32[]{:S(2)}, u32[]{:S(2)}) collective-permute-start(bf16[2,32,2688]{2,1,0:T(8,128)(2,1)S(1)} %get-tuple-element.27), channel_id=1, source_target_pairs={{0,1},{1,0},{2,3},{3,2},{4,5},{5,4},{6,7},{7,6},{8,9},{9,8},{10,11... | collective-permute-start | bytes 1032200 | tf_op jit(solution)/shard_map/ppermute | solution.py:308
  2.6 16.5 %collective-permute-start.5 = (bf16[128,768]{1,0:T(8,128)(2,1)S(1)}, bf16[128,768]{1,0:T(8,128)(2,1)S(1)}, u32[]{:S(2)}, u32[]{:S(2)}) collective-permute-start(bf16[128,768]{1,0:T(8,128)(2,1)S(1)} %bitcast.18), channel_id=1, source_target_pairs={{0,8},{4,12},{8,0},{12,4},{1,9},{5,13},{9,1},{13,5},{2,10},{6,14},... | collective-permute-start | bytes 589832 | tf_op jit(solution)/shard_map/ppermute | solution.py:78
  2.9 11.1 %collective-permute-start.2 = (bf16[128,768]{1,0:T(8,128)(2,1)S(1)}, bf16[128,768]{1,0:T(8,128)(2,1)S(1)}, u32[]{:S(2)}, u32[]{:S(2)}) collective-permute-start(bf16[128,768]{1,0:T(8,128)(2,1)S(1)} %bitcast.19), channel_id=1, source_target_pairs={{0,4},{4,0},{8,12},{12,8},{1,5},{5,1},{9,13},{13,9},{2,6},{6,2},{1... | collective-permute-start | bytes 589832 | tf_op jit(solution)/shard_map/ppermute | solution.py:78
  4.6 8.6 %collective-permute-start.1 = (bf16[896,128]{1,0:T(8,128)(2,1)S(1)}, bf16[896,128]{1,0:T(8,128)(2,1)S(1)}, u32[]{:S(2)}, u32[]{:S(2)}) collective-permute-start(bf16[896,128]{1,0:T(8,128)(2,1)S(1)} %fusion), channel_id=1, source_target_pairs={{0,2},{1,3},{2,0},{3,1},{4,6},{5,7},{6,4},{7,5},{8,10},{9,11},{10,... | collective-permute-start | bytes 688136 | tf_op jit(solution)/shard_map/ppermute | solution.py:309
  5.6 36.8 %copy-start = (bf16[1,128,3584]{2,1,0:T(8,128)(2,1)S(1)}, bf16[1,128,3584]{2,1,0:T(8,128)(2,1)}, u32[]{:S(2)}) copy-start(bf16[1,128,3584]{2,1,0:T(8,128)(2,1)} %param.9) | copy-start | bytes 2752516
  5.6 36.8 %copy-start.1 = (s32[4]{0:T(128)S(1)}, s32[4]{0:T(128)}, u32[]{:S(2)}) copy-start(s32[4]{0:T(128)} %ids.1) | copy-start | bytes 52
  5.6 36.8 %copy-start.2 = (s32[64]{0:T(128)S(1)}, s32[64]{0:T(128)}, u32[]{:S(2)}) copy-start(s32[64]{0:T(128)} %ranks.1) | copy-start | bytes 772
  5.6 11.4 %collective-permute-start.8 = (bf16[32,2688]{1,0:T(8,128)(2,1)S(1)}, bf16[32,2688]{1,0:T(8,128)(2,1)S(1)}, u32[]{:S(2)}, u32[]{:S(2)}) collective-permute-start(bf16[32,2688]{1,0:T(8,128)(2,1)S(1)} %fusion.3), channel_id=1, source_target_pairs={{0,2},{1,3},{2,0},{3,1},{4,6},{5,7},{6,4},{7,5},{8,10},{9,11},{10,... | collective-permute-start | bytes 516104 | tf_op jit(solution)/shard_map/ppermute | solution.py:310
  14.0 13.1 %collective-permute-start.4 = (bf16[896,128]{1,0:T(8,128)(2,1)S(1)}, bf16[896,128]{1,0:T(8,128)(2,1)S(1)}, u32[]{:S(2)}, u32[]{:S(2)}) collective-permute-start(bf16[896,128]{1,0:T(8,128)(2,1)S(1)} %fusion.2.rest_0_), channel_id=1, source_target_pairs={{0,8},{4,12},{8,0},{12,4},{1,9},{5,13},{9,1},{13,5},{2,10},{6,14},... | collective-permute-start | bytes 688136 | tf_op jit(solution)/shard_map/ppermute | solution.py:78
  15.8 14.0 %collective-permute-start.3 = (bf16[896,128]{1,0:T(8,128)(2,1)S(1)}, bf16[896,128]{1,0:T(8,128)(2,1)S(1)}, u32[]{:S(2)}, u32[]{:S(2)}) collective-permute-start(bf16[896,128]{1,0:T(8,128)(2,1)S(1)} %fusion.2.rest_0_), channel_id=1, source_target_pairs={{0,4},{4,0},{8,12},{12,8},{1,5},{5,1},{9,13},{13,9},{2,6},{6,2},{1... | collective-permute-start | bytes 688136 | tf_op jit(solution)/shard_map/ppermute | solution.py:78
  17.1 27.4 %copy-start.3 = (bf16[1,128,2688]{2,1,0:T(8,128)(2,1)S(1)}, bf16[1,128,2688]{2,1,0:T(8,128)(2,1)}, u32[]{:S(2)}) copy-start(bf16[1,128,2688]{2,1,0:T(8,128)(2,1)} %param.10) | copy-start | bytes 2064388
  17.1 15.0 %collective-permute-start.10 = (bf16[32,2688]{1,0:T(8,128)(2,1)S(1)}, bf16[32,2688]{1,0:T(8,128)(2,1)S(1)}, u32[]{:S(2)}, u32[]{:S(2)}) collective-permute-start(bf16[32,2688]{1,0:T(8,128)(2,1)S(1)} %fusion.5.rest_3_), channel_id=1, source_target_pairs={{0,8},{4,12},{8,0},{12,4},{1,9},{5,13},{9,1},{13,5},{2,10},{6,14},... | collective-permute-start | bytes 516104 | tf_op jit(solution)/shard_map/ppermute | solution.py:78
  18.4 17.5 %collective-permute-start.9 = (bf16[32,2688]{1,0:T(8,128)(2,1)S(1)}, bf16[32,2688]{1,0:T(8,128)(2,1)S(1)}, u32[]{:S(2)}, u32[]{:S(2)}) collective-permute-start(bf16[32,2688]{1,0:T(8,128)(2,1)S(1)} %fusion.5.rest_3_), channel_id=1, source_target_pairs={{0,4},{4,0},{8,12},{12,8},{1,5},{5,1},{9,13},{13,9},{2,6},{6,2},{1... | collective-permute-start | bytes 516104 | tf_op jit(solution)/shard_map/ppermute | solution.py:78
  27.1 15.2 %collective-permute-start.6 = (bf16[896,128]{1,0:T(8,128)(2,1)S(1)}, bf16[896,128]{1,0:T(8,128)(2,1)S(1)}, u32[]{:S(2)}, u32[]{:S(2)}) collective-permute-start(bf16[896,128]{1,0:T(8,128)(2,1)S(1)} %collective-permute-done.4.rest_2_), channel_id=1, source_target_pairs={{0,4},{4,0},{8,12},{12,8},{1,5},{5,1},{9,13},{13,9},{2,6},{6,2},{1... | collective-permute-start | bytes 688136 | tf_op jit(solution)/shard_map/ppermute | solution.py:317
  32.1 12.4 %collective-permute-start.11 = (bf16[32,2688]{1,0:T(8,128)(2,1)S(1)}, bf16[32,2688]{1,0:T(8,128)(2,1)S(1)}, u32[]{:S(2)}, u32[]{:S(2)}) collective-permute-start(bf16[32,2688]{1,0:T(8,128)(2,1)S(1)} %collective-permute-done.10.rest_5_), channel_id=1, source_target_pairs={{0,4},{4,0},{8,12},{12,8},{1,5},{5,1},{9,13},{13,9},{2,6},{6,2},{1... | collective-permute-start | bytes 516104 | tf_op jit(solution)/shard_map/ppermute | solution.py:319
  35.9 10.8 %collective-permute-start.12 = (bf16[128,512]{1,0:T(8,128)(2,1)S(1)}, bf16[128,512]{1,0:T(8,128)(2,1)S(1)}, u32[]{:S(2)}, u32[]{:S(2)}) collective-permute-start(bf16[128,512]{1,0:T(8,128)(2,1)S(1)} %pad_maximum_fusion), channel_id=1, source_target_pairs={{0,0},{4,4},{8,12},{12,8},{1,1},{5,5},{9,13},{13,9},{2,2},{6,6},{1... | collective-permute-start | bytes 393224 | tf_op jit(solution)/shard_map/ppermute | solution.py:323
  39.2 9.0 %collective-permute-start.13 = (bf16[128,256]{1,0:T(8,128)(2,1)S(1)}, bf16[128,256]{1,0:T(8,128)(2,1)S(1)}, u32[]{:S(2)}, u32[]{:S(2)}) collective-permute-start(bf16[128,256]{1,0:T(8,128)(2,1)S(1)} %pad_maximum_fusion.1), channel_id=1, source_target_pairs={{0,0},{4,4},{8,12},{12,8},{1,1},{5,5},{9,13},{13,9},{2,2},{6,6},{1... | collective-permute-start | bytes 196616 | tf_op jit(solution)/shard_map/ppermute | solution.py:323

commit v9 on v6

--- a/solution.py
+++ b/solution.py
@@ -72,6 +72,8 @@
 ONE = [(i, i ^ 1) for i in range(4)]
 TWO = [(i, i ^ 2) for i in range(4)]
 LAST = [(0, 0), (1, 1), (2, 3), (3, 2)]
+INWARD = [(0, 1), (3, 2)]
+OUTWARD = [(1, 0), (2, 3)]
 
 
 def spread(shard):
@@ -79,8 +81,7 @@
 
 
 def product_kernel(features, piece, out):
-    rows = piece.shape[0]
-    out[...] = jnp.dot(features[:, -rows:], piece[...], preferred_element_type=jnp.float32)
+    out[...] = jnp.dot(features[...], piece[...], preferred_element_type=jnp.float32)
 
 
 def product(features, piece):
@@ -99,7 +100,7 @@
     rows = pieces[0].shape[0]
     rank = ranks[ids[lax.axis_index("req")]]
     total = partial[...]
-    for flip, piece in zip((0, 2, 3), pieces):
+    for flip, piece in enumerate(pieces):
         place = lax.axis_index("ctx") ^ flip
         columns = pl.ds(pl.multiple_of(place * rows, HD), rows)
         total += jnp.dot(hidden[:, columns], piece[...], preferred_element_type=jnp.float32)
@@ -310,27 +311,30 @@
         adapter_ids, adapter_slots, adapter_down, adapter_up
     )
     kv, hidden = kv_base[0], hidden_states[0]
-    rows = adapter_down.shape[1]
-    start = (lax.axis_index("ctx") ^ 1) * rows
-    columns = lax.dynamic_slice_in_dim(hidden, start, rows, 1)
-    kv_one = lax.ppermute(jnp.concatenate([kv, columns], axis=1), "ctx", ONE)
-    kv_two = lax.ppermute(kv, "ctx", TWO)
+    kv_one, kv_two = spread(kv)
     near_down = lax.ppermute(give_down, "req", SIBLING)
     near_up = lax.ppermute(give_up, "req", SIBLING)
     far_down = lax.ppermute(keep_down[1] + near_down[1], "req", ACROSS)
-    far_up = lax.ppermute(keep_up[1] + near_up[1], "req", ACROSS)
+    pass_up, early = lax.optimization_barrier((keep_up[1] + near_up[1], hidden))
+    far_up = lax.ppermute(pass_up, "req", ACROSS)
+    rows = adapter_down.shape[1]
+    start = (lax.axis_index("ctx") ^ 1) * rows
+    features = lax.ppermute(lax.dynamic_slice_in_dim(early, start, rows, 1), "ctx", INWARD)
     down = keep_down[0] + near_down[0] + far_down
+    down, kv_one = lax.optimization_barrier((down, kv_one))
+    down_one = lax.ppermute(down, "ctx", INWARD)
     down_two = lax.ppermute(down, "ctx", TWO)
-    partial = lax.ppermute(product(kv_one, down), "ctx", ONE)
+    mine = product(features, down)
+    partial = lax.ppermute(mine, "ctx", OUTWARD)
     up = keep_up[0] + near_up[0] + far_up
     up_one, up_two = spread(up)
-    ready = lax.optimization_barrier((down_two, kv_two, partial))[0]
+    ready = lax.optimization_barrier((down_two, kv_two))[0]
     down_three = lax.ppermute(ready, "ctx", ONE)
-    ready = up_two
+    ready = lax.optimization_barrier((up_two, down_one, partial))[0]
     up_three = lax.ppermute(ready, "ctx", ONE)
     kv_last = lax.optimization_barrier((kv_two, up_two, up_one))[0]
     kv_three = lax.ppermute(kv_last, "ctx", LAST)
-    downs = [down, down_two, down_three]
+    downs = [down, down_one, down_two, down_three]
     ups = [up, up_one, up_two, up_three]
     low = low_rank(adapter_ids, rank_buckets, hidden, partial, downs)
     parts = attend(lengths, queries_base[0], low, [kv, kv_one, kv_two], ups)

time: 50.6 us -> 51.3 us (1.014)
  the two profiles are of different devices: /device:TPU:28 before, /device:TPU:18 now
where the time goes in v9:
time: 51.3 us; the launch traced here: 51 us
  starting transfers between devices  22.6 us (44%)
  waiting for transfers between devices  18.4 us (36%)
  Pallas kernels  6.4 us (12%)
  other arithmetic  2.74 us (5%)
  between operations  0.83 us (2%)
    ppermute x1, waiting for transfers between devices, body(): down_two = lax.ppermute(down, 'ctx', TWO)  5.38 us
    ppermute x1, waiting for transfers between devices, body(): far_down = lax.ppermute(keep_down[1] + near_down[1], 'req', ACROSS)  5.03 us
    ppermute x4, starting transfers between devices, spread(): return (lax.ppermute(shard, 'ctx', ONE), lax.ppermute(shard, 'ctx', TWO))  4.71 us
    ppermute x1, waiting for transfers between devices, body(): partial = lax.ppermute(mine, 'ctx', OUTWARD)  3.78 us
    ppermute x1, starting transfers between devices, body(): down_three = lax.ppermute(ready, 'ctx', ONE)  3.56 us
    ppermute x1, starting transfers between devices, body(): down_two = lax.ppermute(down, 'ctx', TWO)  2.67 us
    ppermute x1, waiting for transfers between devices, body(): up_three = lax.ppermute(ready, 'ctx', ONE)  2.61 us
    ppermute x1, starting transfers between devices, body(): up_three = lax.ppermute(ready, 'ctx', ONE)  2.48 us
  transfers between devices with their start and end apart: 15, of which 6 were waited for; matrix products, arithmetic and copies ran while one was open for 4% of the time, Pallas kernels for 6%

profile of v9, /device:TPU:18, one launch (start us, length us, event | category | flops | bytes accessed | tf_op | source)
XLA Modules:
  0.0 51.0 jit_solution(3446571389647817249)
XLA Ops:
  0.0 0.7 %pad_add_fusion.table = s32[68]{0:T(128)S(1)} fusion(s32[64]{0:T(128)} %param.15, s32[4]{0:T(128)} %ids.1), kind=kLoop, calls=%fused_computation.10 | loop fusion | flops 68 | bytes 544 | tf_op jit(solution)/shard_map/concatenate | solution.py:67
  0.7 0.0 copy-start.4
  0.7 1.7 %shard_map.91 = (bf16[2,896,128]{2,1,0:T(8,128)(2,1)S(1)}, bf16[2,896,128]{2,1,0:T(8,128)(2,1)S(1)}, bf16[2,32,2688]{2,1,0:T(8,128)(2,1)S(1)}, bf16[2,32,2688]{2,1,0:T(8,128)(2,1)S(1)}) custom-call(s32[68]{0:T(128)S(1)} %pad_add_fusion.table, bf16[16,896,128]{2,1,0:T(8,128)(2,1)} %rest_0_.1, bf16[16,32,2688]{2,1,0:T(8,128)(2,1)} %rest_1_.1), custom_call_target="tpu_custom_call" | custom-call | tf_op jit(solution)/shard_map/pallas_call | solution.py:60
  2.4 0.0 copy-start
  2.4 0.1 collective-permute-start.2
  2.5 0.5 collective-permute-start
  3.0 0.0 copy-done.4
  3.0 1.6 %collective-permute-start.4 = (bf16[128,768]{1,0:T(8,128)(2,1)S(1)}, bf16[128,768]{1,0:T(8,128)(2,1)S(1)}, u32[]{:S(2)}, u32[]{:S(2)}) collective-permute-start(bf16[128,768]{1,0:T(8,128)(2,1)S(1)} %bitcast.19), channel_id=1, source_target_pairs={{0,4},{4,0},{8,12},{12,8},{1,5},{5,1},{9,13},{13,9},{2,6},{6,2},{1... | collective-permute-start | bytes 589832 | tf_op jit(solution)/shard_map/ppermute | solution.py:80
  4.6 0.3 collective-permute-start.8
  4.9 0.0 collective-permute-done.2
  4.9 1.0 %fusion = bf16[896,128]{1,0:T(8,128)(2,1)S(1)} fusion(bf16[2,896,128]{2,1,0:T(8,128)(2,1)} %collective-permute-done.2, bf16[2,896,128]{2,1,0:T(8,128)(2,1)S(1)} %get-tuple-element.24), kind=kLoop, calls=%fused_computation.1 | loop fusion | flops 114688 | bytes 688128 | tf_op jit(solution)/shard_map/add | solution.py:317
  5.9 0.6 %collective-permute-start.3 = (bf16[896,128]{1,0:T(8,128)(2,1)S(1)}, bf16[896,128]{1,0:T(8,128)(2,1)S(1)}, u32[]{:S(2)}, u32[]{:S(2)}) collective-permute-start(bf16[896,128]{1,0:T(8,128)(2,1)S(1)} %fusion), channel_id=1, source_target_pairs={{0,2},{1,3},{2,0},{3,1},{4,6},{5,7},{6,4},{7,5},{8,10},{9,11},{10,... | collective-permute-start | bytes 688136 | tf_op jit(solution)/shard_map/ppermute | solution.py:317
  6.5 0.0 collective-permute-done
  6.5 0.0 copy-start.1
  6.5 0.0 copy-start.2
  6.5 0.0 copy-done
  6.6 1.3 %collective-permute-start.1 = (bf16[128,896]{1,0:T(8,128)(2,1)S(1)}, bf16[128,896]{1,0:T(8,128)(2,1)S(1)}, u32[]{:S(2)}, u32[]{:S(2)}) collective-permute-start(bf16[128,896]{1,0:T(8,128)(2,1)S(1)} %constant_dynamic-slice_fusion), channel_id=1, source_target_pairs={{0,4},{12,8},{1,5},{13,9},{2,6},{14,10},{3,7},{15,11},{16,20},{28,... | collective-permute-start | bytes 688136 | tf_op jit(solution)/shard_map/ppermute | solution.py:322
  7.9 1.6 %collective-permute-start.10 = (bf16[32,2688]{1,0:T(8,128)(2,1)S(1)}, bf16[32,2688]{1,0:T(8,128)(2,1)S(1)}, u32[]{:S(2)}, u32[]{:S(2)}) collective-permute-start(bf16[32,2688]{1,0:T(8,128)(2,1)S(1)} %fusion.5), channel_id=1, source_target_pairs={{0,2},{1,3},{2,0},{3,1},{4,6},{5,7},{6,4},{7,5},{8,10},{9,11},{10,... | collective-permute-start | bytes 516104 | tf_op jit(solution)/shard_map/ppermute | solution.py:319
  9.5 5.0 %collective-permute-done.3 = bf16[896,128]{1,0:T(8,128)(2,1)S(1)} collective-permute-done((bf16[896,128]{1,0:T(8,128)(2,1)S(1)}, bf16[896,128]{1,0:T(8,128)(2,1)S(1)}, u32[]{:S(2)}, u32[]{:S(2)}) %collective-permute-start.3) | collective-permute-done | bytes 229408 | tf_op jit(solution)/shard_map/ppermute | solution.py:317
  14.5 1.0 %fusion.2.piece.rest_0_ = bf16[896,128]{1,0:T(8,128)(2,1)S(1)} fusion(bf16[896,128]{1,0:T(8,128)(2,1)S(1)} %collective-permute-done.3, bf16[2,896,128]{2,1,0:T(8,128)(2,1)} %collective-permute-done.2, bf16[2,896,128]{2,1,0:T(8,128)(2,1)S(1)} %get-tuple-element.24), kind=kLoop, calls=%fused_computation.4 | loop fusion | flops 229376 | bytes 917504 | tf_op jit(solution)/shard_map/add | solution.py:323
  15.5 0.0 collective-permute-done.4.rest_1_
  15.5 2.7 %collective-permute-start.7 = (bf16[896,128]{1,0:T(8,128)(2,1)S(1)}, bf16[896,128]{1,0:T(8,128)(2,1)S(1)}, u32[]{:S(2)}, u32[]{:S(2)}) collective-permute-start(bf16[896,128]{1,0:T(8,128)(2,1)S(1)} %fusion.2.piece.rest_0_), channel_id=1, source_target_pairs={{0,8},{4,12},{8,0},{12,4},{1,9},{5,13},{9,1},{13,5},{2,10},{6,14},... | collective-permute-start | bytes 688136 | tf_op jit(solution)/shard_map/ppermute | solution.py:326
  18.1 1.3 %collective-permute-start.6 = (bf16[896,128]{1,0:T(8,128)(2,1)S(1)}, bf16[896,128]{1,0:T(8,128)(2,1)S(1)}, u32[]{:S(2)}, u32[]{:S(2)}) collective-permute-start(bf16[896,128]{1,0:T(8,128)(2,1)S(1)} %fusion.2.piece.rest_0_), channel_id=1, source_target_pairs={{0,4},{12,8},{1,5},{13,9},{2,6},{14,10},{3,7},{15,11},{16,20},{28,... | collective-permute-start | bytes 688136 | tf_op jit(solution)/shard_map/ppermute | solution.py:325
  19.4 0.0 collective-permute-done.10
  19.5 0.0 copy-start.3
  19.5 2.0 %collective-permute-start.12 = (bf16[32,2688]{1,0:T(8,128)(2,1)S(1)}, bf16[32,2688]{1,0:T(8,128)(2,1)S(1)}, u32[]{:S(2)}, u32[]{:S(2)}) collective-permute-start(bf16[32,2688]{1,0:T(8,128)(2,1)S(1)} %fusion.4.rest_3_), channel_id=1, source_target_pairs={{0,8},{4,12},{8,0},{12,4},{1,9},{5,13},{9,1},{13,5},{2,10},{6,14},... | collective-permute-start | bytes 516104 | tf_op jit(solution)/shard_map/ppermute | solution.py:80
  21.5 0.0 collective-permute-done.8.rest_2_
  21.5 0.8 %collective-permute-start.11 = (bf16[32,2688]{1,0:T(8,128)(2,1)S(1)}, bf16[32,2688]{1,0:T(8,128)(2,1)S(1)}, u32[]{:S(2)}, u32[]{:S(2)}) collective-permute-start(bf16[32,2688]{1,0:T(8,128)(2,1)S(1)} %fusion.4.rest_3_), channel_id=1, source_target_pairs={{0,4},{4,0},{8,12},{12,8},{1,5},{5,1},{9,13},{13,9},{2,6},{6,2},{1... | collective-permute-start | bytes 516104 | tf_op jit(solution)/shard_map/ppermute | solution.py:80
  22.3 5.4 %collective-permute-done.7.rest_2_ = bf16[896,128]{1,0:T(8,128)(2,1)S(1)} collective-permute-done((bf16[896,128]{1,0:T(8,128)(2,1)S(1)}, bf16[896,128]{1,0:T(8,128)(2,1)S(1)}, u32[]{:S(2)}, u32[]{:S(2)}) %collective-permute-start.7) | collective-permute-done | bytes 229408 | tf_op jit(solution)/shard_map/ppermute | solution.py:326
  27.7 3.6 %collective-permute-start.9 = (bf16[896,128]{1,0:T(8,128)(2,1)S(1)}, bf16[896,128]{1,0:T(8,128)(2,1)S(1)}, u32[]{:S(2)}, u32[]{:S(2)}) collective-permute-start(bf16[896,128]{1,0:T(8,128)(2,1)S(1)} %collective-permute-done.7.rest_2_), channel_id=1, source_target_pairs={{0,4},{4,0},{8,12},{12,8},{1,5},{5,1},{9,13},{13,9},{2,6},{6,2},{1... | collective-permute-start | bytes 688136 | tf_op jit(solution)/shard_map/ppermute | solution.py:332
  31.2 0.0 collective-permute-done.1.features
  31.2 0.2 shard_map.92
  31.5 1.9 %collective-permute-start.5 = (f32[128,128]{1,0:T(8,128)S(1)}, f32[128,128]{1,0:T(8,128)S(1)}, u32[]{:S(2)}, u32[]{:S(2)}) collective-permute-start(f32[128,128]{1,0:T(8,128)S(1)} %shard_map.92), channel_id=1, source_target_pairs={{4,0},{8,12},{5,1},{9,13},{6,2},{10,14},{7,3},{11,15},{20,16},{24,... | collective-permute-start | bytes 196616 | tf_op jit(solution)/shard_map/ppermute | solution.py:328
  33.4 0.3 collective-permute-done.12.rest_5_
  33.7 3.8 %collective-permute-done.5.partial = f32[128,128]{1,0:T(8,128)S(1)} collective-permute-done((f32[128,128]{1,0:T(8,128)S(1)}, f32[128,128]{1,0:T(8,128)S(1)}, u32[]{:S(2)}, u32[]{:S(2)}) %collective-permute-start.5) | collective-permute-done | bytes 65568 | tf_op jit(solution)/shard_map/ppermute | solution.py:328
  37.4 0.0 collective-permute-done.6.rest_1_
  37.4 2.5 %collective-permute-start.13 = (bf16[32,2688]{1,0:T(8,128)(2,1)S(1)}, bf16[32,2688]{1,0:T(8,128)(2,1)S(1)}, u32[]{:S(2)}, u32[]{:S(2)}) collective-permute-start(bf16[32,2688]{1,0:T(8,128)(2,1)S(1)} %collective-permute-done.12.rest_5_), channel_id=1, source_target_pairs={{0,4},{4,0},{8,12},{12,8},{1,5},{5,1},{9,13},{13,9},{2,6},{6,2},{1... | collective-permute-start | bytes 516104 | tf_op jit(solution)/shard_map/ppermute | solution.py:334
  39.9 0.0 collective-permute-done.11.rest_4_
  39.9 1.9 %collective-permute-start.14 = (bf16[128,768]{1,0:T(8,128)(2,1)S(1)}, bf16[128,768]{1,0:T(8,128)(2,1)S(1)}, u32[]{:S(2)}, u32[]{:S(2)}) collective-permute-start(bf16[128,768]{1,0:T(8,128)(2,1)S(1)} %collective-permute-done.8.rest_2_), channel_id=1, source_target_pairs={{0,0},{4,4},{8,12},{12,8},{1,1},{5,5},{9,13},{13,9},{2,2},{6,6},{1... | collective-permute-start | bytes 589832 | tf_op jit(solution)/shard_map/ppermute | solution.py:336
  42.5 0.0 collective-permute-done.9.rest_3_
  42.5 0.0 copy-done.1
  42.5 0.0 copy-done.2
  42.5 0.9 %shard_map.93.low = bf16[128,128]{1,0:T(8,128)(2,1)S(1)} custom-call(s32[4]{0:T(128)S(1)} %copy-done.1, s32[64]{0:T(128)S(1)} %copy-done.2, bf16[128,3584]{1,0:T(8,128)(2,1)S(1)} %bitcast.17, f32[128,128]{1,0:T(8,128)S(1)} %collective-permute-done.5.partial, bf16[896,128]{1,0:T(8,128)(2,1)S(1)} %fusion.2.piece.rest_0_, ...), custom_call_target="tpu_custom_call" | custom-call | flops 134217728 | bytes 4194304 | tf_op jit(solution)/shard_map/pallas_call | solution.py:112
  43.5 2.6 %collective-permute-done.13.rest_6_ = bf16[32,2688]{1,0:T(8,128)(2,1)S(1)} collective-permute-done((bf16[32,2688]{1,0:T(8,128)(2,1)S(1)}, bf16[32,2688]{1,0:T(8,128)(2,1)S(1)}, u32[]{:S(2)}, u32[]{:S(2)}) %collective-permute-start.13) | collective-permute-done | bytes 172064 | tf_op jit(solution)/shard_map/ppermute | solution.py:334
  46.1 0.0 copy-done.3
  46.1 1.7 %shard_map.94 = (bf16[128,2688]{1,0:T(8,128)(2,1)}, bf16[2688,128]{1,0:T(8,128)(2,1)S(1)}, f32[2688,128]{1,0:T(8,128)S(1)}, f32[2688,128]{1,0:T(8,128)S(1)}, f32[2688,128]{1,0:T(8,128)S(1)}) custom-call(s32[1]{0:T(128)S(6)} %copy.12.lengths, bf16[128,2688]{1,0:T(8,128)(2,1)S(1)} %bitcast.18, bf16[128,128]{1,0:T(8,128)(2,1)S(1)} %shard_map.93.low, ...), custom_call_target="tpu_custom_call" | custom-call | flops 1073741824 | bytes 4194304 | tf_op jit(solution)/shard_map/pallas_call | solution.py:229
  47.8 1.3 %collective-permute-done.14.kv = bf16[128,768]{1,0:T(8,128)(2,1)S(1)} collective-permute-done((bf16[128,768]{1,0:T(8,128)(2,1)S(1)}, bf16[128,768]{1,0:T(8,128)(2,1)S(1)}, u32[]{:S(2)}, u32[]{:S(2)}) %collective-permute-start.14) | collective-permute-done | bytes 196640 | tf_op jit(solution)/shard_map/ppermute | solution.py:336
  49.2 1.8 %shard_map.95 = bf16[128,2688]{1,0:T(8,128)(2,1)} custom-call(s32[1]{0:T(128)S(6)} %copy.12.lengths, bf16[128,2688]{1,0:T(8,128)(2,1)} %get-tuple-element.31.so_far, bf16[2688,128]{1,0:T(8,128)(2,1)S(1)} %get-tuple-element.32.queries, f32[2688,128]{1,0:T(8,128)S(1)} %get-tuple-element.33.sums, ...), custom_call_target="tpu_custom_call", output_to_operand_aliasing={{}: (1, {})} | custom-call | flops 268435456 | bytes 2097152 | tf_op jit(solution)/shard_map/pallas_call | solution.py:282
  (3 shorter events, 0.1 us)
Async XLA Ops:
  0.7 2.3 %copy-start.4 = (bf16[1,128,768]{2,1,0:T(8,128)(2,1)S(1)}, bf16[1,128,768]{2,1,0:T(8,128)(2,1)}, u32[]{:S(2)}) copy-start(bf16[1,128,768]{2,1,0:T(8,128)(2,1)} %param.11) | copy-start | bytes 589828
  2.4 4.1 %copy-start = (bf16[1,128,3584]{2,1,0:T(8,128)(2,1)S(1)}, bf16[1,128,3584]{2,1,0:T(8,128)(2,1)}, u32[]{:S(2)}) copy-start(bf16[1,128,3584]{2,1,0:T(8,128)(2,1)} %param.9) | copy-start | bytes 2752516
  2.4 2.5 %collective-permute-start.2 = (bf16[2,896,128]{2,1,0:T(8,128)(2,1)S(1)}, bf16[2,896,128]{2,1,0:T(8,128)(2,1)}, u32[]{:S(2)}, u32[]{:S(2)}) collective-permute-start(bf16[2,896,128]{2,1,0:T(8,128)(2,1)S(1)} %get-tuple-element.25), channel_id=1, source_target_pairs={{0,1},{1,0},{2,3},{3,2},{4,5},{5,4},{6,7},{7,6},{8,9},{9,8},{10,11... | collective-permute-start | bytes 1376264 | tf_op jit(solution)/shard_map/ppermute | solution.py:315
  2.5 4.0 %collective-permute-start = (bf16[2,32,2688]{2,1,0:T(8,128)(2,1)S(1)}, bf16[2,32,2688]{2,1,0:T(8,128)(2,1)S(1)}, u32[]{:S(2)}, u32[]{:S(2)}) collective-permute-start(bf16[2,32,2688]{2,1,0:T(8,128)(2,1)S(1)} %get-tuple-element.22), channel_id=1, source_target_pairs={{0,1},{1,0},{2,3},{3,2},{4,5},{5,4},{6,7},{7,6},{8,9},{9,8},{10,11... | collective-permute-start | bytes 1032200 | tf_op jit(solution)/shard_map/ppermute | solution.py:316
  3.0 12.4 %collective-permute-start.4 = (bf16[128,768]{1,0:T(8,128)(2,1)S(1)}, bf16[128,768]{1,0:T(8,128)(2,1)S(1)}, u32[]{:S(2)}, u32[]{:S(2)}) collective-permute-start(bf16[128,768]{1,0:T(8,128)(2,1)S(1)} %bitcast.19), channel_id=1, source_target_pairs={{0,4},{4,0},{8,12},{12,8},{1,5},{5,1},{9,13},{13,9},{2,6},{6,2},{1... | collective-permute-start | bytes 589832 | tf_op jit(solution)/shard_map/ppermute | solution.py:80
  4.6 16.9 %collective-permute-start.8 = (bf16[128,768]{1,0:T(8,128)(2,1)S(1)}, bf16[128,768]{1,0:T(8,128)(2,1)S(1)}, u32[]{:S(2)}, u32[]{:S(2)}) collective-permute-start(bf16[128,768]{1,0:T(8,128)(2,1)S(1)} %bitcast.20), channel_id=1, source_target_pairs={{0,8},{4,12},{8,0},{12,4},{1,9},{5,13},{9,1},{13,5},{2,10},{6,14},... | collective-permute-start | bytes 589832 | tf_op jit(solution)/shard_map/ppermute | solution.py:80
  5.9 8.6 %collective-permute-start.3 = (bf16[896,128]{1,0:T(8,128)(2,1)S(1)}, bf16[896,128]{1,0:T(8,128)(2,1)S(1)}, u32[]{:S(2)}, u32[]{:S(2)}) collective-permute-start(bf16[896,128]{1,0:T(8,128)(2,1)S(1)} %fusion), channel_id=1, source_target_pairs={{0,2},{1,3},{2,0},{3,1},{4,6},{5,7},{6,4},{7,5},{8,10},{9,11},{10,... | collective-permute-start | bytes 688136 | tf_op jit(solution)/shard_map/ppermute | solution.py:317
  6.5 36.0 %copy-start.1 = (s32[4]{0:T(128)S(1)}, s32[4]{0:T(128)}, u32[]{:S(2)}) copy-start(s32[4]{0:T(128)} %ids.1) | copy-start | bytes 52
  6.5 36.0 %copy-start.2 = (s32[64]{0:T(128)S(1)}, s32[64]{0:T(128)}, u32[]{:S(2)}) copy-start(s32[64]{0:T(128)} %ranks.1) | copy-start | bytes 772
  6.6 24.6 %collective-permute-start.1 = (bf16[128,896]{1,0:T(8,128)(2,1)S(1)}, bf16[128,896]{1,0:T(8,128)(2,1)S(1)}, u32[]{:S(2)}, u32[]{:S(2)}) collective-permute-start(bf16[128,896]{1,0:T(8,128)(2,1)S(1)} %constant_dynamic-slice_fusion), channel_id=1, source_target_pairs={{0,4},{12,8},{1,5},{13,9},{2,6},{14,10},{3,7},{15,11},{16,20},{28,... | collective-permute-start | bytes 688136 | tf_op jit(solution)/shard_map/ppermute | solution.py:322
  7.9 11.5 %collective-permute-start.10 = (bf16[32,2688]{1,0:T(8,128)(2,1)S(1)}, bf16[32,2688]{1,0:T(8,128)(2,1)S(1)}, u32[]{:S(2)}, u32[]{:S(2)}) collective-permute-start(bf16[32,2688]{1,0:T(8,128)(2,1)S(1)} %fusion.5), channel_id=1, source_target_pairs={{0,2},{1,3},{2,0},{3,1},{4,6},{5,7},{6,4},{7,5},{8,10},{9,11},{10,... | collective-permute-start | bytes 516104 | tf_op jit(solution)/shard_map/ppermute | solution.py:319
  15.5 12.2 %collective-permute-start.7 = (bf16[896,128]{1,0:T(8,128)(2,1)S(1)}, bf16[896,128]{1,0:T(8,128)(2,1)S(1)}, u32[]{:S(2)}, u32[]{:S(2)}) collective-permute-start(bf16[896,128]{1,0:T(8,128)(2,1)S(1)} %fusion.2.piece.rest_0_), channel_id=1, source_target_pairs={{0,8},{4,12},{8,0},{12,4},{1,9},{5,13},{9,1},{13,5},{2,10},{6,14},... | collective-permute-start | bytes 688136 | tf_op jit(solution)/shard_map/ppermute | solution.py:326
  18.1 19.3 %collective-permute-start.6 = (bf16[896,128]{1,0:T(8,128)(2,1)S(1)}, bf16[896,128]{1,0:T(8,128)(2,1)S(1)}, u32[]{:S(2)}, u32[]{:S(2)}) collective-permute-start(bf16[896,128]{1,0:T(8,128)(2,1)S(1)} %fusion.2.piece.rest_0_), channel_id=1, source_target_pairs={{0,4},{12,8},{1,5},{13,9},{2,6},{14,10},{3,7},{15,11},{16,20},{28,... | collective-permute-start | bytes 688136 | tf_op jit(solution)/shard_map/ppermute | solution.py:325
  19.5 26.6 %copy-start.3 = (bf16[1,128,2688]{2,1,0:T(8,128)(2,1)S(1)}, bf16[1,128,2688]{2,1,0:T(8,128)(2,1)}, u32[]{:S(2)}) copy-start(bf16[1,128,2688]{2,1,0:T(8,128)(2,1)} %param.10) | copy-start | bytes 2064388
  19.5 14.2 %collective-permute-start.12 = (bf16[32,2688]{1,0:T(8,128)(2,1)S(1)}, bf16[32,2688]{1,0:T(8,128)(2,1)S(1)}, u32[]{:S(2)}, u32[]{:S(2)}) collective-permute-start(bf16[32,2688]{1,0:T(8,128)(2,1)S(1)} %fusion.4.rest_3_), channel_id=1, source_target_pairs={{0,8},{4,12},{8,0},{12,4},{1,9},{5,13},{9,1},{13,5},{2,10},{6,14},... | collective-permute-start | bytes 516104 | tf_op jit(solution)/shard_map/ppermute | solution.py:80
  21.5 18.4 %collective-permute-start.11 = (bf16[32,2688]{1,0:T(8,128)(2,1)S(1)}, bf16[32,2688]{1,0:T(8,128)(2,1)S(1)}, u32[]{:S(2)}, u32[]{:S(2)}) collective-permute-start(bf16[32,2688]{1,0:T(8,128)(2,1)S(1)} %fusion.4.rest_3_), channel_id=1, source_target_pairs={{0,4},{4,0},{8,12},{12,8},{1,5},{5,1},{9,13},{13,9},{2,6},{6,2},{1... | collective-permute-start | bytes 516104 | tf_op jit(solution)/shard_map/ppermute | solution.py:80
  27.7 14.8 %collective-permute-start.9 = (bf16[896,128]{1,0:T(8,128)(2,1)S(1)}, bf16[896,128]{1,0:T(8,128)(2,1)S(1)}, u32[]{:S(2)}, u32[]{:S(2)}) collective-permute-start(bf16[896,128]{1,0:T(8,128)(2,1)S(1)} %collective-permute-done.7.rest_2_), channel_id=1, source_target_pairs={{0,4},{4,0},{8,12},{12,8},{1,5},{5,1},{9,13},{13,9},{2,6},{6,2},{1... | collective-permute-start | bytes 688136 | tf_op jit(solution)/shard_map/ppermute | solution.py:332
  31.5 6.0 %collective-permute-start.5 = (f32[128,128]{1,0:T(8,128)S(1)}, f32[128,128]{1,0:T(8,128)S(1)}, u32[]{:S(2)}, u32[]{:S(2)}) collective-permute-start(f32[128,128]{1,0:T(8,128)S(1)} %shard_map.92), channel_id=1, source_target_pairs={{4,0},{8,12},{5,1},{9,13},{6,2},{10,14},{7,3},{11,15},{20,16},{24,... | collective-permute-start | bytes 196616 | tf_op jit(solution)/shard_map/ppermute | solution.py:328
  37.4 8.6 %collective-permute-start.13 = (bf16[32,2688]{1,0:T(8,128)(2,1)S(1)}, bf16[32,2688]{1,0:T(8,128)(2,1)S(1)}, u32[]{:S(2)}, u32[]{:S(2)}) collective-permute-start(bf16[32,2688]{1,0:T(8,128)(2,1)S(1)} %collective-permute-done.12.rest_5_), channel_id=1, source_target_pairs={{0,4},{4,0},{8,12},{12,8},{1,5},{5,1},{9,13},{13,9},{2,6},{6,2},{1... | collective-permute-start | bytes 516104 | tf_op jit(solution)/shard_map/ppermute | solution.py:334
  39.9 9.2 %collective-permute-start.14 = (bf16[128,768]{1,0:T(8,128)(2,1)S(1)}, bf16[128,768]{1,0:T(8,128)(2,1)S(1)}, u32[]{:S(2)}, u32[]{:S(2)}) collective-permute-start(bf16[128,768]{1,0:T(8,128)(2,1)S(1)} %collective-permute-done.8.rest_2_), channel_id=1, source_target_pairs={{0,0},{4,4},{8,12},{12,8},{1,1},{5,5},{9,13},{13,9},{2,2},{6,6},{1... | collective-permute-start | bytes 589832 | tf_op jit(solution)/shard_map/ppermute | solution.py:336

commit v10 on v4

--- a/solution.py
+++ b/solution.py
@@ -190,7 +190,8 @@
                         result[h, :, g * HD : (g + 1) * HD] = (
                             product[g * tokens : (g + 1) * tokens, :] / totals[g]
                         ).astype(jnp.bfloat16)
-                    copies[h].start()
+                    if h:
+                        copies[h - 1].start()
                 else:
                     queries[h * block : (h + 1) * block, :] = query
                     sums[h * block : (h + 1) * block, :] = product
@@ -198,6 +199,8 @@
                         at = slice(h * block + g * tokens, h * block + (g + 1) * tokens)
                         highs[at, :] = jnp.broadcast_to(tops[g], (tokens, HD))
                         counts[at, :] = jnp.broadcast_to(totals[g], (tokens, HD))
+            if mine < 2:
+                copies[KVH - 1].start()
 
     @pl.when(jnp.logical_not(live) | (z < 2))
     def _():
@@ -238,12 +241,9 @@
 
     @pl.when((z * tokens < lengths[0]) & (z >= 2))
     def _():
-        heads = [head_columns([kv], h) for h in range(KVH)]
-        all_scores = [
-            dot_keys(queries[h * block : (h + 1) * block, :], heads[h][0]) for h in range(KVH)
-        ]
         for h in range(KVH):
-            scores, values = all_scores[h], heads[h][1]
+            keys, values = head_columns([kv], h)
+            scores = dot_keys(queries[h * block : (h + 1) * block, :], keys)
             weights, factors, totals = [], [], []
             for g in range(GROUP):
                 at = slice(h * block + g * tokens, h * block + (g + 1) * tokens)
@@ -261,7 +261,9 @@
                 at = slice(h * block + g * tokens, h * block + (g + 1) * tokens)
                 whole = sums[at, :] * factors[g] + product[g * tokens : (g + 1) * tokens, :]
                 result[h, :, g * HD : (g + 1) * HD] = (whole / totals[g]).astype(jnp.bfloat16)
-            copies[h].start()
+            if h:
+                copies[h - 1].start()
+        copies[KVH - 1].start()
         for copy in copies:
             copy.wait()
 

time: 47.7 us -> 47.1 us (0.987)
  the two profiles are of different devices: /device:TPU:18 before, /device:TPU:24 now
where the time goes in v10:
time: 47.1 us; the launch traced here: 46.8 us
  waiting for transfers between devices  25.4 us (54%)
  starting transfers between devices  14.1 us (30%)
  Pallas kernels  5.64 us (12%)
  other arithmetic  0.89 us (2%)
  between operations  0.73 us (2%)
    ppermute x6, waiting for transfers between devices, spread(): return (lax.ppermute(shard, 'ctx', ONE), lax.ppermute(shard, 'ctx', TWO))  14.4 us
    ppermute x6, starting transfers between devices, spread(): return (lax.ppermute(shard, 'ctx', ONE), lax.ppermute(shard, 'ctx', TWO))  6.69 us
    ppermute x1, waiting for transfers between devices, body(): far_down = lax.ppermute(keep_down[1] + near_down[1], 'req', ACROSS)  5.91 us
    ppermute x1, starting transfers between devices, body(): kv_three = lax.ppermute(kv_last, 'ctx', LAST)  3.45 us
    ppermute x1, waiting for transfers between devices, body(): up_three = lax.ppermute(up_two, 'ctx', ONE)  2.73 us
    ppermute x1, starting transfers between devices, body(): far_down = lax.ppermute(keep_down[1] + near_down[1], 'req', ACROSS)  2.61 us
    pallas_call x1, Pallas kernels, attend(): pl.pallas_call(attend_kernel, out_shape=shapes, in_specs=[spec(SMEM)] + [...  1.99 us
    pallas_call x1, Pallas kernels, finish(): pl.pallas_call(finish_kernel, out_shape=jax.ShapeDtypeStruct(so_far.shape...  1.9 us
  transfers between devices with their start and end apart: 13, of which 8 were waited for; matrix products, arithmetic and copies ran while one was open for 0% of the time, Pallas kernels for 6%

profile of v10, /device:TPU:24, one launch (start us, length us, event | category | flops | bytes accessed | tf_op | source)
XLA Modules:
  0.0 46.8 jit_solution(10789546806280608673)
XLA Ops:
  0.0 0.7 %pad_add_fusion.table = s32[68]{0:T(128)S(1)} fusion(s32[64]{0:T(128)} %param.15, s32[4]{0:T(128)} %ids.1), kind=kLoop, calls=%fused_computation.10 | loop fusion | flops 68 | bytes 544 | tf_op jit(solution)/shard_map/concatenate | solution.py:67
  0.7 0.0 copy-start.4
  0.7 0.8 %shard_map.91 = (bf16[2,896,128]{2,1,0:T(8,128)(2,1)S(1)}, bf16[2,896,128]{2,1,0:T(8,128)(2,1)S(1)}, bf16[2,32,2688]{2,1,0:T(8,128)(2,1)S(1)}, bf16[2,32,2688]{2,1,0:T(8,128)(2,1)S(1)}) custom-call(s32[68]{0:T(128)S(1)} %pad_add_fusion.table, bf16[16,896,128]{2,1,0:T(8,128)(2,1)} %rest_0_.1, bf16[16,32,2688]{2,1,0:T(8,128)(2,1)} %rest_1_.1), custom_call_target="tpu_custom_call" | custom-call | tf_op jit(solution)/shard_map/pallas_call | solution.py:60
  1.6 0.1 collective-permute-start
  1.6 0.5 %collective-permute-start.7 = (bf16[2,32,2688]{2,1,0:T(8,128)(2,1)S(1)}, bf16[2,32,2688]{2,1,0:T(8,128)(2,1)S(1)}, u32[]{:S(2)}, u32[]{:S(2)}) collective-permute-start(bf16[2,32,2688]{2,1,0:T(8,128)(2,1)S(1)} %get-tuple-element.25), channel_id=1, source_target_pairs={{0,1},{1,0},{2,3},{3,2},{4,5},{5,4},{6,7},{7,6},{8,9},{9,8},{10,11... | collective-permute-start | bytes 1032200 | tf_op jit(solution)/shard_map/ppermute | solution.py:307
  2.1 0.0 copy-done.4
  2.1 0.4 collective-permute-start.2
  2.6 0.0 collective-permute-start.5
  2.6 0.8 %collective-permute-done = bf16[2,896,128]{2,1,0:T(8,128)(2,1)S(1)} collective-permute-done((bf16[2,896,128]{2,1,0:T(8,128)(2,1)S(1)}, bf16[2,896,128]{2,1,0:T(8,128)(2,1)S(1)}, u32[]{:S(2)}, u32[]{:S(2)}) %collective-permute-start) | collective-permute-done | bytes 458784 | tf_op jit(solution)/shard_map/ppermute | solution.py:306
  3.4 0.0 copy-start
  3.4 0.0 copy-start.1
  3.4 0.0 copy-start.2
  3.5 2.6 %collective-permute-start.1 = (bf16[896,128]{1,0:T(8,128)(2,1)S(1)}, bf16[896,128]{1,0:T(8,128)(2,1)S(1)}, u32[]{:S(2)}, u32[]{:S(2)}) collective-permute-start(bf16[896,128]{1,0:T(8,128)(2,1)S(1)} %fusion), channel_id=1, source_target_pairs={{0,2},{1,3},{2,0},{3,1},{4,6},{5,7},{6,4},{7,5},{8,10},{9,11},{10,... | collective-permute-start | bytes 688136 | tf_op jit(solution)/shard_map/ppermute | solution.py:308
  6.1 0.0 collective-permute-done.7
  6.1 0.4 collective-permute-start.8
  6.6 5.9 %collective-permute-done.1 = bf16[896,128]{1,0:T(8,128)(2,1)S(1)} collective-permute-done((bf16[896,128]{1,0:T(8,128)(2,1)S(1)}, bf16[896,128]{1,0:T(8,128)(2,1)S(1)}, u32[]{:S(2)}, u32[]{:S(2)}) %collective-permute-start.1) | collective-permute-done | bytes 229408 | tf_op jit(solution)/shard_map/ppermute | solution.py:308
  12.5 0.0 copy-start.3
  12.5 0.0 collective-permute-done.2.rest_1_
  12.6 2.2 %collective-permute-start.4 = (bf16[896,128]{1,0:T(8,128)(2,1)S(1)}, bf16[896,128]{1,0:T(8,128)(2,1)S(1)}, u32[]{:S(2)}, u32[]{:S(2)}) collective-permute-start(bf16[896,128]{1,0:T(8,128)(2,1)S(1)} %fusion.2.rest_0_), channel_id=1, source_target_pairs={{0,8},{4,12},{8,0},{12,4},{1,9},{5,13},{9,1},{13,5},{2,10},{6,14},... | collective-permute-start | bytes 688136 | tf_op jit(solution)/shard_map/ppermute | solution.py:78
  14.8 1.6 %collective-permute-start.3 = (bf16[896,128]{1,0:T(8,128)(2,1)S(1)}, bf16[896,128]{1,0:T(8,128)(2,1)S(1)}, u32[]{:S(2)}, u32[]{:S(2)}) collective-permute-start(bf16[896,128]{1,0:T(8,128)(2,1)S(1)} %fusion.2.rest_0_), channel_id=1, source_target_pairs={{0,4},{4,0},{8,12},{12,8},{1,5},{5,1},{9,13},{13,9},{2,6},{6,2},{1... | collective-permute-start | bytes 688136 | tf_op jit(solution)/shard_map/ppermute | solution.py:78
  16.4 0.0 collective-permute-done.8
  16.4 0.8 %collective-permute-start.10 = (bf16[32,2688]{1,0:T(8,128)(2,1)S(1)}, bf16[32,2688]{1,0:T(8,128)(2,1)S(1)}, u32[]{:S(2)}, u32[]{:S(2)}) collective-permute-start(bf16[32,2688]{1,0:T(8,128)(2,1)S(1)} %fusion.5.rest_3_), channel_id=1, source_target_pairs={{0,8},{4,12},{8,0},{12,4},{1,9},{5,13},{9,1},{13,5},{2,10},{6,14},... | collective-permute-start | bytes 516104 | tf_op jit(solution)/shard_map/ppermute | solution.py:78
  17.3 1.6 %collective-permute-start.9 = (bf16[32,2688]{1,0:T(8,128)(2,1)S(1)}, bf16[32,2688]{1,0:T(8,128)(2,1)S(1)}, u32[]{:S(2)}, u32[]{:S(2)}) collective-permute-start(bf16[32,2688]{1,0:T(8,128)(2,1)S(1)} %fusion.5.rest_3_), channel_id=1, source_target_pairs={{0,4},{4,0},{8,12},{12,8},{1,5},{5,1},{9,13},{13,9},{2,6},{6,2},{1... | collective-permute-start | bytes 516104 | tf_op jit(solution)/shard_map/ppermute | solution.py:78
  18.8 0.0 collective-permute-done.5.rest_2_
  18.8 7.6 %collective-permute-done.4.rest_2_ = bf16[896,128]{1,0:T(8,128)(2,1)S(1)} collective-permute-done((bf16[896,128]{1,0:T(8,128)(2,1)S(1)}, bf16[896,128]{1,0:T(8,128)(2,1)S(1)}, u32[]{:S(2)}, u32[]{:S(2)}) %collective-permute-start.4) | collective-permute-done | bytes 229408 | tf_op jit(solution)/shard_map/ppermute | solution.py:78
  26.4 0.3 collective-permute-start.6
  26.7 5.0 %collective-permute-done.10.rest_5_ = bf16[32,2688]{1,0:T(8,128)(2,1)S(1)} collective-permute-done((bf16[32,2688]{1,0:T(8,128)(2,1)S(1)}, bf16[32,2688]{1,0:T(8,128)(2,1)S(1)}, u32[]{:S(2)}, u32[]{:S(2)}) %collective-permute-start.10) | collective-permute-done | bytes 172064 | tf_op jit(solution)/shard_map/ppermute | solution.py:78
  31.7 0.0 collective-permute-done.3.rest_1_
  31.7 0.0 collective-permute-start.11
  31.7 1.9 %collective-permute-done.9.rest_4_ = bf16[32,2688]{1,0:T(8,128)(2,1)S(1)} collective-permute-done((bf16[32,2688]{1,0:T(8,128)(2,1)S(1)}, bf16[32,2688]{1,0:T(8,128)(2,1)S(1)}, u32[]{:S(2)}, u32[]{:S(2)}) %collective-permute-start.9) | collective-permute-done | bytes 172064 | tf_op jit(solution)/shard_map/ppermute | solution.py:78
  33.6 3.5 %collective-permute-start.12 = (bf16[128,768]{1,0:T(8,128)(2,1)S(1)}, bf16[128,768]{1,0:T(8,128)(2,1)S(1)}, u32[]{:S(2)}, u32[]{:S(2)}) collective-permute-start(bf16[128,768]{1,0:T(8,128)(2,1)S(1)} %collective-permute-done.5.rest_2_), channel_id=1, source_target_pairs={{0,0},{4,4},{8,12},{12,8},{1,1},{5,5},{9,13},{13,9},{2,2},{6,6},{1... | collective-permute-start | bytes 589832 | tf_op jit(solution)/shard_map/ppermute | solution.py:320
  37.7 0.8 %collective-permute-done.6.rest_3_ = bf16[896,128]{1,0:T(8,128)(2,1)S(1)} collective-permute-done((bf16[896,128]{1,0:T(8,128)(2,1)S(1)}, bf16[896,128]{1,0:T(8,128)(2,1)S(1)}, u32[]{:S(2)}, u32[]{:S(2)}) %collective-permute-start.6) | collective-permute-done | bytes 229408 | tf_op jit(solution)/shard_map/ppermute | solution.py:316
  38.5 0.0 copy-done
  38.5 0.0 copy-done.1
  38.5 0.0 copy-done.2
  38.5 0.9 %shard_map.92.low = bf16[128,128]{1,0:T(8,128)(2,1)S(1)} custom-call(s32[4]{0:T(128)S(1)} %copy-done.1, s32[64]{0:T(128)S(1)} %copy-done.2, bf16[128,3584]{1,0:T(8,128)(2,1)S(1)} %bitcast.16, bf16[896,128]{1,0:T(8,128)(2,1)S(1)} %fusion.2.rest_0_, bf16[896,128]{1,0:T(8,128)(2,1)S(1)} %collective-permute-done.3.rest_1_, ...), custom_call_target="tpu_custom_call" | custom-call | flops 134217728 | bytes 4194304 | tf_op jit(solution)/shard_map/pallas_call | solution.py:97
  39.5 2.7 %collective-permute-done.11.rest_6_ = bf16[32,2688]{1,0:T(8,128)(2,1)S(1)} collective-permute-done((bf16[32,2688]{1,0:T(8,128)(2,1)S(1)}, bf16[32,2688]{1,0:T(8,128)(2,1)S(1)}, u32[]{:S(2)}, u32[]{:S(2)}) %collective-permute-start.11) | collective-permute-done | bytes 172064 | tf_op jit(solution)/shard_map/ppermute | solution.py:318
  42.2 0.0 copy-done.3
  42.2 2.0 %shard_map.93 = (bf16[128,2688]{1,0:T(8,128)(2,1)}, bf16[2688,128]{1,0:T(8,128)(2,1)S(1)}, f32[2688,128]{1,0:T(8,128)S(1)}, f32[2688,128]{1,0:T(8,128)S(1)}, f32[2688,128]{1,0:T(8,128)S(1)}) custom-call(s32[1]{0:T(128)S(6)} %copy.12.lengths, bf16[128,2688]{1,0:T(8,128)(2,1)S(1)} %bitcast.17, bf16[128,128]{1,0:T(8,128)(2,1)S(1)} %shard_map.92.low, ...), custom_call_target="tpu_custom_call" | custom-call | flops 1073741824 | bytes 4194304 | tf_op jit(solution)/shard_map/pallas_call | solution.py:218
  44.2 0.6 %collective-permute-done.12.kv = bf16[128,768]{1,0:T(8,128)(2,1)S(1)} collective-permute-done((bf16[128,768]{1,0:T(8,128)(2,1)S(1)}, bf16[128,768]{1,0:T(8,128)(2,1)S(1)}, u32[]{:S(2)}, u32[]{:S(2)}) %collective-permute-start.12) | collective-permute-done | bytes 196640 | tf_op jit(solution)/shard_map/ppermute | solution.py:320
  44.9 1.9 %shard_map.94 = bf16[128,2688]{1,0:T(8,128)(2,1)} custom-call(s32[1]{0:T(128)S(6)} %copy.12.lengths, bf16[128,2688]{1,0:T(8,128)(2,1)} %get-tuple-element.27.so_far, bf16[2688,128]{1,0:T(8,128)(2,1)S(1)} %get-tuple-element.28.queries, f32[2688,128]{1,0:T(8,128)S(1)} %get-tuple-element.29.sums, ...), custom_call_target="tpu_custom_call", output_to_operand_aliasing={{}: (1, {})} | custom-call | flops 268435456 | bytes 2097152 | tf_op jit(solution)/shard_map/pallas_call | solution.py:273
  (4 shorter events, 0.1 us)
Async XLA Ops:
  0.7 1.4 %copy-start.4 = (bf16[1,128,768]{2,1,0:T(8,128)(2,1)S(1)}, bf16[1,128,768]{2,1,0:T(8,128)(2,1)}, u32[]{:S(2)}) copy-start(bf16[1,128,768]{2,1,0:T(8,128)(2,1)} %param.11) | copy-start | bytes 589828
  1.6 1.9 %collective-permute-start = (bf16[2,896,128]{2,1,0:T(8,128)(2,1)S(1)}, bf16[2,896,128]{2,1,0:T(8,128)(2,1)S(1)}, u32[]{:S(2)}, u32[]{:S(2)}) collective-permute-start(bf16[2,896,128]{2,1,0:T(8,128)(2,1)S(1)} %get-tuple-element.20), channel_id=1, source_target_pairs={{0,1},{1,0},{2,3},{3,2},{4,5},{5,4},{6,7},{7,6},{8,9},{9,8},{10,11... | collective-permute-start | bytes 1376264 | tf_op jit(solution)/shard_map/ppermute | solution.py:306
  1.6 4.5 %collective-permute-start.7 = (bf16[2,32,2688]{2,1,0:T(8,128)(2,1)S(1)}, bf16[2,32,2688]{2,1,0:T(8,128)(2,1)S(1)}, u32[]{:S(2)}, u32[]{:S(2)}) collective-permute-start(bf16[2,32,2688]{2,1,0:T(8,128)(2,1)S(1)} %get-tuple-element.25), channel_id=1, source_target_pairs={{0,1},{1,0},{2,3},{3,2},{4,5},{5,4},{6,7},{7,6},{8,9},{9,8},{10,11... | collective-permute-start | bytes 1032200 | tf_op jit(solution)/shard_map/ppermute | solution.py:307
  2.1 10.4 %collective-permute-start.2 = (bf16[128,768]{1,0:T(8,128)(2,1)S(1)}, bf16[128,768]{1,0:T(8,128)(2,1)S(1)}, u32[]{:S(2)}, u32[]{:S(2)}) collective-permute-start(bf16[128,768]{1,0:T(8,128)(2,1)S(1)} %bitcast.18), channel_id=1, source_target_pairs={{0,4},{4,0},{8,12},{12,8},{1,5},{5,1},{9,13},{13,9},{2,6},{6,2},{1... | collective-permute-start | bytes 589832 | tf_op jit(solution)/shard_map/ppermute | solution.py:78
  2.6 16.2 %collective-permute-start.5 = (bf16[128,768]{1,0:T(8,128)(2,1)S(1)}, bf16[128,768]{1,0:T(8,128)(2,1)S(1)}, u32[]{:S(2)}, u32[]{:S(2)}) collective-permute-start(bf16[128,768]{1,0:T(8,128)(2,1)S(1)} %bitcast.19), channel_id=1, source_target_pairs={{0,8},{4,12},{8,0},{12,4},{1,9},{5,13},{9,1},{13,5},{2,10},{6,14},... | collective-permute-start | bytes 589832 | tf_op jit(solution)/shard_map/ppermute | solution.py:78
  3.4 35.1 %copy-start = (bf16[1,128,3584]{2,1,0:T(8,128)(2,1)S(1)}, bf16[1,128,3584]{2,1,0:T(8,128)(2,1)}, u32[]{:S(2)}) copy-start(bf16[1,128,3584]{2,1,0:T(8,128)(2,1)} %param.9) | copy-start | bytes 2752516
  3.4 35.1 %copy-start.1 = (s32[4]{0:T(128)S(1)}, s32[4]{0:T(128)}, u32[]{:S(2)}) copy-start(s32[4]{0:T(128)} %ids.1) | copy-start | bytes 52
  3.4 35.1 %copy-start.2 = (s32[64]{0:T(128)S(1)}, s32[64]{0:T(128)}, u32[]{:S(2)}) copy-start(s32[64]{0:T(128)} %ranks.1) | copy-start | bytes 772
  3.5 9.0 %collective-permute-start.1 = (bf16[896,128]{1,0:T(8,128)(2,1)S(1)}, bf16[896,128]{1,0:T(8,128)(2,1)S(1)}, u32[]{:S(2)}, u32[]{:S(2)}) collective-permute-start(bf16[896,128]{1,0:T(8,128)(2,1)S(1)} %fusion), channel_id=1, source_target_pairs={{0,2},{1,3},{2,0},{3,1},{4,6},{5,7},{6,4},{7,5},{8,10},{9,11},{10,... | collective-permute-start | bytes 688136 | tf_op jit(solution)/shard_map/ppermute | solution.py:308
  6.1 10.2 %collective-permute-start.8 = (bf16[32,2688]{1,0:T(8,128)(2,1)S(1)}, bf16[32,2688]{1,0:T(8,128)(2,1)S(1)}, u32[]{:S(2)}, u32[]{:S(2)}) collective-permute-start(bf16[32,2688]{1,0:T(8,128)(2,1)S(1)} %fusion.3), channel_id=1, source_target_pairs={{0,2},{1,3},{2,0},{3,1},{4,6},{5,7},{6,4},{7,5},{8,10},{9,11},{10,... | collective-permute-start | bytes 516104 | tf_op jit(solution)/shard_map/ppermute | solution.py:309
  12.5 29.7 %copy-start.3 = (bf16[1,128,2688]{2,1,0:T(8,128)(2,1)S(1)}, bf16[1,128,2688]{2,1,0:T(8,128)(2,1)}, u32[]{:S(2)}) copy-start(bf16[1,128,2688]{2,1,0:T(8,128)(2,1)} %param.10) | copy-start | bytes 2064388
  12.6 13.8 %collective-permute-start.4 = (bf16[896,128]{1,0:T(8,128)(2,1)S(1)}, bf16[896,128]{1,0:T(8,128)(2,1)S(1)}, u32[]{:S(2)}, u32[]{:S(2)}) collective-permute-start(bf16[896,128]{1,0:T(8,128)(2,1)S(1)} %fusion.2.rest_0_), channel_id=1, source_target_pairs={{0,8},{4,12},{8,0},{12,4},{1,9},{5,13},{9,1},{13,5},{2,10},{6,14},... | collective-permute-start | bytes 688136 | tf_op jit(solution)/shard_map/ppermute | solution.py:78
  14.8 17.0 %collective-permute-start.3 = (bf16[896,128]{1,0:T(8,128)(2,1)S(1)}, bf16[896,128]{1,0:T(8,128)(2,1)S(1)}, u32[]{:S(2)}, u32[]{:S(2)}) collective-permute-start(bf16[896,128]{1,0:T(8,128)(2,1)S(1)} %fusion.2.rest_0_), channel_id=1, source_target_pairs={{0,4},{4,0},{8,12},{12,8},{1,5},{5,1},{9,13},{13,9},{2,6},{6,2},{1... | collective-permute-start | bytes 688136 | tf_op jit(solution)/shard_map/ppermute | solution.py:78
  16.4 15.3 %collective-permute-start.10 = (bf16[32,2688]{1,0:T(8,128)(2,1)S(1)}, bf16[32,2688]{1,0:T(8,128)(2,1)S(1)}, u32[]{:S(2)}, u32[]{:S(2)}) collective-permute-start(bf16[32,2688]{1,0:T(8,128)(2,1)S(1)} %fusion.5.rest_3_), channel_id=1, source_target_pairs={{0,8},{4,12},{8,0},{12,4},{1,9},{5,13},{9,1},{13,5},{2,10},{6,14},... | collective-permute-start | bytes 516104 | tf_op jit(solution)/shard_map/ppermute | solution.py:78
  17.3 16.3 %collective-permute-start.9 = (bf16[32,2688]{1,0:T(8,128)(2,1)S(1)}, bf16[32,2688]{1,0:T(8,128)(2,1)S(1)}, u32[]{:S(2)}, u32[]{:S(2)}) collective-permute-start(bf16[32,2688]{1,0:T(8,128)(2,1)S(1)} %fusion.5.rest_3_), channel_id=1, source_target_pairs={{0,4},{4,0},{8,12},{12,8},{1,5},{5,1},{9,13},{13,9},{2,6},{6,2},{1... | collective-permute-start | bytes 516104 | tf_op jit(solution)/shard_map/ppermute | solution.py:78
  26.4 12.1 %collective-permute-start.6 = (bf16[896,128]{1,0:T(8,128)(2,1)S(1)}, bf16[896,128]{1,0:T(8,128)(2,1)S(1)}, u32[]{:S(2)}, u32[]{:S(2)}) collective-permute-start(bf16[896,128]{1,0:T(8,128)(2,1)S(1)} %collective-permute-done.4.rest_2_), channel_id=1, source_target_pairs={{0,4},{4,0},{8,12},{12,8},{1,5},{5,1},{9,13},{13,9},{2,6},{6,2},{1... | collective-permute-start | bytes 688136 | tf_op jit(solution)/shard_map/ppermute | solution.py:316
  31.7 10.5 %collective-permute-start.11 = (bf16[32,2688]{1,0:T(8,128)(2,1)S(1)}, bf16[32,2688]{1,0:T(8,128)(2,1)S(1)}, u32[]{:S(2)}, u32[]{:S(2)}) collective-permute-start(bf16[32,2688]{1,0:T(8,128)(2,1)S(1)} %collective-permute-done.10.rest_5_), channel_id=1, source_target_pairs={{0,4},{4,0},{8,12},{12,8},{1,5},{5,1},{9,13},{13,9},{2,6},{6,2},{1... | collective-permute-start | bytes 516104 | tf_op jit(solution)/shard_map/ppermute | solution.py:318
  33.6 11.2 %collective-permute-start.12 = (bf16[128,768]{1,0:T(8,128)(2,1)S(1)}, bf16[128,768]{1,0:T(8,128)(2,1)S(1)}, u32[]{:S(2)}, u32[]{:S(2)}) collective-permute-start(bf16[128,768]{1,0:T(8,128)(2,1)S(1)} %collective-permute-done.5.rest_2_), channel_id=1, source_target_pairs={{0,0},{4,4},{8,12},{12,8},{1,1},{5,5},{9,13},{13,9},{2,2},{6,6},{1... | collective-permute-start | bytes 589832 | tf_op jit(solution)/shard_map/ppermute | solution.py:320

commit v11 on v2

--- a/solution.py
+++ b/solution.py
@@ -121,9 +121,15 @@
 
 
 def out_copies(result, out, sems):
-    width = GROUP * HD
     return [
-        pltpu.make_async_copy(result.at[h], out.at[:, pl.ds(h * width, width)], sems.at[h])
+        [
+            pltpu.make_async_copy(
+                result.at[h, :, pl.ds(g * HD, HD)],
+                out.at[:, pl.ds((h * GROUP + g) * HD, HD)],
+                sems.at[h * GROUP + g],
+            )
+            for g in range(GROUP)
+        ]
         for h in range(KVH)
     ]
 
@@ -141,7 +147,7 @@
     @pl.when(jnp.logical_not(live))
     def _():
         result[...] = jnp.zeros_like(result)
-        for copy in copies:
+        for copy in sum(copies, []):
             copy.start()
 
     @pl.when(live)
@@ -183,7 +189,7 @@
                         result[h, :, g * HD : (g + 1) * HD] = (
                             product[g * tokens : (g + 1) * tokens, :] / totals[g]
                         ).astype(jnp.bfloat16)
-                    copies[h].start()
+                        copies[h][g].start()
                 else:
                     sums[h * block : (h + 1) * block, :] = product
                     for g in range(GROUP):
@@ -193,7 +199,7 @@
 
     @pl.when(jnp.logical_not(live) | (z < 2))
     def _():
-        for copy in copies:
+        for copy in sum(copies, []):
             copy.wait()
 
 
@@ -212,7 +218,7 @@
         scratch_shapes=[
             VMEM((low.shape[1], width), jnp.bfloat16),
             VMEM((KVH, tokens, GROUP * HD), jnp.bfloat16),
-            pltpu.SemaphoreType.DMA((KVH,)),
+            pltpu.SemaphoreType.DMA((HEADS,)),
         ],
         compiler_params=PARAMS,
         cost_estimate=pl.CostEstimate(
@@ -250,8 +256,8 @@
                 at = slice(h * block + g * tokens, h * block + (g + 1) * tokens)
                 whole = sums[at, :] * factors[g] + product[g * tokens : (g + 1) * tokens, :]
                 result[h, :, g * HD : (g + 1) * HD] = (whole / totals[g]).astype(jnp.bfloat16)
-            copies[h].start()
-        for copy in copies:
+                copies[h][g].start()
+        for copy in sum(copies, []):
             copy.wait()
 
 
@@ -265,7 +271,7 @@
         input_output_aliases={1: 0},
         scratch_shapes=[
             VMEM((KVH, tokens, GROUP * HD), jnp.bfloat16),
-            pltpu.SemaphoreType.DMA((KVH,)),
+            pltpu.SemaphoreType.DMA((HEADS,)),
         ],
         compiler_params=PARAMS,
         cost_estimate=pl.CostEstimate(

time: 47.4 us -> 47.6 us (level)
  transfers between devices with their start and end apart: 13 -> 13, of which waited for: 7 -> 7; matrix products, arithmetic and copies ran while one was open for 0% -> 0% of each run, Pallas kernels for 5% -> 6%
where the time goes in v11:
time: 47.6 us; the launch traced here: 46.7 us
  waiting for transfers between devices  21.3 us (45%)
  starting transfers between devices  17.4 us (37%)
  Pallas kernels  6.42 us (13%)
  other arithmetic  0.89 us (2%)
  between operations  0.73 us (2%)
    ppermute x6, waiting for transfers between devices, spread(): return (lax.ppermute(shard, 'ctx', ONE), lax.ppermute(shard, 'ctx', TWO))  10.7 us
    ppermute x6, starting transfers between devices, spread(): return (lax.ppermute(shard, 'ctx', ONE), lax.ppermute(shard, 'ctx', TWO))  7.12 us
    ppermute x1, waiting for transfers between devices, body(): far_down = lax.ppermute(keep_down[1] + near_down[1], 'req', ACROSS)  6.41 us
    ppermute x1, starting transfers between devices, body(): kv_three = lax.ppermute(kv_last, 'ctx', LAST)  2.87 us
    ppermute x1, waiting for transfers between devices, body(): up_three = lax.ppermute(up_two, 'ctx', ONE)  2.7 us
    ppermute x1, starting transfers between devices, body(): down_three = lax.ppermute(down_two, 'ctx', ONE)  2.36 us
    ppermute x1, starting transfers between devices, body(): up_three = lax.ppermute(up_two, 'ctx', ONE)  2.3 us
    pallas_call x1, Pallas kernels, finish(): pl.pallas_call(finish_kernel, out_shape=jax.ShapeDtypeStruct(so_far.shape...  1.92 us
  transfers between devices with their start and end apart: 13, of which 7 were waited for; matrix products, arithmetic and copies ran while one was open for 0% of the time, Pallas kernels for 6%

profile of v11, /device:TPU:18, one launch (start us, length us, event | category | flops | bytes accessed | tf_op | source)
XLA Modules:
  0.0 46.7 jit_solution(12298648446943791750)
XLA Ops:
  0.0 0.7 %pad_add_fusion.table = s32[68]{0:T(128)S(1)} fusion(s32[64]{0:T(128)} %param.15, s32[4]{0:T(128)} %ids.1), kind=kLoop, calls=%fused_computation.10 | loop fusion | flops 68 | bytes 544 | tf_op jit(solution)/shard_map/concatenate | solution.py:67
  0.7 0.0 copy-start.4
  0.7 1.9 %shard_map.91 = (bf16[2,896,128]{2,1,0:T(8,128)(2,1)S(1)}, bf16[2,896,128]{2,1,0:T(8,128)(2,1)S(1)}, bf16[2,32,2688]{2,1,0:T(8,128)(2,1)S(1)}, bf16[2,32,2688]{2,1,0:T(8,128)(2,1)S(1)}) custom-call(s32[68]{0:T(128)S(1)} %pad_add_fusion.table, bf16[16,896,128]{2,1,0:T(8,128)(2,1)} %rest_0_.1, bf16[16,32,2688]{2,1,0:T(8,128)(2,1)} %rest_1_.1), custom_call_target="tpu_custom_call" | custom-call | tf_op jit(solution)/shard_map/pallas_call | solution.py:60
  2.6 0.1 collective-permute-start
  2.7 0.5 %collective-permute-start.7 = (bf16[2,32,2688]{2,1,0:T(8,128)(2,1)S(1)}, bf16[2,32,2688]{2,1,0:T(8,128)(2,1)S(1)}, u32[]{:S(2)}, u32[]{:S(2)}) collective-permute-start(bf16[2,32,2688]{2,1,0:T(8,128)(2,1)S(1)} %get-tuple-element.25), channel_id=1, source_target_pairs={{0,1},{1,0},{2,3},{3,2},{4,5},{5,4},{6,7},{7,6},{8,9},{9,8},{10,11... | collective-permute-start | bytes 1032200 | tf_op jit(solution)/shard_map/ppermute | solution.py:300
  3.2 0.0 copy-done.4
  3.2 1.6 %collective-permute-start.2 = (bf16[128,768]{1,0:T(8,128)(2,1)S(1)}, bf16[128,768]{1,0:T(8,128)(2,1)S(1)}, u32[]{:S(2)}, u32[]{:S(2)}) collective-permute-start(bf16[128,768]{1,0:T(8,128)(2,1)S(1)} %bitcast.18), channel_id=1, source_target_pairs={{0,4},{4,0},{8,12},{12,8},{1,5},{5,1},{9,13},{13,9},{2,6},{6,2},{1... | collective-permute-start | bytes 589832 | tf_op jit(solution)/shard_map/ppermute | solution.py:78
  4.8 0.3 collective-permute-start.5
  5.1 0.0 collective-permute-done
  5.1 0.0 copy-start
  5.1 0.0 copy-start.1
  5.1 0.0 copy-start.2
  5.2 0.4 collective-permute-start.1
  5.6 0.0 collective-permute-done.7
  5.6 1.8 %collective-permute-start.8 = (bf16[32,2688]{1,0:T(8,128)(2,1)S(1)}, bf16[32,2688]{1,0:T(8,128)(2,1)S(1)}, u32[]{:S(2)}, u32[]{:S(2)}) collective-permute-start(bf16[32,2688]{1,0:T(8,128)(2,1)S(1)} %fusion.3), channel_id=1, source_target_pairs={{0,2},{1,3},{2,0},{3,1},{4,6},{5,7},{6,4},{7,5},{8,10},{9,11},{10,... | collective-permute-start | bytes 516104 | tf_op jit(solution)/shard_map/ppermute | solution.py:302
  7.3 6.4 %collective-permute-done.1 = bf16[896,128]{1,0:T(8,128)(2,1)S(1)} collective-permute-done((bf16[896,128]{1,0:T(8,128)(2,1)S(1)}, bf16[896,128]{1,0:T(8,128)(2,1)S(1)}, u32[]{:S(2)}, u32[]{:S(2)}) %collective-permute-start.1) | collective-permute-done | bytes 229408 | tf_op jit(solution)/shard_map/ppermute | solution.py:301
  13.8 0.0 copy-start.3
  13.8 0.0 collective-permute-done.2.rest_1_
  13.8 2.7 %collective-permute-start.4 = (bf16[896,128]{1,0:T(8,128)(2,1)S(1)}, bf16[896,128]{1,0:T(8,128)(2,1)S(1)}, u32[]{:S(2)}, u32[]{:S(2)}) collective-permute-start(bf16[896,128]{1,0:T(8,128)(2,1)S(1)} %fusion.2.rest_0_), channel_id=1, source_target_pairs={{0,8},{4,12},{8,0},{12,4},{1,9},{5,13},{9,1},{13,5},{2,10},{6,14},... | collective-permute-start | bytes 688136 | tf_op jit(solution)/shard_map/ppermute | solution.py:78
  16.5 0.4 collective-permute-start.3
  16.9 0.0 collective-permute-done.8
  17.0 1.7 %collective-permute-start.10 = (bf16[32,2688]{1,0:T(8,128)(2,1)S(1)}, bf16[32,2688]{1,0:T(8,128)(2,1)S(1)}, u32[]{:S(2)}, u32[]{:S(2)}) collective-permute-start(bf16[32,2688]{1,0:T(8,128)(2,1)S(1)} %fusion.5.rest_3_), channel_id=1, source_target_pairs={{0,8},{4,12},{8,0},{12,4},{1,9},{5,13},{9,1},{13,5},{2,10},{6,14},... | collective-permute-start | bytes 516104 | tf_op jit(solution)/shard_map/ppermute | solution.py:78
  18.6 0.4 collective-permute-start.9
  19.1 0.0 collective-permute-done.5.rest_2_
  19.1 7.8 %collective-permute-done.4.rest_2_ = bf16[896,128]{1,0:T(8,128)(2,1)S(1)} collective-permute-done((bf16[896,128]{1,0:T(8,128)(2,1)S(1)}, bf16[896,128]{1,0:T(8,128)(2,1)S(1)}, u32[]{:S(2)}, u32[]{:S(2)}) %collective-permute-start.4) | collective-permute-done | bytes 229408 | tf_op jit(solution)/shard_map/ppermute | solution.py:78
  26.9 2.4 %collective-permute-start.6 = (bf16[896,128]{1,0:T(8,128)(2,1)S(1)}, bf16[896,128]{1,0:T(8,128)(2,1)S(1)}, u32[]{:S(2)}, u32[]{:S(2)}) collective-permute-start(bf16[896,128]{1,0:T(8,128)(2,1)S(1)} %collective-permute-done.4.rest_2_), channel_id=1, source_target_pairs={{0,4},{4,0},{8,12},{12,8},{1,5},{5,1},{9,13},{13,9},{2,6},{6,2},{1... | collective-permute-start | bytes 688136 | tf_op jit(solution)/shard_map/ppermute | solution.py:309
  29.2 2.8 %collective-permute-done.10.rest_5_ = bf16[32,2688]{1,0:T(8,128)(2,1)S(1)} collective-permute-done((bf16[32,2688]{1,0:T(8,128)(2,1)S(1)}, bf16[32,2688]{1,0:T(8,128)(2,1)S(1)}, u32[]{:S(2)}, u32[]{:S(2)}) %collective-permute-start.10) | collective-permute-done | bytes 172064 | tf_op jit(solution)/shard_map/ppermute | solution.py:78
  32.0 0.0 collective-permute-done.3.rest_1_
  32.0 2.3 %collective-permute-start.11 = (bf16[32,2688]{1,0:T(8,128)(2,1)S(1)}, bf16[32,2688]{1,0:T(8,128)(2,1)S(1)}, u32[]{:S(2)}, u32[]{:S(2)}) collective-permute-start(bf16[32,2688]{1,0:T(8,128)(2,1)S(1)} %collective-permute-done.10.rest_5_), channel_id=1, source_target_pairs={{0,4},{4,0},{8,12},{12,8},{1,5},{5,1},{9,13},{13,9},{2,6},{6,2},{1... | collective-permute-start | bytes 516104 | tf_op jit(solution)/shard_map/ppermute | solution.py:311
  34.3 0.2 collective-permute-done.9.rest_4_
  34.5 2.9 %collective-permute-start.12 = (bf16[128,768]{1,0:T(8,128)(2,1)S(1)}, bf16[128,768]{1,0:T(8,128)(2,1)S(1)}, u32[]{:S(2)}, u32[]{:S(2)}) collective-permute-start(bf16[128,768]{1,0:T(8,128)(2,1)S(1)} %collective-permute-done.5.rest_2_), channel_id=1, source_target_pairs={{0,0},{4,4},{8,12},{12,8},{1,1},{5,5},{9,13},{13,9},{2,2},{6,6},{1... | collective-permute-start | bytes 589832 | tf_op jit(solution)/shard_map/ppermute | solution.py:313
  38.0 1.1 %collective-permute-done.6.rest_3_ = bf16[896,128]{1,0:T(8,128)(2,1)S(1)} collective-permute-done((bf16[896,128]{1,0:T(8,128)(2,1)S(1)}, bf16[896,128]{1,0:T(8,128)(2,1)S(1)}, u32[]{:S(2)}, u32[]{:S(2)}) %collective-permute-start.6) | collective-permute-done | bytes 229408 | tf_op jit(solution)/shard_map/ppermute | solution.py:309
  39.1 0.0 copy-done
  39.1 0.0 copy-done.1
  39.1 0.0 copy-done.2
  39.1 0.9 %shard_map.92.low = bf16[128,128]{1,0:T(8,128)(2,1)S(1)} custom-call(s32[4]{0:T(128)S(1)} %copy-done.1, s32[64]{0:T(128)S(1)} %copy-done.2, bf16[128,3584]{1,0:T(8,128)(2,1)S(1)} %bitcast.16, bf16[896,128]{1,0:T(8,128)(2,1)S(1)} %fusion.2.rest_0_, bf16[896,128]{1,0:T(8,128)(2,1)S(1)} %collective-permute-done.3.rest_1_, ...), custom_call_target="tpu_custom_call" | custom-call | flops 134217728 | bytes 4194304 | tf_op jit(solution)/shard_map/pallas_call | solution.py:97
  40.0 2.7 %collective-permute-done.11.rest_6_ = bf16[32,2688]{1,0:T(8,128)(2,1)S(1)} collective-permute-done((bf16[32,2688]{1,0:T(8,128)(2,1)S(1)}, bf16[32,2688]{1,0:T(8,128)(2,1)S(1)}, u32[]{:S(2)}, u32[]{:S(2)}) %collective-permute-start.11) | collective-permute-done | bytes 172064 | tf_op jit(solution)/shard_map/ppermute | solution.py:311
  42.7 0.0 copy-done.3
  42.7 1.7 %shard_map.93 = (bf16[128,2688]{1,0:T(8,128)(2,1)}, bf16[2688,128]{1,0:T(8,128)(2,1)S(1)}, f32[2688,128]{1,0:T(8,128)S(1)}, f32[2688,128]{1,0:T(8,128)S(1)}, f32[2688,128]{1,0:T(8,128)S(1)}) custom-call(s32[1]{0:T(128)S(6)} %copy.12.lengths, bf16[128,2688]{1,0:T(8,128)(2,1)S(1)} %bitcast.17, bf16[128,128]{1,0:T(8,128)(2,1)S(1)} %shard_map.92.low, ...), custom_call_target="tpu_custom_call" | custom-call | flops 1073741824 | bytes 4194304 | tf_op jit(solution)/shard_map/pallas_call | solution.py:213
  44.4 0.4 collective-permute-done.12.kv
  44.8 1.9 %shard_map.94 = bf16[128,2688]{1,0:T(8,128)(2,1)} custom-call(s32[1]{0:T(128)S(6)} %copy.12.lengths, bf16[128,2688]{1,0:T(8,128)(2,1)} %get-tuple-element.27.so_far, bf16[2688,128]{1,0:T(8,128)(2,1)S(1)} %get-tuple-element.28.queries, f32[2688,128]{1,0:T(8,128)S(1)} %get-tuple-element.29.sums, ...), custom_call_target="tpu_custom_call", output_to_operand_aliasing={{}: (1, {})} | custom-call | flops 268435456 | bytes 2097152 | tf_op jit(solution)/shard_map/pallas_call | solution.py:266
  (4 shorter events, 0.1 us)
Async XLA Ops:
  0.7 2.4 %copy-start.4 = (bf16[1,128,768]{2,1,0:T(8,128)(2,1)S(1)}, bf16[1,128,768]{2,1,0:T(8,128)(2,1)}, u32[]{:S(2)}) copy-start(bf16[1,128,768]{2,1,0:T(8,128)(2,1)} %param.11) | copy-start | bytes 589828
  2.6 2.5 %collective-permute-start = (bf16[2,896,128]{2,1,0:T(8,128)(2,1)S(1)}, bf16[2,896,128]{2,1,0:T(8,128)(2,1)S(1)}, u32[]{:S(2)}, u32[]{:S(2)}) collective-permute-start(bf16[2,896,128]{2,1,0:T(8,128)(2,1)S(1)} %get-tuple-element.20), channel_id=1, source_target_pairs={{0,1},{1,0},{2,3},{3,2},{4,5},{5,4},{6,7},{7,6},{8,9},{9,8},{10,11... | collective-permute-start | bytes 1376264 | tf_op jit(solution)/shard_map/ppermute | solution.py:299
  2.7 2.9 %collective-permute-start.7 = (bf16[2,32,2688]{2,1,0:T(8,128)(2,1)S(1)}, bf16[2,32,2688]{2,1,0:T(8,128)(2,1)S(1)}, u32[]{:S(2)}, u32[]{:S(2)}) collective-permute-start(bf16[2,32,2688]{2,1,0:T(8,128)(2,1)S(1)} %get-tuple-element.25), channel_id=1, source_target_pairs={{0,1},{1,0},{2,3},{3,2},{4,5},{5,4},{6,7},{7,6},{8,9},{9,8},{10,11... | collective-permute-start | bytes 1032200 | tf_op jit(solution)/shard_map/ppermute | solution.py:300
  3.2 10.6 %collective-permute-start.2 = (bf16[128,768]{1,0:T(8,128)(2,1)S(1)}, bf16[128,768]{1,0:T(8,128)(2,1)S(1)}, u32[]{:S(2)}, u32[]{:S(2)}) collective-permute-start(bf16[128,768]{1,0:T(8,128)(2,1)S(1)} %bitcast.18), channel_id=1, source_target_pairs={{0,4},{4,0},{8,12},{12,8},{1,5},{5,1},{9,13},{13,9},{2,6},{6,2},{1... | collective-permute-start | bytes 589832 | tf_op jit(solution)/shard_map/ppermute | solution.py:78
  4.8 14.3 %collective-permute-start.5 = (bf16[128,768]{1,0:T(8,128)(2,1)S(1)}, bf16[128,768]{1,0:T(8,128)(2,1)S(1)}, u32[]{:S(2)}, u32[]{:S(2)}) collective-permute-start(bf16[128,768]{1,0:T(8,128)(2,1)S(1)} %bitcast.19), channel_id=1, source_target_pairs={{0,8},{4,12},{8,0},{12,4},{1,9},{5,13},{9,1},{13,5},{2,10},{6,14},... | collective-permute-start | bytes 589832 | tf_op jit(solution)/shard_map/ppermute | solution.py:78
  5.1 34.0 %copy-start = (bf16[1,128,3584]{2,1,0:T(8,128)(2,1)S(1)}, bf16[1,128,3584]{2,1,0:T(8,128)(2,1)}, u32[]{:S(2)}) copy-start(bf16[1,128,3584]{2,1,0:T(8,128)(2,1)} %param.9) | copy-start | bytes 2752516
  5.1 34.0 %copy-start.1 = (s32[4]{0:T(128)S(1)}, s32[4]{0:T(128)}, u32[]{:S(2)}) copy-start(s32[4]{0:T(128)} %ids.1) | copy-start | bytes 52
  5.1 34.0 %copy-start.2 = (s32[64]{0:T(128)S(1)}, s32[64]{0:T(128)}, u32[]{:S(2)}) copy-start(s32[64]{0:T(128)} %ranks.1) | copy-start | bytes 772
  5.2 8.6 %collective-permute-start.1 = (bf16[896,128]{1,0:T(8,128)(2,1)S(1)}, bf16[896,128]{1,0:T(8,128)(2,1)S(1)}, u32[]{:S(2)}, u32[]{:S(2)}) collective-permute-start(bf16[896,128]{1,0:T(8,128)(2,1)S(1)} %fusion), channel_id=1, source_target_pairs={{0,2},{1,3},{2,0},{3,1},{4,6},{5,7},{6,4},{7,5},{8,10},{9,11},{10,... | collective-permute-start | bytes 688136 | tf_op jit(solution)/shard_map/ppermute | solution.py:301
  5.6 11.3 %collective-permute-start.8 = (bf16[32,2688]{1,0:T(8,128)(2,1)S(1)}, bf16[32,2688]{1,0:T(8,128)(2,1)S(1)}, u32[]{:S(2)}, u32[]{:S(2)}) collective-permute-start(bf16[32,2688]{1,0:T(8,128)(2,1)S(1)} %fusion.3), channel_id=1, source_target_pairs={{0,2},{1,3},{2,0},{3,1},{4,6},{5,7},{6,4},{7,5},{8,10},{9,11},{10,... | collective-permute-start | bytes 516104 | tf_op jit(solution)/shard_map/ppermute | solution.py:302
  13.8 28.9 %copy-start.3 = (bf16[1,128,2688]{2,1,0:T(8,128)(2,1)S(1)}, bf16[1,128,2688]{2,1,0:T(8,128)(2,1)}, u32[]{:S(2)}) copy-start(bf16[1,128,2688]{2,1,0:T(8,128)(2,1)} %param.10) | copy-start | bytes 2064388
  13.8 13.0 %collective-permute-start.4 = (bf16[896,128]{1,0:T(8,128)(2,1)S(1)}, bf16[896,128]{1,0:T(8,128)(2,1)S(1)}, u32[]{:S(2)}, u32[]{:S(2)}) collective-permute-start(bf16[896,128]{1,0:T(8,128)(2,1)S(1)} %fusion.2.rest_0_), channel_id=1, source_target_pairs={{0,8},{4,12},{8,0},{12,4},{1,9},{5,13},{9,1},{13,5},{2,10},{6,14},... | collective-permute-start | bytes 688136 | tf_op jit(solution)/shard_map/ppermute | solution.py:78
  16.5 15.5 %collective-permute-start.3 = (bf16[896,128]{1,0:T(8,128)(2,1)S(1)}, bf16[896,128]{1,0:T(8,128)(2,1)S(1)}, u32[]{:S(2)}, u32[]{:S(2)}) collective-permute-start(bf16[896,128]{1,0:T(8,128)(2,1)S(1)} %fusion.2.rest_0_), channel_id=1, source_target_pairs={{0,4},{4,0},{8,12},{12,8},{1,5},{5,1},{9,13},{13,9},{2,6},{6,2},{1... | collective-permute-start | bytes 688136 | tf_op jit(solution)/shard_map/ppermute | solution.py:78
  17.0 15.0 %collective-permute-start.10 = (bf16[32,2688]{1,0:T(8,128)(2,1)S(1)}, bf16[32,2688]{1,0:T(8,128)(2,1)S(1)}, u32[]{:S(2)}, u32[]{:S(2)}) collective-permute-start(bf16[32,2688]{1,0:T(8,128)(2,1)S(1)} %fusion.5.rest_3_), channel_id=1, source_target_pairs={{0,8},{4,12},{8,0},{12,4},{1,9},{5,13},{9,1},{13,5},{2,10},{6,14},... | collective-permute-start | bytes 516104 | tf_op jit(solution)/shard_map/ppermute | solution.py:78
  18.6 15.8 %collective-permute-start.9 = (bf16[32,2688]{1,0:T(8,128)(2,1)S(1)}, bf16[32,2688]{1,0:T(8,128)(2,1)S(1)}, u32[]{:S(2)}, u32[]{:S(2)}) collective-permute-start(bf16[32,2688]{1,0:T(8,128)(2,1)S(1)} %fusion.5.rest_3_), channel_id=1, source_target_pairs={{0,4},{4,0},{8,12},{12,8},{1,5},{5,1},{9,13},{13,9},{2,6},{6,2},{1... | collective-permute-start | bytes 516104 | tf_op jit(solution)/shard_map/ppermute | solution.py:78
  26.9 12.2 %collective-permute-start.6 = (bf16[896,128]{1,0:T(8,128)(2,1)S(1)}, bf16[896,128]{1,0:T(8,128)(2,1)S(1)}, u32[]{:S(2)}, u32[]{:S(2)}) collective-permute-start(bf16[896,128]{1,0:T(8,128)(2,1)S(1)} %collective-permute-done.4.rest_2_), channel_id=1, source_target_pairs={{0,4},{4,0},{8,12},{12,8},{1,5},{5,1},{9,13},{13,9},{2,6},{6,2},{1... | collective-permute-start | bytes 688136 | tf_op jit(solution)/shard_map/ppermute | solution.py:309
  32.0 10.7 %collective-permute-start.11 = (bf16[32,2688]{1,0:T(8,128)(2,1)S(1)}, bf16[32,2688]{1,0:T(8,128)(2,1)S(1)}, u32[]{:S(2)}, u32[]{:S(2)}) collective-permute-start(bf16[32,2688]{1,0:T(8,128)(2,1)S(1)} %collective-permute-done.10.rest_5_), channel_id=1, source_target_pairs={{0,4},{4,0},{8,12},{12,8},{1,5},{5,1},{9,13},{13,9},{2,6},{6,2},{1... | collective-permute-start | bytes 516104 | tf_op jit(solution)/shard_map/ppermute | solution.py:311
  34.5 10.4 %collective-permute-start.12 = (bf16[128,768]{1,0:T(8,128)(2,1)S(1)}, bf16[128,768]{1,0:T(8,128)(2,1)S(1)}, u32[]{:S(2)}, u32[]{:S(2)}) collective-permute-start(bf16[128,768]{1,0:T(8,128)(2,1)S(1)} %collective-permute-done.5.rest_2_), channel_id=1, source_target_pairs={{0,0},{4,4},{8,12},{12,8},{1,1},{5,5},{9,13},{13,9},{2,2},{6,6},{1... | collective-permute-start | bytes 589832 | tf_op jit(solution)/shard_map/ppermute | solution.py:313

commit v12 on v2

--- a/solution.py
+++ b/solution.py
@@ -303,10 +303,12 @@
     down_three = lax.ppermute(down_two, "ctx", ONE)
     up_two = lax.optimization_barrier((up_two, down_one))[0]
     up_three = lax.ppermute(up_two, "ctx", ONE)
-    kv_last = lax.optimization_barrier((kv_two, up_two, up_one))[0]
+    kv_last = lax.optimization_barrier((kv_two, up_two))[0]
     kv_three = lax.ppermute(kv_last, "ctx", LAST)
     downs = [down, down_one, down_two, down_three]
     ups = [up, up_one, up_two, up_three]
+    down_three, up_one = lax.optimization_barrier((down_three, up_one))
+    downs[3], ups[1] = down_three, up_one
     low = low_rank(adapter_ids, rank_buckets, hidden_states[0], downs)
     parts = attend(lengths, queries_base[0], low, [kv, kv_one, kv_two], ups)
     return finish(lengths, *parts, kv_three)[None]

time: 47.4 us -> 51 us (1.076)
  the two profiles are of different devices: /device:TPU:18 before, /device:TPU:30 now
where the time goes in v12:
time: 51 us; the launch traced here: 50.8 us
  waiting for transfers between devices  29.2 us (57%)
  starting transfers between devices  14.5 us (28%)
  Pallas kernels  5.55 us (11%)
  other arithmetic  0.89 us (2%)
  between operations  0.72 us (1%)
    ppermute x6, waiting for transfers between devices, spread(): return (lax.ppermute(shard, 'ctx', ONE), lax.ppermute(shard, 'ctx', TWO))  17.4 us
    ppermute x6, starting transfers between devices, spread(): return (lax.ppermute(shard, 'ctx', ONE), lax.ppermute(shard, 'ctx', TWO))  7.22 us
    ppermute x1, waiting for transfers between devices, body(): far_down = lax.ppermute(keep_down[1] + near_down[1], 'req', ACROSS)  6.3 us
    ppermute x1, starting transfers between devices, body(): kv_three = lax.ppermute(kv_last, 'ctx', LAST)  3.92 us
    ppermute x1, waiting for transfers between devices, body(): up_three = lax.ppermute(up_two, 'ctx', ONE)  2.72 us
    ppermute x1, waiting for transfers between devices, body(): kv_three = lax.ppermute(kv_last, 'ctx', LAST)  2.15 us
    pallas_call x1, Pallas kernels, attend(): pl.pallas_call(attend_kernel, out_shape=shapes, in_specs=[spec(SMEM)] + [...  1.97 us
    pallas_call x1, Pallas kernels, finish(): pl.pallas_call(finish_kernel, out_shape=jax.ShapeDtypeStruct(so_far.shape...  1.83 us
  transfers between devices with their start and end apart: 13, of which 9 were waited for; matrix products, arithmetic and copies ran while one was open for 0% of the time, Pallas kernels for 6%

profile of v12, /device:TPU:30, one launch (start us, length us, event | category | flops | bytes accessed | tf_op | source)
XLA Modules:
  0.0 50.8 jit_solution(10503801765349533973)
XLA Ops:
  0.0 0.7 %pad_add_fusion.table = s32[68]{0:T(128)S(1)} fusion(s32[64]{0:T(128)} %param.15, s32[4]{0:T(128)} %ids.1), kind=kLoop, calls=%fused_computation.10 | loop fusion | flops 68 | bytes 544 | tf_op jit(solution)/shard_map/concatenate | solution.py:67
  0.7 0.0 copy-start.4
  0.7 0.8 %shard_map.91 = (bf16[2,896,128]{2,1,0:T(8,128)(2,1)S(1)}, bf16[2,896,128]{2,1,0:T(8,128)(2,1)S(1)}, bf16[2,32,2688]{2,1,0:T(8,128)(2,1)S(1)}, bf16[2,32,2688]{2,1,0:T(8,128)(2,1)S(1)}) custom-call(s32[68]{0:T(128)S(1)} %pad_add_fusion.table, bf16[16,896,128]{2,1,0:T(8,128)(2,1)} %rest_0_.1, bf16[16,32,2688]{2,1,0:T(8,128)(2,1)} %rest_1_.1), custom_call_target="tpu_custom_call" | custom-call | tf_op jit(solution)/shard_map/pallas_call | solution.py:60
  1.6 1.1 %collective-permute-start = (bf16[2,896,128]{2,1,0:T(8,128)(2,1)S(1)}, bf16[2,896,128]{2,1,0:T(8,128)(2,1)S(1)}, u32[]{:S(2)}, u32[]{:S(2)}) collective-permute-start(bf16[2,896,128]{2,1,0:T(8,128)(2,1)S(1)} %get-tuple-element.22), channel_id=1, source_target_pairs={{0,1},{1,0},{2,3},{3,2},{4,5},{5,4},{6,7},{7,6},{8,9},{9,8},{10,11... | collective-permute-start | bytes 1376264 | tf_op jit(solution)/shard_map/ppermute | solution.py:293
  2.6 0.1 collective-permute-start.7
  2.7 0.0 copy-done.4
  2.7 0.4 collective-permute-start.2
  3.2 0.3 collective-permute-start.5
  3.5 0.6 %collective-permute-done = bf16[2,896,128]{2,1,0:T(8,128)(2,1)S(1)} collective-permute-done((bf16[2,896,128]{2,1,0:T(8,128)(2,1)S(1)}, bf16[2,896,128]{2,1,0:T(8,128)(2,1)S(1)}, u32[]{:S(2)}, u32[]{:S(2)}) %collective-permute-start) | collective-permute-done | bytes 458784 | tf_op jit(solution)/shard_map/ppermute | solution.py:293
  4.1 0.0 copy-start
  4.1 0.0 copy-start.1
  4.1 0.0 copy-start.2
  4.1 0.8 %collective-permute-start.1 = (bf16[896,128]{1,0:T(8,128)(2,1)S(1)}, bf16[896,128]{1,0:T(8,128)(2,1)S(1)}, u32[]{:S(2)}, u32[]{:S(2)}) collective-permute-start(bf16[896,128]{1,0:T(8,128)(2,1)S(1)} %fusion), channel_id=1, source_target_pairs={{0,2},{1,3},{2,0},{3,1},{4,6},{5,7},{6,4},{7,5},{8,10},{9,11},{10,... | collective-permute-start | bytes 688136 | tf_op jit(solution)/shard_map/ppermute | solution.py:295
  4.9 0.0 collective-permute-done.7
  5.0 1.4 %collective-permute-start.8 = (bf16[32,2688]{1,0:T(8,128)(2,1)S(1)}, bf16[32,2688]{1,0:T(8,128)(2,1)S(1)}, u32[]{:S(2)}, u32[]{:S(2)}) collective-permute-start(bf16[32,2688]{1,0:T(8,128)(2,1)S(1)} %fusion.3), channel_id=1, source_target_pairs={{0,2},{1,3},{2,0},{3,1},{4,6},{5,7},{6,4},{7,5},{8,10},{9,11},{10,... | collective-permute-start | bytes 516104 | tf_op jit(solution)/shard_map/ppermute | solution.py:296
  6.3 6.3 %collective-permute-done.1 = bf16[896,128]{1,0:T(8,128)(2,1)S(1)} collective-permute-done((bf16[896,128]{1,0:T(8,128)(2,1)S(1)}, bf16[896,128]{1,0:T(8,128)(2,1)S(1)}, u32[]{:S(2)}, u32[]{:S(2)}) %collective-permute-start.1) | collective-permute-done | bytes 229408 | tf_op jit(solution)/shard_map/ppermute | solution.py:295
  12.7 0.0 copy-start.3
  12.7 0.3 collective-permute-done.2.rest_1_
  12.9 1.9 %collective-permute-start.4 = (bf16[896,128]{1,0:T(8,128)(2,1)S(1)}, bf16[896,128]{1,0:T(8,128)(2,1)S(1)}, u32[]{:S(2)}, u32[]{:S(2)}) collective-permute-start(bf16[896,128]{1,0:T(8,128)(2,1)S(1)} %fusion.2.rest_0_), channel_id=1, source_target_pairs={{0,8},{4,12},{8,0},{12,4},{1,9},{5,13},{9,1},{13,5},{2,10},{6,14},... | collective-permute-start | bytes 688136 | tf_op jit(solution)/shard_map/ppermute | solution.py:78
  14.8 1.6 %collective-permute-start.3 = (bf16[896,128]{1,0:T(8,128)(2,1)S(1)}, bf16[896,128]{1,0:T(8,128)(2,1)S(1)}, u32[]{:S(2)}, u32[]{:S(2)}) collective-permute-start(bf16[896,128]{1,0:T(8,128)(2,1)S(1)} %fusion.2.rest_0_), channel_id=1, source_target_pairs={{0,4},{4,0},{8,12},{12,8},{1,5},{5,1},{9,13},{13,9},{2,6},{6,2},{1... | collective-permute-start | bytes 688136 | tf_op jit(solution)/shard_map/ppermute | solution.py:78
  16.4 0.0 collective-permute-done.8
  16.4 0.9 %collective-permute-start.10 = (bf16[32,2688]{1,0:T(8,128)(2,1)S(1)}, bf16[32,2688]{1,0:T(8,128)(2,1)S(1)}, u32[]{:S(2)}, u32[]{:S(2)}) collective-permute-start(bf16[32,2688]{1,0:T(8,128)(2,1)S(1)} %fusion.5.rest_3_), channel_id=1, source_target_pairs={{0,8},{4,12},{8,0},{12,4},{1,9},{5,13},{9,1},{13,5},{2,10},{6,14},... | collective-permute-start | bytes 516104 | tf_op jit(solution)/shard_map/ppermute | solution.py:78
  17.4 0.4 collective-permute-done.5.rest_2_
  17.8 11.0 %collective-permute-done.4.rest_2_ = bf16[896,128]{1,0:T(8,128)(2,1)S(1)} collective-permute-done((bf16[896,128]{1,0:T(8,128)(2,1)S(1)}, bf16[896,128]{1,0:T(8,128)(2,1)S(1)}, u32[]{:S(2)}, u32[]{:S(2)}) %collective-permute-start.4) | collective-permute-done | bytes 229408 | tf_op jit(solution)/shard_map/ppermute | solution.py:78
  28.9 0.0 collective-permute-start.6
  28.9 2.0 %collective-permute-start.9 = (bf16[32,2688]{1,0:T(8,128)(2,1)S(1)}, bf16[32,2688]{1,0:T(8,128)(2,1)S(1)}, u32[]{:S(2)}, u32[]{:S(2)}) collective-permute-start(bf16[32,2688]{1,0:T(8,128)(2,1)S(1)} %fusion.5.rest_3_), channel_id=1, source_target_pairs={{0,4},{4,0},{8,12},{12,8},{1,5},{5,1},{9,13},{13,9},{2,6},{6,2},{1... | collective-permute-start | bytes 516104 | tf_op jit(solution)/shard_map/ppermute | solution.py:78
  30.9 1.7 %collective-permute-done.10.rest_5_ = bf16[32,2688]{1,0:T(8,128)(2,1)S(1)} collective-permute-done((bf16[32,2688]{1,0:T(8,128)(2,1)S(1)}, bf16[32,2688]{1,0:T(8,128)(2,1)S(1)}, u32[]{:S(2)}, u32[]{:S(2)}) %collective-permute-start.10) | collective-permute-done | bytes 172064 | tf_op jit(solution)/shard_map/ppermute | solution.py:78
  32.6 0.0 collective-permute-done.3.rest_1_
  32.6 0.0 collective-permute-start.11
  32.6 3.9 %collective-permute-start.12 = (bf16[128,768]{1,0:T(8,128)(2,1)S(1)}, bf16[128,768]{1,0:T(8,128)(2,1)S(1)}, u32[]{:S(2)}, u32[]{:S(2)}) collective-permute-start(bf16[128,768]{1,0:T(8,128)(2,1)S(1)} %collective-permute-done.5.rest_2_), channel_id=1, source_target_pairs={{0,0},{4,4},{8,12},{12,8},{1,1},{5,5},{9,13},{13,9},{2,2},{6,6},{1... | collective-permute-start | bytes 589832 | tf_op jit(solution)/shard_map/ppermute | solution.py:307
  37.2 4.0 %collective-permute-done.9.rest_4_ = bf16[32,2688]{1,0:T(8,128)(2,1)S(1)} collective-permute-done((bf16[32,2688]{1,0:T(8,128)(2,1)S(1)}, bf16[32,2688]{1,0:T(8,128)(2,1)S(1)}, u32[]{:S(2)}, u32[]{:S(2)}) %collective-permute-start.9) | collective-permute-done | bytes 172064 | tf_op jit(solution)/shard_map/ppermute | solution.py:78
  41.2 0.0 collective-permute-done.6.rest_3_
  41.2 0.0 copy-done
  41.2 0.0 copy-done.1
  41.2 0.0 copy-done.2
  41.2 0.9 %shard_map.92.low = bf16[128,128]{1,0:T(8,128)(2,1)S(1)} custom-call(s32[4]{0:T(128)S(1)} %copy-done.1, s32[64]{0:T(128)S(1)} %copy-done.2, bf16[128,3584]{1,0:T(8,128)(2,1)S(1)} %bitcast.16, bf16[896,128]{1,0:T(8,128)(2,1)S(1)} %fusion.2.rest_0_, bf16[896,128]{1,0:T(8,128)(2,1)S(1)} %collective-permute-done.3.rest_1_, ...), custom_call_target="tpu_custom_call" | custom-call | flops 134217728 | bytes 4194304 | tf_op jit(solution)/shard_map/pallas_call | solution.py:97
  42.2 2.7 %collective-permute-done.11.rest_6_ = bf16[32,2688]{1,0:T(8,128)(2,1)S(1)} collective-permute-done((bf16[32,2688]{1,0:T(8,128)(2,1)S(1)}, bf16[32,2688]{1,0:T(8,128)(2,1)S(1)}, u32[]{:S(2)}, u32[]{:S(2)}) %collective-permute-start.11) | collective-permute-done | bytes 172064 | tf_op jit(solution)/shard_map/ppermute | solution.py:305
  44.9 0.0 copy-done.3
  44.9 2.0 %shard_map.93 = (bf16[128,2688]{1,0:T(8,128)(2,1)}, bf16[2688,128]{1,0:T(8,128)(2,1)S(1)}, f32[2688,128]{1,0:T(8,128)S(1)}, f32[2688,128]{1,0:T(8,128)S(1)}, f32[2688,128]{1,0:T(8,128)S(1)}) custom-call(s32[1]{0:T(128)S(6)} %copy.12.lengths, bf16[128,2688]{1,0:T(8,128)(2,1)S(1)} %bitcast.17, bf16[128,128]{1,0:T(8,128)(2,1)S(1)} %shard_map.92.low, ...), custom_call_target="tpu_custom_call" | custom-call | flops 1073741824 | bytes 4194304 | tf_op jit(solution)/shard_map/pallas_call | solution.py:207
  46.9 2.1 %collective-permute-done.12.kv = bf16[128,768]{1,0:T(8,128)(2,1)S(1)} collective-permute-done((bf16[128,768]{1,0:T(8,128)(2,1)S(1)}, bf16[128,768]{1,0:T(8,128)(2,1)S(1)}, u32[]{:S(2)}, u32[]{:S(2)}) %collective-permute-start.12) | collective-permute-done | bytes 196640 | tf_op jit(solution)/shard_map/ppermute | solution.py:307
  49.0 1.8 %shard_map.94 = bf16[128,2688]{1,0:T(8,128)(2,1)} custom-call(s32[1]{0:T(128)S(6)} %copy.12.lengths, bf16[128,2688]{1,0:T(8,128)(2,1)} %get-tuple-element.31.so_far, bf16[2688,128]{1,0:T(8,128)(2,1)S(1)} %get-tuple-element.32.queries, f32[2688,128]{1,0:T(8,128)S(1)} %get-tuple-element.33.sums, ...), custom_call_target="tpu_custom_call", output_to_operand_aliasing={{}: (1, {})} | custom-call | flops 268435456 | bytes 2097152 | tf_op jit(solution)/shard_map/pallas_call | solution.py:260
  (4 shorter events, 0.1 us)
Async XLA Ops:
  0.7 2.0 %copy-start.4 = (bf16[1,128,768]{2,1,0:T(8,128)(2,1)S(1)}, bf16[1,128,768]{2,1,0:T(8,128)(2,1)}, u32[]{:S(2)}) copy-start(bf16[1,128,768]{2,1,0:T(8,128)(2,1)} %param.11) | copy-start | bytes 589828
  1.6 2.5 %collective-permute-start = (bf16[2,896,128]{2,1,0:T(8,128)(2,1)S(1)}, bf16[2,896,128]{2,1,0:T(8,128)(2,1)S(1)}, u32[]{:S(2)}, u32[]{:S(2)}) collective-permute-start(bf16[2,896,128]{2,1,0:T(8,128)(2,1)S(1)} %get-tuple-element.22), channel_id=1, source_target_pairs={{0,1},{1,0},{2,3},{3,2},{4,5},{5,4},{6,7},{7,6},{8,9},{9,8},{10,11... | collective-permute-start | bytes 1376264 | tf_op jit(solution)/shard_map/ppermute | solution.py:293
  2.6 2.3 %collective-permute-start.7 = (bf16[2,32,2688]{2,1,0:T(8,128)(2,1)S(1)}, bf16[2,32,2688]{2,1,0:T(8,128)(2,1)S(1)}, u32[]{:S(2)}, u32[]{:S(2)}) collective-permute-start(bf16[2,32,2688]{2,1,0:T(8,128)(2,1)S(1)} %get-tuple-element.26), channel_id=1, source_target_pairs={{0,1},{1,0},{2,3},{3,2},{4,5},{5,4},{6,7},{7,6},{8,9},{9,8},{10,11... | collective-permute-start | bytes 1032200 | tf_op jit(solution)/shard_map/ppermute | solution.py:294
  2.7 10.2 %collective-permute-start.2 = (bf16[128,768]{1,0:T(8,128)(2,1)S(1)}, bf16[128,768]{1,0:T(8,128)(2,1)S(1)}, u32[]{:S(2)}, u32[]{:S(2)}) collective-permute-start(bf16[128,768]{1,0:T(8,128)(2,1)S(1)} %bitcast.18), channel_id=1, source_target_pairs={{0,4},{4,0},{8,12},{12,8},{1,5},{5,1},{9,13},{13,9},{2,6},{6,2},{1... | collective-permute-start | bytes 589832 | tf_op jit(solution)/shard_map/ppermute | solution.py:78
  3.2 14.7 %collective-permute-start.5 = (bf16[128,768]{1,0:T(8,128)(2,1)S(1)}, bf16[128,768]{1,0:T(8,128)(2,1)S(1)}, u32[]{:S(2)}, u32[]{:S(2)}) collective-permute-start(bf16[128,768]{1,0:T(8,128)(2,1)S(1)} %bitcast.19), channel_id=1, source_target_pairs={{0,8},{4,12},{8,0},{12,4},{1,9},{5,13},{9,1},{13,5},{2,10},{6,14},... | collective-permute-start | bytes 589832 | tf_op jit(solution)/shard_map/ppermute | solution.py:78
  4.1 37.1 %copy-start = (bf16[1,128,3584]{2,1,0:T(8,128)(2,1)S(1)}, bf16[1,128,3584]{2,1,0:T(8,128)(2,1)}, u32[]{:S(2)}) copy-start(bf16[1,128,3584]{2,1,0:T(8,128)(2,1)} %param.9) | copy-start | bytes 2752516
  4.1 37.1 %copy-start.1 = (s32[4]{0:T(128)S(1)}, s32[4]{0:T(128)}, u32[]{:S(2)}) copy-start(s32[4]{0:T(128)} %ids.1) | copy-start | bytes 52
  4.1 37.1 %copy-start.2 = (s32[64]{0:T(128)S(1)}, s32[64]{0:T(128)}, u32[]{:S(2)}) copy-start(s32[64]{0:T(128)} %ranks.1) | copy-start | bytes 772
  4.1 8.5 %collective-permute-start.1 = (bf16[896,128]{1,0:T(8,128)(2,1)S(1)}, bf16[896,128]{1,0:T(8,128)(2,1)S(1)}, u32[]{:S(2)}, u32[]{:S(2)}) collective-permute-start(bf16[896,128]{1,0:T(8,128)(2,1)S(1)} %fusion), channel_id=1, source_target_pairs={{0,2},{1,3},{2,0},{3,1},{4,6},{5,7},{6,4},{7,5},{8,10},{9,11},{10,... | collective-permute-start | bytes 688136 | tf_op jit(solution)/shard_map/ppermute | solution.py:295
  5.0 11.4 %collective-permute-start.8 = (bf16[32,2688]{1,0:T(8,128)(2,1)S(1)}, bf16[32,2688]{1,0:T(8,128)(2,1)S(1)}, u32[]{:S(2)}, u32[]{:S(2)}) collective-permute-start(bf16[32,2688]{1,0:T(8,128)(2,1)S(1)} %fusion.3), channel_id=1, source_target_pairs={{0,2},{1,3},{2,0},{3,1},{4,6},{5,7},{6,4},{7,5},{8,10},{9,11},{10,... | collective-permute-start | bytes 516104 | tf_op jit(solution)/shard_map/ppermute | solution.py:296
  12.7 32.2 %copy-start.3 = (bf16[1,128,2688]{2,1,0:T(8,128)(2,1)S(1)}, bf16[1,128,2688]{2,1,0:T(8,128)(2,1)}, u32[]{:S(2)}) copy-start(bf16[1,128,2688]{2,1,0:T(8,128)(2,1)} %param.10) | copy-start | bytes 2064388
  12.9 15.9 %collective-permute-start.4 = (bf16[896,128]{1,0:T(8,128)(2,1)S(1)}, bf16[896,128]{1,0:T(8,128)(2,1)S(1)}, u32[]{:S(2)}, u32[]{:S(2)}) collective-permute-start(bf16[896,128]{1,0:T(8,128)(2,1)S(1)} %fusion.2.rest_0_), channel_id=1, source_target_pairs={{0,8},{4,12},{8,0},{12,4},{1,9},{5,13},{9,1},{13,5},{2,10},{6,14},... | collective-permute-start | bytes 688136 | tf_op jit(solution)/shard_map/ppermute | solution.py:78
  14.8 17.8 %collective-permute-start.3 = (bf16[896,128]{1,0:T(8,128)(2,1)S(1)}, bf16[896,128]{1,0:T(8,128)(2,1)S(1)}, u32[]{:S(2)}, u32[]{:S(2)}) collective-permute-start(bf16[896,128]{1,0:T(8,128)(2,1)S(1)} %fusion.2.rest_0_), channel_id=1, source_target_pairs={{0,4},{4,0},{8,12},{12,8},{1,5},{5,1},{9,13},{13,9},{2,6},{6,2},{1... | collective-permute-start | bytes 688136 | tf_op jit(solution)/shard_map/ppermute | solution.py:78
  16.4 16.2 %collective-permute-start.10 = (bf16[32,2688]{1,0:T(8,128)(2,1)S(1)}, bf16[32,2688]{1,0:T(8,128)(2,1)S(1)}, u32[]{:S(2)}, u32[]{:S(2)}) collective-permute-start(bf16[32,2688]{1,0:T(8,128)(2,1)S(1)} %fusion.5.rest_3_), channel_id=1, source_target_pairs={{0,8},{4,12},{8,0},{12,4},{1,9},{5,13},{9,1},{13,5},{2,10},{6,14},... | collective-permute-start | bytes 516104 | tf_op jit(solution)/shard_map/ppermute | solution.py:78
  28.9 12.3 %collective-permute-start.6 = (bf16[896,128]{1,0:T(8,128)(2,1)S(1)}, bf16[896,128]{1,0:T(8,128)(2,1)S(1)}, u32[]{:S(2)}, u32[]{:S(2)}) collective-permute-start(bf16[896,128]{1,0:T(8,128)(2,1)S(1)} %collective-permute-done.4.rest_2_), channel_id=1, source_target_pairs={{0,4},{4,0},{8,12},{12,8},{1,5},{5,1},{9,13},{13,9},{2,6},{6,2},{1... | collective-permute-start | bytes 688136 | tf_op jit(solution)/shard_map/ppermute | solution.py:303
  28.9 12.3 %collective-permute-start.9 = (bf16[32,2688]{1,0:T(8,128)(2,1)S(1)}, bf16[32,2688]{1,0:T(8,128)(2,1)S(1)}, u32[]{:S(2)}, u32[]{:S(2)}) collective-permute-start(bf16[32,2688]{1,0:T(8,128)(2,1)S(1)} %fusion.5.rest_3_), channel_id=1, source_target_pairs={{0,4},{4,0},{8,12},{12,8},{1,5},{5,1},{9,13},{13,9},{2,6},{6,2},{1... | collective-permute-start | bytes 516104 | tf_op jit(solution)/shard_map/ppermute | solution.py:78
  32.6 12.3 %collective-permute-start.11 = (bf16[32,2688]{1,0:T(8,128)(2,1)S(1)}, bf16[32,2688]{1,0:T(8,128)(2,1)S(1)}, u32[]{:S(2)}, u32[]{:S(2)}) collective-permute-start(bf16[32,2688]{1,0:T(8,128)(2,1)S(1)} %collective-permute-done.10.rest_5_), channel_id=1, source_target_pairs={{0,4},{4,0},{8,12},{12,8},{1,5},{5,1},{9,13},{13,9},{2,6},{6,2},{1... | collective-permute-start | bytes 516104 | tf_op jit(solution)/shard_map/ppermute | solution.py:305
  32.6 16.4 %collective-permute-start.12 = (bf16[128,768]{1,0:T(8,128)(2,1)S(1)}, bf16[128,768]{1,0:T(8,128)(2,1)S(1)}, u32[]{:S(2)}, u32[]{:S(2)}) collective-permute-start(bf16[128,768]{1,0:T(8,128)(2,1)S(1)} %collective-permute-done.5.rest_2_), channel_id=1, source_target_pairs={{0,0},{4,4},{8,12},{12,8},{1,1},{5,5},{9,13},{13,9},{2,2},{6,6},{1... | collective-permute-start | bytes 589832 | tf_op jit(solution)/shard_map/ppermute | solution.py:307
